TPU v7x, 512 devices: a whole 4x8x8 slice. The times are simulated.
512 devices in a mesh: blk: 8 (over z), wide: 64 (over y, x, core).
Axes of the slice: x: 4, y: 8, z: 8, core: 2. Of those that a mesh axis runs over, the one named last changes fastest.
Arguments:
- resid: bfloat16 [8192, 4096], P('wide', 'blk'), may hold values from -24 to 24
- samples: bfloat16 [8192, 4096], P('wide', 'blk'), may hold values from -6 to 6
- precision: float32 [64, 8, 8, 128, 128], P('wide', 'blk'), as said below
- active: int32 [64, 8, 8], P('wide', 'blk'), may hold values 0 or 1
Outputs:
- updated: float32 [64, 8, 8, 128, 128], P('wide', 'blk')
Inputs may be any that keep to these rules, and one draw needn't show every extreme that they name: `precision`: entries on the diagonal of W lie between 1 and 2.
All inputs are finite; a program needn't handle non-finite values. No bound on the sum of `active` on one device may be relied on, other than what follows from the above.
Results may differ from a plain program's by a relative error of at most 0.0003.
Values may be sent and summed in bfloat16 or wider, within the bound.
No kernel may reach another device: no remote copies, remote signals or barrier semaphores. Data moves between devices by JAX's collectives and lax.ppermute only.
A program may use at most 128 MiB of HBM per device.

v0:
```python
import jax
import jax.numpy as jnp
from jax import lax
from jax.sharding import PartitionSpec as P

STEP = 1.0
LASSO = 0.1
RIDGE = 0.5


def sent_together(arrays, axis, dim, along):
    ends, at = ([], 0)
    for a in arrays[:-1]:
        at += a.shape[along]
        ends.append(at)
    both = jnp.concatenate(arrays, axis=along)
    return tuple(jnp.split(lax.all_gather(both, axis, axis=dim, tiled=True), ends, axis=along))


def local(resid, samples, precision, active):
    groups = lax.axis_size("blk")
    column_group = lax.axis_index("blk")
    panel_index = lax.axis_index("wide")
    row_tiles = precision.shape[0]
    per_class = precision.shape[2]
    tile_size = precision.shape[3]
    tiles = per_class * groups
    local_samples = resid.shape[1]
    total_samples = local_samples * groups
    own_rows = panel_index * row_tiles + jnp.arange(row_tiles, dtype=jnp.int32)
    first_column = (column_group - own_rows) % groups
    own_resid = resid.reshape(row_tiles, tile_size, local_samples)
    own_data = samples.reshape(row_tiles, tile_size, local_samples)
    all_resid, all_data = sent_together((resid, samples), "wide", 0, 1)
    resid_tiles = all_resid.reshape(tiles, tile_size, local_samples)
    data_tiles = all_data.reshape(tiles, tile_size, local_samples)
    positions = jnp.arange(per_class * lax.axis_size("blk"), dtype=jnp.int32)
    classes = positions // per_class
    within = positions % per_class
    column_ids = (classes[:, None] - own_rows[None, :]) % groups + groups * within[:, None]
    forward = jnp.einsum(
        "kis,pkjs->pkij", own_resid, data_tiles[column_ids], preferred_element_type=jnp.float32
    )
    backward = jnp.einsum(
        "kis,pkjs->pkij", own_data, resid_tiles[column_ids], preferred_element_type=jnp.float32
    )
    summed = (
        lax.psum_scatter(0.5 * (forward + backward), "blk", scatter_dimension=0, tiled=True)
        / total_samples
    )
    precision_tiles = precision[:, 0]
    active_flags = active[:, 0].astype(jnp.float32)
    gradient_part = summed.transpose(1, 0, 2, 3)
    column_ids = first_column[:, None] + groups * jnp.arange(per_class, dtype=jnp.int32)[None, :]
    same_tile = column_ids == own_rows[:, None]
    identity = jnp.eye(tile_size, dtype=bool)
    on_diag = same_tile[:, :, None, None] & identity
    inverse = jnp.where(on_diag, 1.0 / jnp.where(on_diag, precision_tiles, 1.0), 0.0)
    stepped = precision_tiles - STEP * (gradient_part + RIDGE * precision_tiles - inverse)
    shrunk = jnp.sign(stepped) * jnp.maximum(jnp.abs(stepped) - STEP * LASSO, 0.0)
    updated = jnp.where(on_diag, stepped, shrunk) * active_flags[:, :, None, None]
    return updated[:, None]


def solution(mesh):
    in_specs = (
        P("wide", "blk"),
        P("wide", "blk"),
        P("wide", "blk", None, None, None),
        P("wide", "blk", None),
    )
    out_specs = P("wide", "blk", None, None, None)
    return jax.shard_map(local, mesh=mesh, in_specs=in_specs, out_specs=out_specs, check_vma=False)
```

profile of v0, /device:TPU:1, one launch (start us, length us, event | category | flops | bytes accessed | tf_op | source)
XLA Modules:
  0.0 232.7 jit_solution(11015258892992603365)
XLA Ops:
  6.5 0.0 all-gather.2.cloned.1.call-start
  6.5 1.7 pad_maximum_fusion
  8.2 0.0 all-gather.2.cloned.1.call-update
  8.3 0.0 reduce-scatter.2.cloned.1.call-start
  8.3 113.1 %all-gather.2.cloned.1.call-done = bf16[8192,1024]{1,0:T(8,128)(2,1)} async-done(((bf16[128,1024]{1,0:T(8,128)(2,1)}), bf16[8192,1024]{1,0:T(8,128)(2,1)}) %all-gather.2.cloned.1.call-update) | async-done | bytes 16777232 | tf_op jit(solution)/shard_map/all_gather | solution.py:17
  121.5 11.3 %fusion.12 = (bf16[8192,512]{1,0:T(8,128)(2,1)}, bf16[8192,512]{1,0:T(8,128)(2,1)}) fusion(bf16[8192,1024]{1,0:T(8,128)(2,1)} %all-gather.2.cloned.1.call-done), kind=kLoop, calls=%fused_computation.33 | loop fusion | bytes 33554432 | tf_op jit(solution)/shard_map/split | solution.py:17
  132.8 0.0 copy-start
  132.8 9.0 %gather_fusion = bf16[64,128,512]{2,1,0:T(8,128)(2,1)} fusion(bf16[64,128,512]{2,1,0:T(8,128)(2,1)} %bitcast.27, s32[1024]{0:T(1024)S(1)} %pad_clamp_fusion), kind=kCustom, calls=%fused_computation | custom fusion | bytes 16777472 | tf_op jit(solution)/shard_map/gather | solution.py:42
  141.7 0.0 copy-done
  141.7 7.7 %fusion.5 = f32[64,128,128]{2,1,0:T(8,128)} fusion(bf16[64,128,512]{2,1,0:T(8,128)(2,1)} %gather_fusion, bf16[128,512]{1,0:T(8,128)(2,1)S(1)} %copy-done), kind=kOutput, calls=%fused_computation.13 | convolution fusion | flops 1073741824 | bytes 12713984 | tf_op jit(solution)/shard_map/kis,pkjs->pkij/dot_general | solution.py:41
  149.4 0.0 copy-start.1
  149.4 9.0 %gather_fusion.1 = bf16[64,128,512]{2,1,0:T(8,128)(2,1)} fusion(bf16[64,128,512]{2,1,0:T(8,128)(2,1)} %bitcast.26, s32[1024]{0:T(1024)S(1)} %pad_clamp_fusion), kind=kCustom, calls=%fused_computation.1 | custom fusion | bytes 16777472 | tf_op jit(solution)/shard_map/gather | solution.py:45
  158.4 0.0 copy-done.1
  158.4 0.0 copy-start.2
  158.4 0.0 copy-start.3
  158.4 8.9 %multiply_bitcast_fusion = f32[64,1,128,128]{2,3,0,1:T(8,128)} fusion(f32[64,128,128]{2,1,0:T(8,128)} %fusion.5, bf16[64,128,512]{2,1,0:T(8,128)(2,1)} %gather_fusion.1, bf16[128,512]{1,0:T(8,128)(2,1)S(1)} %copy-done.1), kind=kOutput, calls=%fused_computation.2 | convolution fusion | flops 1075838976 | bytes 16908288 | tf_op jit(solution)/shard_map/kis,pkjs->pkij/dot_general | solution.py:44
  167.3 0.0 reduce-scatter.2.cloned.1.call-update
  167.4 0.0 copy-done.2
  167.4 0.2 copy.7
  167.6 0.0 copy-done.3
  167.7 55.7 %reduce-scatter.2.cloned.1.call-done = f32[8,1,128,128]{2,3,0,1:T(8,128)} async-done(((f32[64,1,128,128]{2,3,0,1:T(8,128)}), f32[8,1,128,128]{2,3,0,1:T(8,128)}) %reduce-scatter.2.cloned.1.call-update) | async-done | bytes 524304 | tf_op jit(solution)/shard_map/reduce_scatter | solution.py:48
  223.4 1.5 fusion.3
  224.9 1.0 copy.8
  (5 shorter events, 0.1 us)
Async XLA Ops:
  6.5 114.9 %all-gather.2.cloned.1.call-start = ((), (), s32[]{:S(2)}) async-start(), calls=%async_computation.1 | async-start | bytes 17039360 | tf_op jit(solution)/shard_map/all_gather | solution.py:17
  8.3 215.1 %reduce-scatter.2.cloned.1.call-start = ((), (), s32[]{:S(2)}) async-start(), calls=%async_computation.2 | async-start | bytes 4718592 | tf_op jit(solution)/shard_map/reduce_scatter | solution.py:48
  132.8 9.0 %copy-start = (bf16[128,512]{1,0:T(8,128)(2,1)S(1)}, bf16[128,512]{1,0:T(8,128)(2,1)}, u32[]{:S(2)}) copy-start(bf16[128,512]{1,0:T(8,128)(2,1)} %param.4) | copy-start | bytes 393220
  149.4 9.0 %copy-start.1 = (bf16[128,512]{1,0:T(8,128)(2,1)S(1)}, bf16[128,512]{1,0:T(8,128)(2,1)}, u32[]{:S(2)}) copy-start(bf16[128,512]{1,0:T(8,128)(2,1)} %param.5) | copy-start | bytes 393220
  158.4 9.0 %copy-start.2 = (f32[1,1,8,128,128]{4,3,2,1,0:T(8,128)S(1)}, f32[1,1,8,128,128]{4,3,2,1,0:T(8,128)}, u32[]{:S(2)}) copy-start(f32[1,1,8,128,128]{4,3,2,1,0:T(8,128)} %param.6) | copy-start | bytes 1572868
  158.4 9.2 %copy-start.3 = (s32[1,1,8]{2,1,0:T(1,128)S(1)}, s32[1,1,8]{2,1,0:T(1,128)}, u32[]{:S(2)}) copy-start(s32[1,1,8]{2,1,0:T(1,128)} %param.7) | copy-start | bytes 100
Sparse Core Ops, SparseCore 0:
  10.7 110.7 all-gather.1
  167.5 55.8 reduce-scatter.1
where the time goes:
time: 233 us
  waiting for transfers between devices  169 us (73%)
  local copies, waits for them, and re-layouts  30.4 us (13%)
  matrix products  16.6 us (7%)
  between operations  13.5 us (6%)
  other arithmetic  3.24 us (1%)
    all_gather x1, waiting for transfers between devices, sent_together(): lax.all_gather(both, axis, axis=dim, tiled=True)  113 us
    reduce_scatter x1, waiting for transfers between devices, local(): lax.psum_scatter(0.5 * (forward + backward), 'blk', scatter_dimension=0,...  55.7 us
    split x1, local copies, waits for them, and re-layouts, sent_together(): jnp.split(lax.all_gather(both, axis, axis=dim, tiled=True), ends, axis=al...  11.3 us
    gather x1, local copies, waits for them, and re-layouts, local(): data_tiles[column_ids]  8.96 us
    gather x1, local copies, waits for them, and re-layouts, local(): resid_tiles[column_ids]  8.96 us
    dot_general x1, matrix products, local(): jnp.einsum('kis,pkjs->pkij', own_data, resid_tiles[column_ids], preferred...  8.94 us
    dot_general x1, matrix products, local(): jnp.einsum('kis,pkjs->pkij', own_resid, data_tiles[column_ids], preferred...  7.69 us
  transfers between devices with their start and end apart: 2, of which 2 were waited for; matrix products, arithmetic and copies ran while one was open for 0% of the time, Pallas kernels for 0%

commit v1 on v0

v1 whole, which is shorter than its diff:
```python
import functools

import jax
import jax.numpy as jnp
from jax import lax
from jax.experimental import pallas as pl
from jax.experimental.pallas import tpu as pltpu
from jax.sharding import Mesh, PartitionSpec as P

STEP = 1.0
LASSO = 0.1
RIDGE = 0.5
AXES = ("z", "y", "k")


def products(n, half, tile, depth, place, *refs):
    panels, column_ref, out_ref, picked = refs[:n], refs[n], refs[n + 1], refs[n + 2]
    y, k = place[0], place[1]
    for d in range(half):
        rows = pl.ds(pl.multiple_of(lax.rem(y + d, n) * tile, tile), tile)
        picked[d * tile:(d + 1) * tile, :depth] = column_ref[rows, depth:]
        picked[d * tile:(d + 1) * tile, depth:] = column_ref[rows, :depth]
    for e in range(n):
        part = lax.dot_general(
            panels[e][...], picked[...], (((1,), (1,)), ((), ())), preferred_element_type=jnp.float32
        )
        m = lax.rem(2 * k - e + n, n)
        for d in range(half):
            out_ref[m, d] = part[:, d * tile:(d + 1) * tile]


def finish(n, half, tile, scale, place, active_ref, own_ref, mirrored_ref, *refs):
    shifted, precision_ref, out_ref = refs[:n - half], refs[n - half], refs[n - half + 1]
    y, k, z = place[0], place[1], place[2]
    row = lax.broadcasted_iota(jnp.int32, (tile, tile), 0)
    column = lax.broadcasted_iota(jnp.int32, (tile, tile), 1)
    for d in range(n):
        t = lax.rem(y + d, n)
        if d == 0:
            total = own_ref[0].T
        elif d < half:
            total = mirrored_ref[d]
        else:
            total = shifted[n - d - 1][...].T
        w = precision_ref[t]
        gradient = total * scale + RIDGE * w
        if d == 0:
            same_tile = lax.rem(2 * k - z + n, n) == 0
            on_diag = (row == column) & same_tile
            inverse = jnp.where(on_diag, 1.0 / jnp.where(on_diag, w, 1.0), 0.0)
            stepped = w - STEP * (gradient - inverse)
        else:
            stepped = w - STEP * gradient
        shrunk = jnp.where(
            stepped > 0, jnp.maximum(stepped - STEP * LASSO, 0.0), jnp.minimum(stepped + STEP * LASSO, 0.0)
        )
        if d == 0:
            shrunk = jnp.where(on_diag, stepped, shrunk)
        out_ref[t] = shrunk * active_ref[t].astype(jnp.float32)


def local(n, resid, samples, precision, active):
    z, y, k = (lax.axis_index(a) for a in AXES)
    place = jnp.stack([y, k, z]).astype(jnp.int32)
    tile, depth = resid.shape
    half = n // 2 + 1

    def moved(a, to):
        ids = [(z * n + y) * n + k for z in range(n) for y in range(n) for k in range(n)]
        ends = []
        for i in ids:
            c = to(i // (n * n), i // n % n, i % n)
            ends.append((c[0] % n * n + c[1] % n) * n + c[2] % n)
        return lax.ppermute(a, AXES, list(zip(ids, ends)))

    own = jnp.concatenate([resid, samples], axis=1)
    column = lax.all_gather(own, "y", axis=0, tiled=True)
    panels = [own] + [moved(own, lambda z, y, k, e=e: (z, y, k + e)) for e in range(1, n)]
    vmem, smem = pl.BlockSpec(memory_space=pltpu.VMEM), pl.BlockSpec(memory_space=pltpu.SMEM)
    partial = pl.pallas_call(
        functools.partial(products, n, half, tile, depth),
        out_shape=jax.ShapeDtypeStruct((n, half, tile, tile), jnp.float32),
        in_specs=[smem] + [vmem] * (n + 1),
        out_specs=vmem,
        scratch_shapes=[pltpu.VMEM((half * tile, 2 * depth), jnp.bfloat16)],
        compiler_params=pltpu.CompilerParams(vmem_limit_bytes=32 * 2**20),
        cost_estimate=pl.CostEstimate(
            flops=4 * n * half * tile * tile * depth, bytes_accessed=8 * 2**20, transcendentals=0
        ),
    )(place, *panels, column)
    summed = lax.psum_scatter(partial, "z", scatter_dimension=0, tiled=True)[0]
    mirrored = moved(summed, lambda z, y, k: (z, y, z - k))
    shifted = [moved(summed[d], lambda z, y, k, d=d: (z, y + d, k)) for d in range(1, n - half + 1)]
    updated = pl.pallas_call(
        functools.partial(finish, n, half, tile, 0.5 / (depth * n)),
        out_shape=jax.ShapeDtypeStruct((n, tile, tile), jnp.float32),
        in_specs=[smem, smem] + [vmem] * (3 + n - half),
        out_specs=vmem,
    )(place, active.reshape(n), summed, mirrored, *shifted, precision.reshape(n, tile, tile))
    return updated.reshape(precision.shape)


def solution(mesh):
    n = mesh.shape["blk"]
    grid = Mesh(mesh.devices.reshape(n, n, n), AXES)
    rows = ("y", "k")
    in_specs = (P(rows, "z"), P(rows, "z"), P(rows, "z"), P(rows, "z"))
    return jax.shard_map(
        functools.partial(local, n), mesh=grid, in_specs=in_specs, out_specs=P(rows, "z"), check_vma=False
    )
```

time: 233 us -> 145 us (0.62)
  the two profiles are of different devices: /device:TPU:1 before, /device:TPU:2 now
where the time goes in v1:
time: 145 us
  waiting for transfers between devices  79.7 us (55%)
  starting transfers between devices  36.8 us (25%)
  between operations  13.6 us (9%)
  Pallas kernels  7.7 us (5%)
  local copies, waits for them, and re-layouts  6.72 us (5%)
    reduce_scatter x1, waiting for transfers between devices, local(): summed = lax.psum_scatter(partial, 'z', scatter_dimension=0, tiled=True)[0]  46.6 us
    ppermute x11, starting transfers between devices, moved(): return lax.ppermute(a, AXES, list(zip(ids, ends)))  36.8 us
    ppermute x11, waiting for transfers between devices, moved(): return lax.ppermute(a, AXES, list(zip(ids, ends)))  20.7 us
    all_gather x1, waiting for transfers between devices, local(): column = lax.all_gather(own, 'y', axis=0, tiled=True)  12.4 us
    pallas_call x1, Pallas kernels, local(): pl.pallas_call(functools.partial(products, n, half, tile, depth), out_sha...  5.3 us
    unnamed x17, local copies, waits for them, and re-layouts  4.89 us
  transfers between devices with their start and end apart: 13, of which 8 were waited for; matrix products, arithmetic and copies ran while one was open for 1% of the time, Pallas kernels for 0%

profile of v1, /device:TPU:2, one launch (start us, length us, event | category | flops | bytes accessed | tf_op | source)
XLA Modules:
  0.0 144.6 jit_solution(6883021010162470500)
XLA Ops:
  6.5 0.9 constant_dynamic-update-slice_fusion.1
  7.5 0.9 constant_dynamic-update-slice_fusion.refs_0_
  8.4 0.7 copy-done.1
  9.1 0.0 all-gather.2.cloned.1.call-update
  9.1 0.0 reduce-scatter.2.cloned.1.call-start
  9.2 7.8 %collective-permute-start.5 = (bf16[128,1024]{1,0:T(8,128)(2,1)}, bf16[128,1024]{1,0:T(8,128)(2,1)S(1)}, u32[]{:S(2)}, u32[]{:S(2)}) collective-permute-start(bf16[128,1024]{1,0:T(8,128)(2,1)} %copy-done.1), channel_id=1, source_target_pairs={{0,6},{1,7},{2,0},{3,1},{4,2},{5,3},{6,4},{7,5},{8,14},{9,15},{10,... | collective-permute-start | bytes 786440 | tf_op jit(solution)/shard_map/ppermute | solution.py:74
  17.0 1.9 %collective-permute-start.4 = (bf16[128,1024]{1,0:T(8,128)(2,1)}, bf16[128,1024]{1,0:T(8,128)(2,1)S(1)}, u32[]{:S(2)}, u32[]{:S(2)}) collective-permute-start(bf16[128,1024]{1,0:T(8,128)(2,1)} %copy-done.1), channel_id=1, source_target_pairs={{0,5},{1,6},{2,7},{3,0},{4,1},{5,2},{6,3},{7,4},{8,13},{9,14},{10,... | collective-permute-start | bytes 786440 | tf_op jit(solution)/shard_map/ppermute | solution.py:74
  18.9 5.2 %collective-permute-start.3 = (bf16[128,1024]{1,0:T(8,128)(2,1)}, bf16[128,1024]{1,0:T(8,128)(2,1)S(1)}, u32[]{:S(2)}, u32[]{:S(2)}) collective-permute-start(bf16[128,1024]{1,0:T(8,128)(2,1)} %copy-done.1), channel_id=1, source_target_pairs={{0,4},{1,5},{2,6},{3,7},{4,0},{5,1},{6,2},{7,3},{8,12},{9,13},{10,... | collective-permute-start | bytes 786440 | tf_op jit(solution)/shard_map/ppermute | solution.py:74
  24.2 1.9 %collective-permute-start.2 = (bf16[128,1024]{1,0:T(8,128)(2,1)}, bf16[128,1024]{1,0:T(8,128)(2,1)S(1)}, u32[]{:S(2)}, u32[]{:S(2)}) collective-permute-start(bf16[128,1024]{1,0:T(8,128)(2,1)} %copy-done.1), channel_id=1, source_target_pairs={{0,3},{1,4},{2,5},{3,6},{4,7},{5,0},{6,1},{7,2},{8,11},{9,12},{10,... | collective-permute-start | bytes 786440 | tf_op jit(solution)/shard_map/ppermute | solution.py:74
  26.1 2.2 %collective-permute-start.1 = (bf16[128,1024]{1,0:T(8,128)(2,1)}, bf16[128,1024]{1,0:T(8,128)(2,1)S(1)}, u32[]{:S(2)}, u32[]{:S(2)}) collective-permute-start(bf16[128,1024]{1,0:T(8,128)(2,1)} %copy-done.1), channel_id=1, source_target_pairs={{0,2},{1,3},{2,4},{3,5},{4,6},{5,7},{6,0},{7,1},{8,10},{9,11},{10,... | collective-permute-start | bytes 786440 | tf_op jit(solution)/shard_map/ppermute | solution.py:74
  28.3 1.3 collective-permute-start
  29.6 0.1 pad_add_fusion.place
  29.7 6.4 %collective-permute-done.4.refs_5_ = bf16[128,1024]{1,0:T(8,128)(2,1)S(1)} collective-permute-done((bf16[128,1024]{1,0:T(8,128)(2,1)}, bf16[128,1024]{1,0:T(8,128)(2,1)S(1)}, u32[]{:S(2)}, u32[]{:S(2)}) %collective-permute-start.4) | collective-permute-done | bytes 262176 | tf_op jit(solution)/shard_map/ppermute | solution.py:74
  36.1 2.7 %collective-permute-done.2.refs_3_ = bf16[128,1024]{1,0:T(8,128)(2,1)S(1)} collective-permute-done((bf16[128,1024]{1,0:T(8,128)(2,1)}, bf16[128,1024]{1,0:T(8,128)(2,1)S(1)}, u32[]{:S(2)}, u32[]{:S(2)}) %collective-permute-start.2) | collective-permute-done | bytes 262176 | tf_op jit(solution)/shard_map/ppermute | solution.py:74
  38.8 5.6 %collective-permute-done.1.refs_2_ = bf16[128,1024]{1,0:T(8,128)(2,1)S(1)} collective-permute-done((bf16[128,1024]{1,0:T(8,128)(2,1)}, bf16[128,1024]{1,0:T(8,128)(2,1)S(1)}, u32[]{:S(2)}, u32[]{:S(2)}) %collective-permute-start.1) | collective-permute-done | bytes 262176 | tf_op jit(solution)/shard_map/ppermute | solution.py:74
  44.4 1.1 collective-permute-done.refs_1_
  45.5 12.4 %all-gather.2.cloned.1.call-done.refs_8_ = bf16[1024,1024]{1,0:T(8,128)(2,1)} async-done(((bf16[128,1024]{1,0:T(8,128)(2,1)}), bf16[1024,1024]{1,0:T(8,128)(2,1)}) %all-gather.2.cloned.1.call-update) | async-done | bytes 2097168 | tf_op jit(solution)/shard_map/all_gather | solution.py:77
  57.9 1.6 %copy-done = bf16[1024,1024]{1,0:T(8,128)(2,1)S(1)} copy-done((bf16[1024,1024]{1,0:T(8,128)(2,1)S(1)}, bf16[1024,1024]{1,0:T(8,128)(2,1)}, u32[]{:S(2)}) %copy-start) | copy-done | bytes 2097176
  59.5 0.9 copy-done.2
  60.4 5.3 %shard_map.46 = f32[8,5,128,128]{3,2,1,0:T(8,128)} custom-call(s32[3]{0:T(128)S(1)} %pad_add_fusion.place, bf16[128,1024]{1,0:T(8,128)(2,1)S(1)} %copy-done.2, bf16[128,1024]{1,0:T(8,128)(2,1)S(1)} %collective-permute-done.refs_1_, bf16[128,1024]{1,0:T(8,128)(2,1)S(1)} %collective-permute-done.1.refs_2_, ...), custom_call_target="tpu_custom_call" | custom-call | flops 1342177280 | bytes 8388608 | tf_op jit(solution)/shard_map/pallas_call | solution.py:80
  65.7 0.0 reduce-scatter.2.cloned.1.call-update
  65.8 46.6 %reduce-scatter.2.cloned.1.call-done = f32[1,5,128,128]{3,2,1,0:T(8,128)} async-done(((f32[8,5,128,128]{3,2,1,0:T(8,128)}), f32[1,5,128,128]{3,2,1,0:T(8,128)}) %reduce-scatter.2.cloned.1.call-update) | async-done | bytes 327696 | tf_op jit(solution)/shard_map/reduce_scatter | solution.py:91
  112.3 3.9 %collective-permute-start.7 = (f32[5,128,128]{2,1,0:T(8,128)}, f32[5,128,128]{2,1,0:T(8,128)S(1)}, u32[]{:S(2)}, u32[]{:S(2)}) collective-permute-start(f32[5,128,128]{2,1,0:T(8,128)} %bitcast.13), channel_id=1, source_target_pairs={{0,0},{1,7},{2,6},{3,5},{4,4},{5,3},{6,2},{7,1},{8,8},{9,15},{10,1... | collective-permute-start | bytes 983048 | tf_op jit(solution)/shard_map/ppermute | solution.py:74
  116.3 0.9 slice_bitcast_fusion
  117.2 5.4 %collective-permute-start.10 = (f32[128,128]{1,0:T(8,128)S(1)}, f32[128,128]{1,0:T(8,128)S(1)}, u32[]{:S(2)}, u32[]{:S(2)}) collective-permute-start(f32[128,128]{1,0:T(8,128)S(1)} %get-tuple-element.5), channel_id=1, source_target_pairs={{0,24},{1,25},{2,26},{3,27},{4,28},{5,29},{6,30},{7,31},{8,32},{9,... | collective-permute-start | bytes 196616 | tf_op jit(solution)/shard_map/ppermute | solution.py:74
  122.6 4.6 %collective-permute-start.9 = (f32[128,128]{1,0:T(8,128)S(1)}, f32[128,128]{1,0:T(8,128)S(1)}, u32[]{:S(2)}, u32[]{:S(2)}) collective-permute-start(f32[128,128]{1,0:T(8,128)S(1)} %get-tuple-element.6), channel_id=1, source_target_pairs={{0,16},{1,17},{2,18},{3,19},{4,20},{5,21},{6,22},{7,23},{8,24},{9,... | collective-permute-start | bytes 196616 | tf_op jit(solution)/shard_map/ppermute | solution.py:74
  127.3 2.4 %collective-permute-start.8 = (f32[128,128]{1,0:T(8,128)S(1)}, f32[128,128]{1,0:T(8,128)S(1)}, u32[]{:S(2)}, u32[]{:S(2)}) collective-permute-start(f32[128,128]{1,0:T(8,128)S(1)} %get-tuple-element.7), channel_id=1, source_target_pairs={{0,8},{1,9},{2,10},{3,11},{4,12},{5,13},{6,14},{7,15},{8,16},{9,17... | collective-permute-start | bytes 196616 | tf_op jit(solution)/shard_map/ppermute | solution.py:74
  129.7 2.0 %collective-permute-done.9.refs_1_ = f32[128,128]{1,0:T(8,128)S(1)} collective-permute-done((f32[128,128]{1,0:T(8,128)S(1)}, f32[128,128]{1,0:T(8,128)S(1)}, u32[]{:S(2)}, u32[]{:S(2)}) %collective-permute-start.9) | collective-permute-done | bytes 65568 | tf_op jit(solution)/shard_map/ppermute | solution.py:74
  131.7 2.9 %collective-permute-done.8.refs_0_ = f32[128,128]{1,0:T(8,128)S(1)} collective-permute-done((f32[128,128]{1,0:T(8,128)S(1)}, f32[128,128]{1,0:T(8,128)S(1)}, u32[]{:S(2)}, u32[]{:S(2)}) %collective-permute-start.8) | collective-permute-done | bytes 65568 | tf_op jit(solution)/shard_map/ppermute | solution.py:74
  134.7 0.6 copy-done.7
  135.3 0.1 copy-done.4
  135.4 2.4 %shard_map.47 = f32[8,128,128]{2,1,0:T(8,128)} custom-call(s32[3]{0:T(128)} %copy-done.3, s32[8]{0:T(128)} %bitcast.16, f32[5,128,128]{2,1,0:T(8,128)} %bitcast.14, f32[5,128,128]{2,1,0:T(8,128)} %copy-done.4, f32[128,128]{1,0:T(8,128)} %copy-done.7, f32[128,128]{1,0:T(8,128)} %copy-done.6, f32[128,128]{1,0:T(8,128)} %copy-done.5, f32[8,128,128]{2,1,0:T(8,128)} %bitcast.15), custom_call_target="tpu_custom_call" | custom-call | tf_op jit(solution)/shard_map/pallas_call | solution.py:94
  (18 shorter events, 0.1 us)
Async XLA Ops:
  6.5 51.4 %all-gather.2.cloned.1.call-start = ((), (), s32[]{:S(2)}) async-start(), calls=%async_computation.1 | async-start | bytes 2359296 | tf_op jit(solution)/shard_map/all_gather | solution.py:77
  8.4 0.7 copy-start.1
  9.1 103.2 %reduce-scatter.2.cloned.1.call-start = ((), (), s32[]{:S(2)}) async-start(), calls=%async_computation.2 | async-start | bytes 2949120 | tf_op jit(solution)/shard_map/reduce_scatter | solution.py:91
  9.2 16.9 %collective-permute-start.6 = (bf16[128,1024]{1,0:T(8,128)(2,1)}, bf16[128,1024]{1,0:T(8,128)(2,1)S(1)}, u32[]{:S(2)}, u32[]{:S(2)}) collective-permute-start(bf16[128,1024]{1,0:T(8,128)(2,1)} %copy-done.1), channel_id=1, source_target_pairs={{0,7},{1,0},{2,1},{3,2},{4,3},{5,4},{6,5},{7,6},{8,15},{9,8},{10,9... | collective-permute-start | bytes 786440 | tf_op jit(solution)/shard_map/ppermute | solution.py:74
  9.2 19.1 %collective-permute-start.5 = (bf16[128,1024]{1,0:T(8,128)(2,1)}, bf16[128,1024]{1,0:T(8,128)(2,1)S(1)}, u32[]{:S(2)}, u32[]{:S(2)}) collective-permute-start(bf16[128,1024]{1,0:T(8,128)(2,1)} %copy-done.1), channel_id=1, source_target_pairs={{0,6},{1,7},{2,0},{3,1},{4,2},{5,3},{6,4},{7,5},{8,14},{9,15},{10,... | collective-permute-start | bytes 786440 | tf_op jit(solution)/shard_map/ppermute | solution.py:74
  17.0 19.1 %collective-permute-start.4 = (bf16[128,1024]{1,0:T(8,128)(2,1)}, bf16[128,1024]{1,0:T(8,128)(2,1)S(1)}, u32[]{:S(2)}, u32[]{:S(2)}) collective-permute-start(bf16[128,1024]{1,0:T(8,128)(2,1)} %copy-done.1), channel_id=1, source_target_pairs={{0,5},{1,6},{2,7},{3,0},{4,1},{5,2},{6,3},{7,4},{8,13},{9,14},{10,... | collective-permute-start | bytes 786440 | tf_op jit(solution)/shard_map/ppermute | solution.py:74
  18.9 17.2 %collective-permute-start.3 = (bf16[128,1024]{1,0:T(8,128)(2,1)}, bf16[128,1024]{1,0:T(8,128)(2,1)S(1)}, u32[]{:S(2)}, u32[]{:S(2)}) collective-permute-start(bf16[128,1024]{1,0:T(8,128)(2,1)} %copy-done.1), channel_id=1, source_target_pairs={{0,4},{1,5},{2,6},{3,7},{4,0},{5,1},{6,2},{7,3},{8,12},{9,13},{10,... | collective-permute-start | bytes 786440 | tf_op jit(solution)/shard_map/ppermute | solution.py:74
  24.2 14.7 %collective-permute-start.2 = (bf16[128,1024]{1,0:T(8,128)(2,1)}, bf16[128,1024]{1,0:T(8,128)(2,1)S(1)}, u32[]{:S(2)}, u32[]{:S(2)}) collective-permute-start(bf16[128,1024]{1,0:T(8,128)(2,1)} %copy-done.1), channel_id=1, source_target_pairs={{0,3},{1,4},{2,5},{3,6},{4,7},{5,0},{6,1},{7,2},{8,11},{9,12},{10,... | collective-permute-start | bytes 786440 | tf_op jit(solution)/shard_map/ppermute | solution.py:74
  26.1 18.3 %collective-permute-start.1 = (bf16[128,1024]{1,0:T(8,128)(2,1)}, bf16[128,1024]{1,0:T(8,128)(2,1)S(1)}, u32[]{:S(2)}, u32[]{:S(2)}) collective-permute-start(bf16[128,1024]{1,0:T(8,128)(2,1)} %copy-done.1), channel_id=1, source_target_pairs={{0,2},{1,3},{2,4},{3,5},{4,6},{5,7},{6,0},{7,1},{8,10},{9,11},{10,... | collective-permute-start | bytes 786440 | tf_op jit(solution)/shard_map/ppermute | solution.py:74
  28.3 17.2 %collective-permute-start = (bf16[128,1024]{1,0:T(8,128)(2,1)}, bf16[128,1024]{1,0:T(8,128)(2,1)S(1)}, u32[]{:S(2)}, u32[]{:S(2)}) collective-permute-start(bf16[128,1024]{1,0:T(8,128)(2,1)} %copy-done.1), channel_id=1, source_target_pairs={{0,1},{1,2},{2,3},{3,4},{4,5},{5,6},{6,7},{7,0},{8,9},{9,10},{10,1... | collective-permute-start | bytes 786440 | tf_op jit(solution)/shard_map/ppermute | solution.py:74
  29.7 36.0 %copy-start.3 = (s32[3]{0:T(128)}, s32[3]{0:T(128)S(1)}, u32[]{:S(2)}) copy-start(s32[3]{0:T(128)S(1)} %pad_add_fusion.place) | copy-start | bytes 40
  57.9 1.6 %copy-start = (bf16[1024,1024]{1,0:T(8,128)(2,1)S(1)}, bf16[1024,1024]{1,0:T(8,128)(2,1)}, u32[]{:S(2)}) copy-start(bf16[1024,1024]{1,0:T(8,128)(2,1)} %all-gather.2.cloned.1.call-done.refs_8_) | copy-start | bytes 6291460
  59.5 0.9 copy-start.2
  112.3 22.3 %collective-permute-start.7 = (f32[5,128,128]{2,1,0:T(8,128)}, f32[5,128,128]{2,1,0:T(8,128)S(1)}, u32[]{:S(2)}, u32[]{:S(2)}) collective-permute-start(f32[5,128,128]{2,1,0:T(8,128)} %bitcast.13), channel_id=1, source_target_pairs={{0,0},{1,7},{2,6},{3,5},{4,4},{5,3},{6,2},{7,1},{8,8},{9,15},{10,1... | collective-permute-start | bytes 983048 | tf_op jit(solution)/shard_map/ppermute | solution.py:74
  117.2 12.5 %collective-permute-start.10 = (f32[128,128]{1,0:T(8,128)S(1)}, f32[128,128]{1,0:T(8,128)S(1)}, u32[]{:S(2)}, u32[]{:S(2)}) collective-permute-start(f32[128,128]{1,0:T(8,128)S(1)} %get-tuple-element.5), channel_id=1, source_target_pairs={{0,24},{1,25},{2,26},{3,27},{4,28},{5,29},{6,30},{7,31},{8,32},{9,... | collective-permute-start | bytes 196616 | tf_op jit(solution)/shard_map/ppermute | solution.py:74
  122.6 9.1 %collective-permute-start.9 = (f32[128,128]{1,0:T(8,128)S(1)}, f32[128,128]{1,0:T(8,128)S(1)}, u32[]{:S(2)}, u32[]{:S(2)}) collective-permute-start(f32[128,128]{1,0:T(8,128)S(1)} %get-tuple-element.6), channel_id=1, source_target_pairs={{0,16},{1,17},{2,18},{3,19},{4,20},{5,21},{6,22},{7,23},{8,24},{9,... | collective-permute-start | bytes 196616 | tf_op jit(solution)/shard_map/ppermute | solution.py:74
  127.3 7.4 %collective-permute-start.8 = (f32[128,128]{1,0:T(8,128)S(1)}, f32[128,128]{1,0:T(8,128)S(1)}, u32[]{:S(2)}, u32[]{:S(2)}) collective-permute-start(f32[128,128]{1,0:T(8,128)S(1)} %get-tuple-element.7), channel_id=1, source_target_pairs={{0,8},{1,9},{2,10},{3,11},{4,12},{5,13},{6,14},{7,15},{8,16},{9,17... | collective-permute-start | bytes 196616 | tf_op jit(solution)/shard_map/ppermute | solution.py:74
  129.7 5.0 %copy-start.5 = (f32[128,128]{1,0:T(8,128)}, f32[128,128]{1,0:T(8,128)S(1)}, u32[]{:S(2)}) copy-start(f32[128,128]{1,0:T(8,128)S(1)} %collective-permute-done.10.refs_2_) | copy-start | bytes 196612
  131.7 3.0 %copy-start.6 = (f32[128,128]{1,0:T(8,128)}, f32[128,128]{1,0:T(8,128)S(1)}, u32[]{:S(2)}) copy-start(f32[128,128]{1,0:T(8,128)S(1)} %collective-permute-done.9.refs_1_) | copy-start | bytes 196612
  134.6 0.6 copy-start.7
  134.7 0.7 copy-start.4
Sparse Core Ops, SparseCore 0:
  9.4 48.4 all-gather.1
  65.9 46.4 reduce-scatter.1

commit v2 on v1

v2 whole, which is shorter than its diff:
```python
import functools

import jax
import jax.numpy as jnp
from jax import lax
from jax.experimental import pallas as pl
from jax.experimental.pallas import tpu as pltpu
from jax.sharding import Mesh, PartitionSpec as P

STEP = 1.0
LASSO = 0.1
RIDGE = 0.5
AXES = ("z", "y", "k")
EARLY = (0, 1, 2)
LATE = (5, 4)
CHIP_STEPS = (0, 2, 6, 4)


def products(n, tile, depth, count, place, *refs):
    near, far = refs[:n // 2], refs[n // 2]
    columns, (out_ref, picked) = refs[n // 2 + 1:n // 2 + 1 + count], refs[n // 2 + 1 + count:]
    k = place[1]
    other = k + 1 - 2 * lax.rem(k, 2)
    for i, ref in enumerate(columns):
        picked[i * tile:(i + 1) * tile, :depth] = ref[:, depth:]
        picked[i * tile:(i + 1) * tile, depth:] = ref[:, :depth]
    for e in range(n):
        at = e // 2
        panel = near[at][...] if e % 2 == 0 else far[at * tile:(at + 1) * tile, :]
        home = k if e % 2 == 0 else other
        part = lax.dot_general(panel, picked[...], (((1,), (1,)), ((), ())), preferred_element_type=jnp.float32)
        m = lax.rem(home - CHIP_STEPS[at] + k + n, n)
        for i in range(count):
            out_ref[m, i] = part[:, i * tile:(i + 1) * tile]


def finish(n, tile, scale, place, active_ref, *refs):
    own, early, late, one, two, three, precision_ref, out_ref = refs
    y, k, z = place[0], place[1], place[2]
    row = lax.broadcasted_iota(jnp.int32, (tile, tile), 0)
    column = lax.broadcasted_iota(jnp.int32, (tile, tile), 1)
    found = (
        lambda: own[0].T, lambda: early[1], lambda: early[2], lambda: three[...].T,
        lambda: late[1], lambda: late[0], lambda: two[...].T, lambda: one[...].T,
    )
    for d in range(n):
        t = lax.rem(y + d, n)
        w = precision_ref[t]
        gradient = found[d]() * scale + RIDGE * w
        if d == 0:
            same_tile = lax.rem(2 * k - z + n, n) == 0
            on_diag = (row == column) & same_tile
            inverse = jnp.where(on_diag, 1.0 / jnp.where(on_diag, w, 1.0), 0.0)
            stepped = w - STEP * (gradient - inverse)
        else:
            stepped = w - STEP * gradient
        shrunk = jnp.where(
            stepped > 0, jnp.maximum(stepped - STEP * LASSO, 0.0), jnp.minimum(stepped + STEP * LASSO, 0.0)
        )
        if d == 0:
            shrunk = jnp.where(on_diag, stepped, shrunk)
        out_ref[t] = shrunk * active_ref[t].astype(jnp.float32)


def added(ref, out_ref):
    out_ref[...] = jnp.sum(ref[...], axis=0)


def local(n, resid, samples, precision, active):
    z, y, k = (lax.axis_index(a) for a in AXES)
    place = jnp.stack([y, k, z]).astype(jnp.int32)
    tile, depth = resid.shape
    vmem, smem = pl.BlockSpec(memory_space=pltpu.VMEM), pl.BlockSpec(memory_space=pltpu.SMEM)

    def moved(a, to):
        ids = [(z * n + y) * n + k for z in range(n) for y in range(n) for k in range(n)]
        ends = []
        for i in ids:
            c = to(i // (n * n), i // n % n, i % n)
            ends.append((c[0] % n * n + c[1] % n) * n + c[2] % n)
        return lax.ppermute(a, AXES, list(zip(ids, ends)))

    def multiplied(near, far, columns):
        count = len(columns)
        return pl.pallas_call(
            functools.partial(products, n, tile, depth, count),
            out_shape=jax.ShapeDtypeStruct((n, count, tile, tile), jnp.float32),
            in_specs=[smem] + [vmem] * (n // 2 + 1 + count),
            out_specs=vmem,
            scratch_shapes=[pltpu.VMEM((count * tile, 2 * depth), jnp.bfloat16)],
            compiler_params=pltpu.CompilerParams(vmem_limit_bytes=32 * 2**20),
            cost_estimate=pl.CostEstimate(
                flops=4 * n * count * tile * tile * depth, bytes_accessed=4 * 2**20, transcendentals=0
            ),
        )(place, *near, far, *columns)

    own = jnp.concatenate([resid, samples], axis=1)
    near = [own] + [moved(own, lambda z, y, k, s=s: (z, y, k + s)) for s in CHIP_STEPS[1:]]
    panel = {d: moved(own, lambda z, y, k, d=d: (z, y - d, k)) for d in (1, 2, 5, 4)}
    panel[0] = own
    far = moved(jnp.concatenate(near, axis=0), lambda z, y, k: (z, y, k ^ 1))
    early = lax.psum_scatter(
        multiplied(near, far, [panel[d] for d in EARLY]), "z", scatter_dimension=0, tiled=True
    )[0]
    parts = lax.all_to_all(multiplied(near, far, [panel[d] for d in LATE]), "z", 0, 0, tiled=True)
    late = pl.pallas_call(
        added, out_shape=jax.ShapeDtypeStruct(parts.shape[1:], jnp.float32), in_specs=[vmem], out_specs=vmem
    )(parts)
    three = moved(late[0], lambda z, y, k: (z, y + 5, k))
    late = moved(late, lambda z, y, k: (z, y, z - k))
    one = moved(early[1], lambda z, y, k: (z, y + 1, k))
    two = moved(early[2], lambda z, y, k: (z, y + 2, k))
    mirrored = moved(early, lambda z, y, k: (z, y, z - k))
    updated = pl.pallas_call(
        functools.partial(finish, n, tile, 0.5 / (depth * n)),
        out_shape=jax.ShapeDtypeStruct((n, tile, tile), jnp.float32),
        in_specs=[smem, smem] + [vmem] * 7,
        out_specs=vmem,
    )(place, active.reshape(n), early, mirrored, late, one, two, three, precision.reshape(n, tile, tile))
    return updated.reshape(precision.shape)


def solution(mesh):
    n = mesh.shape["blk"]
    grid = Mesh(mesh.devices.reshape(n, n, n), AXES)
    rows = ("y", "k")
    in_specs = (P(rows, "z"), P(rows, "z"), P(rows, "z"), P(rows, "z"))
    return jax.shard_map(
        functools.partial(local, n), mesh=grid, in_specs=in_specs, out_specs=P(rows, "z"), check_vma=False
    )
```

time: 145 us -> 172 us (1.19)
  blocking collectives: 0 us -> 40.1 us
  waiting for transfers between devices: 79.7 us -> 43.2 us
  starting transfers between devices: 36.8 us -> 59.4 us
  local copies, waits for them, and re-layouts: 6.72 us -> 4.25 us
  Pallas kernels: 7.7 us -> 10.1 us
    reduce_scatter x1, waiting for transfers between devices: 46.6 us -> 0.02 us  [local(): lax.psum_scatter(multiplied(near, far, [panel[d] for d in EARLY]), 'z', s...]
    all_to_all x0 -> x1, blocking collectives: none -> 40.1 us  [local(): lax.all_to_all(multiplied(near, far, [panel[d] for d in LATE]), 'z', 0, 0...]
    ppermute x11 -> x13, starting transfers between devices: 36.8 us -> 59.4 us  [moved(): return lax.ppermute(a, AXES, list(zip(ids, ends)))]
    ppermute x11 -> x13, waiting for transfers between devices: 20.7 us -> 43.2 us  [moved(): return lax.ppermute(a, AXES, list(zip(ids, ends)))]
    all_gather x1 -> x0, waiting for transfers between devices: 12.4 us -> none  [local(): column = lax.all_gather(own, 'y', axis=0, tiled=True)]
    unnamed x17 -> x13, local copies, waits for them, and re-layouts: 4.89 us -> 1.58 us
    pallas_call x2 -> x4, Pallas kernels: 7.7 us -> 10.1 us  [the longest x2 5.68 us: multiplied(): pl.pallas_call(functools.partial(products, n, tile, depth, count), out_sh...]
  transfers between devices with their start and end apart: 13 -> 14, of which waited for: 8 -> 6; matrix products, arithmetic and copies ran while one was open for 1% -> 1% of each run, Pallas kernels for 0% -> 2%
where the time goes in v2:
time: 172 us
  starting transfers between devices  59.4 us (35%)
  waiting for transfers between devices  43.2 us (25%)
  blocking collectives  40.1 us (23%)
  between operations  13.6 us (8%)
  Pallas kernels  10.1 us (6%)
  local copies, waits for them, and re-layouts  4.25 us (2%)
    ppermute x13, starting transfers between devices, moved(): return lax.ppermute(a, AXES, list(zip(ids, ends)))  59.4 us
    ppermute x13, waiting for transfers between devices, moved(): return lax.ppermute(a, AXES, list(zip(ids, ends)))  43.2 us
    all_to_all x1, blocking collectives, local(): lax.all_to_all(multiplied(near, far, [panel[d] for d in LATE]), 'z', 0, 0...  40.1 us
    pallas_call x2, Pallas kernels, multiplied(): pl.pallas_call(functools.partial(products, n, tile, depth, count), out_sh...  5.68 us
  transfers between devices with their start and end apart: 14, of which 6 were waited for; matrix products, arithmetic and copies ran while one was open for 1% of the time, Pallas kernels for 2%

profile of v2, /device:TPU:2, one launch (start us, length us, event | category | flops | bytes accessed | tf_op | source)
XLA Modules:
  0.0 171.8 jit_solution(15565794315874974108)
XLA Ops:
  6.5 0.9 constant_dynamic-update-slice_fusion.1
  7.5 0.9 constant_dynamic-update-slice_fusion.refs_0_.refs_5_
  8.4 3.4 %collective-permute-start = (bf16[128,1024]{1,0:T(8,128)(2,1)S(1)}, bf16[128,1024]{1,0:T(8,128)(2,1)S(1)}, u32[]{:S(2)}, u32[]{:S(2)}) collective-permute-start(bf16[128,1024]{1,0:T(8,128)(2,1)S(1)} %constant_dynamic-update-slice_fusion.refs_0_.refs_5_), channel_id=1, source_target_pairs={{0,2},{1,3},{2,4},{3,5},{4,6},{5,7},{6,0},{7,1},{8,10},{9,11},{10,... | collective-permute-start | bytes 786440 | tf_op jit(solution)/shard_map/ppermute | solution.py:81
  11.8 6.3 %collective-permute-start.1 = (bf16[128,1024]{1,0:T(8,128)(2,1)S(1)}, bf16[128,1024]{1,0:T(8,128)(2,1)S(1)}, u32[]{:S(2)}, u32[]{:S(2)}) collective-permute-start(bf16[128,1024]{1,0:T(8,128)(2,1)S(1)} %constant_dynamic-update-slice_fusion.refs_0_.refs_5_), channel_id=1, source_target_pairs={{0,6},{1,7},{2,0},{3,1},{4,2},{5,3},{6,4},{7,5},{8,14},{9,15},{10,... | collective-permute-start | bytes 786440 | tf_op jit(solution)/shard_map/ppermute | solution.py:81
  18.1 4.0 %collective-permute-start.2 = (bf16[128,1024]{1,0:T(8,128)(2,1)S(1)}, bf16[128,1024]{1,0:T(8,128)(2,1)S(1)}, u32[]{:S(2)}, u32[]{:S(2)}) collective-permute-start(bf16[128,1024]{1,0:T(8,128)(2,1)S(1)} %constant_dynamic-update-slice_fusion.refs_0_.refs_5_), channel_id=1, source_target_pairs={{0,4},{1,5},{2,6},{3,7},{4,0},{5,1},{6,2},{7,3},{8,12},{9,13},{10,... | collective-permute-start | bytes 786440 | tf_op jit(solution)/shard_map/ppermute | solution.py:81
  22.1 2.1 %collective-permute-done.1.refs_2_ = bf16[128,1024]{1,0:T(8,128)(2,1)S(1)} collective-permute-done((bf16[128,1024]{1,0:T(8,128)(2,1)S(1)}, bf16[128,1024]{1,0:T(8,128)(2,1)S(1)}, u32[]{:S(2)}, u32[]{:S(2)}) %collective-permute-start.1) | collective-permute-done | bytes 262176 | tf_op jit(solution)/shard_map/ppermute | solution.py:81
  24.2 3.7 %collective-permute-done.2.refs_3_ = bf16[128,1024]{1,0:T(8,128)(2,1)S(1)} collective-permute-done((bf16[128,1024]{1,0:T(8,128)(2,1)S(1)}, bf16[128,1024]{1,0:T(8,128)(2,1)S(1)}, u32[]{:S(2)}, u32[]{:S(2)}) %collective-permute-start.2) | collective-permute-done | bytes 262176 | tf_op jit(solution)/shard_map/ppermute | solution.py:81
  28.0 1.1 pad_maximum_fusion
  29.0 1.9 %collective-permute-start.3 = (bf16[512,1024]{1,0:T(8,128)(2,1)}, bf16[512,1024]{1,0:T(8,128)(2,1)S(1)}, u32[]{:S(2)}, u32[]{:S(2)}) collective-permute-start(bf16[512,1024]{1,0:T(8,128)(2,1)} %pad_maximum_fusion), channel_id=1, source_target_pairs={{0,1},{1,0},{2,3},{3,2},{4,5},{5,4},{6,7},{7,6},{8,9},{9,8},{10,11... | collective-permute-start | bytes 3145736 | tf_op jit(solution)/shard_map/ppermute | solution.py:81
  30.9 5.1 %collective-permute-start.4 = (bf16[128,1024]{1,0:T(8,128)(2,1)S(1)}, bf16[128,1024]{1,0:T(8,128)(2,1)S(1)}, u32[]{:S(2)}, u32[]{:S(2)}) collective-permute-start(bf16[128,1024]{1,0:T(8,128)(2,1)S(1)} %constant_dynamic-update-slice_fusion.refs_0_.refs_5_), channel_id=1, source_target_pairs={{0,56},{1,57},{2,58},{3,59},{4,60},{5,61},{6,62},{7,63},{8,0},{9,1... | collective-permute-start | bytes 786440 | tf_op jit(solution)/shard_map/ppermute | solution.py:81
  36.1 4.0 %collective-permute-start.5 = (bf16[128,1024]{1,0:T(8,128)(2,1)S(1)}, bf16[128,1024]{1,0:T(8,128)(2,1)S(1)}, u32[]{:S(2)}, u32[]{:S(2)}) collective-permute-start(bf16[128,1024]{1,0:T(8,128)(2,1)S(1)} %constant_dynamic-update-slice_fusion.refs_0_.refs_5_), channel_id=1, source_target_pairs={{0,48},{1,49},{2,50},{3,51},{4,52},{5,53},{6,54},{7,55},{8,56},{9,... | collective-permute-start | bytes 786440 | tf_op jit(solution)/shard_map/ppermute | solution.py:81
  40.1 0.1 pad_add_fusion.place
  40.2 5.3 %collective-permute-done.4.refs_6_ = bf16[128,1024]{1,0:T(8,128)(2,1)S(1)} collective-permute-done((bf16[128,1024]{1,0:T(8,128)(2,1)S(1)}, bf16[128,1024]{1,0:T(8,128)(2,1)S(1)}, u32[]{:S(2)}, u32[]{:S(2)}) %collective-permute-start.4) | collective-permute-done | bytes 262176 | tf_op jit(solution)/shard_map/ppermute | solution.py:81
  45.5 8.0 %collective-permute-done.5.refs_7_ = bf16[128,1024]{1,0:T(8,128)(2,1)S(1)} collective-permute-done((bf16[128,1024]{1,0:T(8,128)(2,1)S(1)}, bf16[128,1024]{1,0:T(8,128)(2,1)S(1)}, u32[]{:S(2)}, u32[]{:S(2)}) %collective-permute-start.5) | collective-permute-done | bytes 262176 | tf_op jit(solution)/shard_map/ppermute | solution.py:81
  53.5 3.7 %shard_map.46 = f32[8,3,128,128]{3,2,1,0:T(8,128)} custom-call(s32[3]{0:T(128)S(1)} %pad_add_fusion.place, bf16[128,1024]{1,0:T(8,128)(2,1)S(1)} %constant_dynamic-update-slice_fusion.refs_0_.refs_5_, bf16[128,1024]{1,0:T(8,128)(2,1)S(1)} %collective-permute-done.refs_1_, bf16[128,1024]{1,0:T(8,128)(2,1)S(1)} %collective-permute-done.1.refs_2_, ...), custom_call_target="tpu_custom_call" | custom-call | flops 805306368 | bytes 4194304 | tf_op jit(solution)/shard_map/pallas_call | solution.py:85
  57.2 2.1 %collective-permute-start.7 = (bf16[128,1024]{1,0:T(8,128)(2,1)S(1)}, bf16[128,1024]{1,0:T(8,128)(2,1)S(1)}, u32[]{:S(2)}, u32[]{:S(2)}) collective-permute-start(bf16[128,1024]{1,0:T(8,128)(2,1)S(1)} %constant_dynamic-update-slice_fusion.refs_0_.refs_5_), channel_id=1, source_target_pairs={{0,24},{1,25},{2,26},{3,27},{4,28},{5,29},{6,30},{7,31},{8,32},{9,... | collective-permute-start | bytes 786440 | tf_op jit(solution)/shard_map/ppermute | solution.py:81
  59.3 6.7 %collective-permute-start.8 = (bf16[128,1024]{1,0:T(8,128)(2,1)S(1)}, bf16[128,1024]{1,0:T(8,128)(2,1)S(1)}, u32[]{:S(2)}, u32[]{:S(2)}) collective-permute-start(bf16[128,1024]{1,0:T(8,128)(2,1)S(1)} %constant_dynamic-update-slice_fusion.refs_0_.refs_5_), channel_id=1, source_target_pairs={{0,32},{1,33},{2,34},{3,35},{4,36},{5,37},{6,38},{7,39},{8,40},{9,... | collective-permute-start | bytes 786440 | tf_op jit(solution)/shard_map/ppermute | solution.py:81
  66.0 17.7 %collective-permute-done.7.refs_5_ = bf16[128,1024]{1,0:T(8,128)(2,1)S(1)} collective-permute-done((bf16[128,1024]{1,0:T(8,128)(2,1)S(1)}, bf16[128,1024]{1,0:T(8,128)(2,1)S(1)}, u32[]{:S(2)}, u32[]{:S(2)}) %collective-permute-start.7) | collective-permute-done | bytes 262176 | tf_op jit(solution)/shard_map/ppermute | solution.py:81
  83.7 2.0 %shard_map.47 = f32[8,2,128,128]{3,2,1,0:T(8,128)S(1)} custom-call(s32[3]{0:T(128)S(1)} %pad_add_fusion.place, bf16[128,1024]{1,0:T(8,128)(2,1)S(1)} %constant_dynamic-update-slice_fusion.refs_0_.refs_5_, bf16[128,1024]{1,0:T(8,128)(2,1)S(1)} %collective-permute-done.refs_1_, bf16[128,1024]{1,0:T(8,128)(2,1)S(1)} %collective-permute-done.1.refs_2_, ...), custom_call_target="tpu_custom_call" | custom-call | flops 536870912 | bytes 4194304 | tf_op jit(solution)/shard_map/pallas_call | solution.py:85
  85.7 40.1 %all_to_all.5.ref = f32[8,2,128,128]{3,2,1,0:T(8,128)} all-to-all(f32[8,2,128,128]{3,2,1,0:T(8,128)S(1)} %shard_map.47), channel_id=1, replica_groups=mesh['z'=8,'y'=8,'k'=8] {'z'}, dimensions={0} | all-to-all | bytes 2097152 | tf_op jit(solution)/shard_map/all_to_all | solution.py:105
  125.8 1.9 %shard_map.48 = f32[2,128,128]{2,1,0:T(8,128)} custom-call(f32[8,2,128,128]{3,2,1,0:T(8,128)} %all_to_all.5.ref), custom_call_target="tpu_custom_call" | custom-call | tf_op jit(solution)/shard_map/pallas_call | solution.py:106
  127.8 3.5 %collective-permute-start.9 = (f32[2,128,128]{2,1,0:T(8,128)}, f32[2,128,128]{2,1,0:T(8,128)S(1)}, u32[]{:S(2)}, u32[]{:S(2)}) collective-permute-start(f32[2,128,128]{2,1,0:T(8,128)} %shard_map.48), channel_id=1, source_target_pairs={{0,0},{1,7},{2,6},{3,5},{4,4},{5,3},{6,2},{7,1},{8,8},{9,15},{10,1... | collective-permute-start | bytes 393224 | tf_op jit(solution)/shard_map/ppermute | solution.py:81
  131.3 0.9 slice_bitcast_fusion
  132.2 6.4 %collective-permute-start.12 = (f32[128,128]{1,0:T(8,128)S(1)}, f32[128,128]{1,0:T(8,128)S(1)}, u32[]{:S(2)}, u32[]{:S(2)}) collective-permute-start(f32[128,128]{1,0:T(8,128)S(1)} %slice_bitcast_fusion), channel_id=1, source_target_pairs={{0,40},{1,41},{2,42},{3,43},{4,44},{5,45},{6,46},{7,47},{8,48},{9,... | collective-permute-start | bytes 196616 | tf_op jit(solution)/shard_map/ppermute | solution.py:81
  138.6 3.9 %collective-permute-start.6 = (f32[3,128,128]{2,1,0:T(8,128)}, f32[3,128,128]{2,1,0:T(8,128)S(1)}, u32[]{:S(2)}, u32[]{:S(2)}) collective-permute-start(f32[3,128,128]{2,1,0:T(8,128)} %bitcast.13), channel_id=1, source_target_pairs={{0,0},{1,7},{2,6},{3,5},{4,4},{5,3},{6,2},{7,1},{8,8},{9,15},{10,1... | collective-permute-start | bytes 589832 | tf_op jit(solution)/shard_map/ppermute | solution.py:81
  142.4 0.9 slice_bitcast_fusion.1
  143.3 10.2 %collective-permute-start.10 = (f32[128,128]{1,0:T(8,128)S(1)}, f32[128,128]{1,0:T(8,128)S(1)}, u32[]{:S(2)}, u32[]{:S(2)}) collective-permute-start(f32[128,128]{1,0:T(8,128)S(1)} %get-tuple-element.6), channel_id=1, source_target_pairs={{0,8},{1,9},{2,10},{3,11},{4,12},{5,13},{6,14},{7,15},{8,16},{9,17... | collective-permute-start | bytes 196616 | tf_op jit(solution)/shard_map/ppermute | solution.py:81
  153.6 1.9 %collective-permute-start.11 = (f32[128,128]{1,0:T(8,128)S(1)}, f32[128,128]{1,0:T(8,128)S(1)}, u32[]{:S(2)}, u32[]{:S(2)}) collective-permute-start(f32[128,128]{1,0:T(8,128)S(1)} %get-tuple-element.5), channel_id=1, source_target_pairs={{0,16},{1,17},{2,18},{3,19},{4,20},{5,21},{6,22},{7,23},{8,24},{9,... | collective-permute-start | bytes 196616 | tf_op jit(solution)/shard_map/ppermute | solution.py:81
  155.6 6.3 %collective-permute-done.11.refs_4_ = f32[128,128]{1,0:T(8,128)S(1)} collective-permute-done((f32[128,128]{1,0:T(8,128)S(1)}, f32[128,128]{1,0:T(8,128)S(1)}, u32[]{:S(2)}, u32[]{:S(2)}) %collective-permute-start.11) | collective-permute-done | bytes 65568 | tf_op jit(solution)/shard_map/ppermute | solution.py:81
  161.9 0.6 copy-done.5
  162.5 0.1 copy-done.1
  162.5 2.4 %shard_map.49 = f32[8,128,128]{2,1,0:T(8,128)} custom-call(s32[3]{0:T(128)} %copy-done, s32[8]{0:T(128)} %bitcast.16, f32[3,128,128]{2,1,0:T(8,128)} %bitcast.14, f32[3,128,128]{2,1,0:T(8,128)} %copy-done.1, f32[2,128,128]{2,1,0:T(8,128)} %copy-done.2, f32[128,128]{1,0:T(8,128)} %copy-done.4, f32[128,128]{1,0:T(8,128)} %copy-done.5, f32[128,128]{1,0:T(8,128)} %copy-done.3, ...), custom_call_target="tpu_custom_call" | custom-call | tf_op jit(solution)/shard_map/pallas_call | solution.py:114
  (20 shorter events, 0.1 us)
Async XLA Ops:
  6.5 132.0 %reduce-scatter.2.cloned.1.call-start = ((), (), s32[]{:S(2)}) async-start(), calls=%async_computation.2 | async-start | bytes 1769472 | tf_op jit(solution)/shard_map/reduce_scatter | solution.py:102
  8.4 13.7 %collective-permute-start = (bf16[128,1024]{1,0:T(8,128)(2,1)S(1)}, bf16[128,1024]{1,0:T(8,128)(2,1)S(1)}, u32[]{:S(2)}, u32[]{:S(2)}) collective-permute-start(bf16[128,1024]{1,0:T(8,128)(2,1)S(1)} %constant_dynamic-update-slice_fusion.refs_0_.refs_5_), channel_id=1, source_target_pairs={{0,2},{1,3},{2,4},{3,5},{4,6},{5,7},{6,0},{7,1},{8,10},{9,11},{10,... | collective-permute-start | bytes 786440 | tf_op jit(solution)/shard_map/ppermute | solution.py:81
  11.8 12.5 %collective-permute-start.1 = (bf16[128,1024]{1,0:T(8,128)(2,1)S(1)}, bf16[128,1024]{1,0:T(8,128)(2,1)S(1)}, u32[]{:S(2)}, u32[]{:S(2)}) collective-permute-start(bf16[128,1024]{1,0:T(8,128)(2,1)S(1)} %constant_dynamic-update-slice_fusion.refs_0_.refs_5_), channel_id=1, source_target_pairs={{0,6},{1,7},{2,0},{3,1},{4,2},{5,3},{6,4},{7,5},{8,14},{9,15},{10,... | collective-permute-start | bytes 786440 | tf_op jit(solution)/shard_map/ppermute | solution.py:81
  18.1 9.8 %collective-permute-start.2 = (bf16[128,1024]{1,0:T(8,128)(2,1)S(1)}, bf16[128,1024]{1,0:T(8,128)(2,1)S(1)}, u32[]{:S(2)}, u32[]{:S(2)}) collective-permute-start(bf16[128,1024]{1,0:T(8,128)(2,1)S(1)} %constant_dynamic-update-slice_fusion.refs_0_.refs_5_), channel_id=1, source_target_pairs={{0,4},{1,5},{2,6},{3,7},{4,0},{5,1},{6,2},{7,3},{8,12},{9,13},{10,... | collective-permute-start | bytes 786440 | tf_op jit(solution)/shard_map/ppermute | solution.py:81
  29.0 24.5 %collective-permute-start.3 = (bf16[512,1024]{1,0:T(8,128)(2,1)}, bf16[512,1024]{1,0:T(8,128)(2,1)S(1)}, u32[]{:S(2)}, u32[]{:S(2)}) collective-permute-start(bf16[512,1024]{1,0:T(8,128)(2,1)} %pad_maximum_fusion), channel_id=1, source_target_pairs={{0,1},{1,0},{2,3},{3,2},{4,5},{5,4},{6,7},{7,6},{8,9},{9,8},{10,11... | collective-permute-start | bytes 3145736 | tf_op jit(solution)/shard_map/ppermute | solution.py:81
  30.9 14.6 %collective-permute-start.4 = (bf16[128,1024]{1,0:T(8,128)(2,1)S(1)}, bf16[128,1024]{1,0:T(8,128)(2,1)S(1)}, u32[]{:S(2)}, u32[]{:S(2)}) collective-permute-start(bf16[128,1024]{1,0:T(8,128)(2,1)S(1)} %constant_dynamic-update-slice_fusion.refs_0_.refs_5_), channel_id=1, source_target_pairs={{0,56},{1,57},{2,58},{3,59},{4,60},{5,61},{6,62},{7,63},{8,0},{9,1... | collective-permute-start | bytes 786440 | tf_op jit(solution)/shard_map/ppermute | solution.py:81
  36.1 17.5 %collective-permute-start.5 = (bf16[128,1024]{1,0:T(8,128)(2,1)S(1)}, bf16[128,1024]{1,0:T(8,128)(2,1)S(1)}, u32[]{:S(2)}, u32[]{:S(2)}) collective-permute-start(bf16[128,1024]{1,0:T(8,128)(2,1)S(1)} %constant_dynamic-update-slice_fusion.refs_0_.refs_5_), channel_id=1, source_target_pairs={{0,48},{1,49},{2,50},{3,51},{4,52},{5,53},{6,54},{7,55},{8,56},{9,... | collective-permute-start | bytes 786440 | tf_op jit(solution)/shard_map/ppermute | solution.py:81
  40.2 43.5 %copy-start = (s32[3]{0:T(128)}, s32[3]{0:T(128)S(1)}, u32[]{:S(2)}) copy-start(s32[3]{0:T(128)S(1)} %pad_add_fusion.place) | copy-start | bytes 40
  57.2 26.5 %collective-permute-start.7 = (bf16[128,1024]{1,0:T(8,128)(2,1)S(1)}, bf16[128,1024]{1,0:T(8,128)(2,1)S(1)}, u32[]{:S(2)}, u32[]{:S(2)}) collective-permute-start(bf16[128,1024]{1,0:T(8,128)(2,1)S(1)} %constant_dynamic-update-slice_fusion.refs_0_.refs_5_), channel_id=1, source_target_pairs={{0,24},{1,25},{2,26},{3,27},{4,28},{5,29},{6,30},{7,31},{8,32},{9,... | collective-permute-start | bytes 786440 | tf_op jit(solution)/shard_map/ppermute | solution.py:81
  59.3 24.4 %collective-permute-start.8 = (bf16[128,1024]{1,0:T(8,128)(2,1)S(1)}, bf16[128,1024]{1,0:T(8,128)(2,1)S(1)}, u32[]{:S(2)}, u32[]{:S(2)}) collective-permute-start(bf16[128,1024]{1,0:T(8,128)(2,1)S(1)} %constant_dynamic-update-slice_fusion.refs_0_.refs_5_), channel_id=1, source_target_pairs={{0,32},{1,33},{2,34},{3,35},{4,36},{5,37},{6,38},{7,39},{8,40},{9,... | collective-permute-start | bytes 786440 | tf_op jit(solution)/shard_map/ppermute | solution.py:81
  127.8 27.8 %collective-permute-start.9 = (f32[2,128,128]{2,1,0:T(8,128)}, f32[2,128,128]{2,1,0:T(8,128)S(1)}, u32[]{:S(2)}, u32[]{:S(2)}) collective-permute-start(f32[2,128,128]{2,1,0:T(8,128)} %shard_map.48), channel_id=1, source_target_pairs={{0,0},{1,7},{2,6},{3,5},{4,4},{5,3},{6,2},{7,1},{8,8},{9,15},{10,1... | collective-permute-start | bytes 393224 | tf_op jit(solution)/shard_map/ppermute | solution.py:81
  132.2 23.3 %collective-permute-start.12 = (f32[128,128]{1,0:T(8,128)S(1)}, f32[128,128]{1,0:T(8,128)S(1)}, u32[]{:S(2)}, u32[]{:S(2)}) collective-permute-start(f32[128,128]{1,0:T(8,128)S(1)} %slice_bitcast_fusion), channel_id=1, source_target_pairs={{0,40},{1,41},{2,42},{3,43},{4,44},{5,45},{6,46},{7,47},{8,48},{9,... | collective-permute-start | bytes 196616 | tf_op jit(solution)/shard_map/ppermute | solution.py:81
  138.6 23.3 %collective-permute-start.6 = (f32[3,128,128]{2,1,0:T(8,128)}, f32[3,128,128]{2,1,0:T(8,128)S(1)}, u32[]{:S(2)}, u32[]{:S(2)}) collective-permute-start(f32[3,128,128]{2,1,0:T(8,128)} %bitcast.13), channel_id=1, source_target_pairs={{0,0},{1,7},{2,6},{3,5},{4,4},{5,3},{6,2},{7,1},{8,8},{9,15},{10,1... | collective-permute-start | bytes 589832 | tf_op jit(solution)/shard_map/ppermute | solution.py:81
  143.3 12.2 %collective-permute-start.10 = (f32[128,128]{1,0:T(8,128)S(1)}, f32[128,128]{1,0:T(8,128)S(1)}, u32[]{:S(2)}, u32[]{:S(2)}) collective-permute-start(f32[128,128]{1,0:T(8,128)S(1)} %get-tuple-element.6), channel_id=1, source_target_pairs={{0,8},{1,9},{2,10},{3,11},{4,12},{5,13},{6,14},{7,15},{8,16},{9,17... | collective-permute-start | bytes 196616 | tf_op jit(solution)/shard_map/ppermute | solution.py:81
  153.6 8.3 %collective-permute-start.11 = (f32[128,128]{1,0:T(8,128)S(1)}, f32[128,128]{1,0:T(8,128)S(1)}, u32[]{:S(2)}, u32[]{:S(2)}) collective-permute-start(f32[128,128]{1,0:T(8,128)S(1)} %get-tuple-element.5), channel_id=1, source_target_pairs={{0,16},{1,17},{2,18},{3,19},{4,20},{5,21},{6,22},{7,23},{8,24},{9,... | collective-permute-start | bytes 196616 | tf_op jit(solution)/shard_map/ppermute | solution.py:81
  155.5 6.3 %copy-start.3 = (f32[128,128]{1,0:T(8,128)}, f32[128,128]{1,0:T(8,128)S(1)}, u32[]{:S(2)}) copy-start(f32[128,128]{1,0:T(8,128)S(1)} %collective-permute-done.12.refs_5_) | copy-start | bytes 196612
  155.5 6.3 %copy-start.2 = (f32[2,128,128]{2,1,0:T(8,128)}, f32[2,128,128]{2,1,0:T(8,128)S(1)}, u32[]{:S(2)}) copy-start(f32[2,128,128]{2,1,0:T(8,128)S(1)} %collective-permute-done.9.refs_2_) | copy-start | bytes 393220
  155.5 6.3 %copy-start.4 = (f32[128,128]{1,0:T(8,128)}, f32[128,128]{1,0:T(8,128)S(1)}, u32[]{:S(2)}) copy-start(f32[128,128]{1,0:T(8,128)S(1)} %collective-permute-done.10.refs_3_) | copy-start | bytes 196612
  161.8 0.6 copy-start.5
  161.8 0.7 copy-start.1
Sparse Core Ops, SparseCore 0:
  57.3 51.3 reduce-scatter.1

commit v3 on v1

v3 whole, which is shorter than its diff:
```python
import functools

import jax
import jax.numpy as jnp
from jax import lax
from jax.experimental import pallas as pl
from jax.experimental.pallas import tpu as pltpu
from jax.sharding import Mesh, PartitionSpec as P

STEP = 1.0
LASSO = 0.1
RIDGE = 0.5
AXES = ("z", "y", "k")
DIRECT = (0, 7, 2, 3, 4)
TURNED = (1, 2, 3)


def products(tile, depth, place, panel, *refs):
    columns, (out_ref, picked) = refs[:-2], refs[-2:]

    @pl.when(pl.program_id(0) == 0)
    def _():
        for i, ref in enumerate(columns):
            picked[i * tile:(i + 1) * tile, :depth] = ref[:, depth:]
            picked[i * tile:(i + 1) * tile, depth:] = ref[:, :depth]

    part = lax.dot_general(panel[...], picked[...], (((1,), (1,)), ((), ())), preferred_element_type=jnp.float32)
    for i in range(len(columns)):
        out_ref[0, i] = part[:, i * tile:(i + 1) * tile]


def proximal(total, w, scale, inverse=0.0):
    stepped = w - STEP * (total * scale + RIDGE * w - inverse)
    shrunk = jnp.where(
        stepped > 0, jnp.maximum(stepped - STEP * LASSO, 0.0), jnp.minimum(stepped + STEP * LASSO, 0.0)
    )
    return stepped, shrunk


def finish_direct(n, tile, scale, place, active_ref, summed, precision_ref, out_ref):
    y, k, z = place[0], place[1], place[2]
    row = lax.broadcasted_iota(jnp.int32, (tile, tile), 0)
    column = lax.broadcasted_iota(jnp.int32, (tile, tile), 1)
    for i, d in enumerate(DIRECT):
        t = lax.rem(y + d, n)
        w = precision_ref[t]
        if d == 0:
            on_diag = (row == column) & (lax.rem(2 * k - z + n, n) == 0)
            inverse = jnp.where(on_diag, 1.0 / jnp.where(on_diag, w, 1.0), 0.0)
            stepped, shrunk = proximal(summed[i], w, scale, inverse)
            shrunk = jnp.where(on_diag, stepped, shrunk)
        else:
            _, shrunk = proximal(summed[i], w, scale)
        out_ref[t] = shrunk * active_ref[t].astype(jnp.float32)


def finish_turned(n, scale, place, active_ref, *refs):
    arrived, (precision_ref, _, out_ref) = refs[:-3], refs[-3:]
    for i, a in enumerate(arrived):

        @pl.when(pl.program_id(0) == i)
        def _(a=a, d=n - DIRECT[TURNED[i]]):
            t = lax.rem(place[0] + d, n)
            _, shrunk = proximal(a[...].T, precision_ref[0], scale)
            out_ref[0] = shrunk * active_ref[t].astype(jnp.float32)


def local(n, resid, samples, precision, active):
    z, y, k = (lax.axis_index(a) for a in AXES)
    place = jnp.stack([y, k, z]).astype(jnp.int32)
    tile, depth = resid.shape
    vmem, smem = pl.BlockSpec(memory_space=pltpu.VMEM), pl.BlockSpec(memory_space=pltpu.SMEM)

    def index(z, y, k):
        return (z % n * n + y % n) * n + k % n

    def moved(a, to):
        ids = [(z, y, k) for z in range(n) for y in range(n) for k in range(n)]
        return lax.ppermute(a, AXES, [(index(*i), index(*to(*i))) for i in ids])

    own = jnp.concatenate([resid, samples], axis=1)
    rows = lax.all_gather(own, "k", axis=0, tiled=True)
    columns = [moved(own, lambda z, y, k, d=d: (z, y - d, z - k)) for d in DIRECT]
    whole = pl.BlockSpec((tile, 2 * depth), lambda e, place: (0, 0))
    partial = pl.pallas_call(
        functools.partial(products, tile, depth),
        out_shape=jax.ShapeDtypeStruct((n, len(DIRECT), tile, tile), jnp.float32),
        grid_spec=pltpu.PrefetchScalarGridSpec(
            num_scalar_prefetch=1,
            grid=(n,),
            in_specs=[pl.BlockSpec((tile, 2 * depth), lambda e, place: (e, 0))] + [whole] * len(DIRECT),
            out_specs=pl.BlockSpec(
                (1, len(DIRECT), tile, tile),
                lambda e, place: (lax.rem(e + place[2] - place[1] + n, n), 0, 0, 0),
            ),
            scratch_shapes=[pltpu.VMEM((len(DIRECT) * tile, 2 * depth), jnp.bfloat16)],
        ),
        compiler_params=pltpu.CompilerParams(vmem_limit_bytes=60 * 2**20),
        cost_estimate=pl.CostEstimate(
            flops=4 * n * len(DIRECT) * tile * tile * depth, bytes_accessed=5 * 2**20, transcendentals=0
        ),
    )(place, rows, *columns)
    diagonals = [[index(z, y, z - k) for z in range(n)] for y in range(n) for k in range(n)]
    summed = lax.psum_scatter(partial, AXES, scatter_dimension=0, axis_index_groups=diagonals, tiled=True)[0]
    arrived = [
        moved(summed[i], lambda z, y, k, d=DIRECT[i]: (z, y + d, z - k)) for i in TURNED
    ]
    scale = 0.5 / (depth * n)
    flags, tiles = active.reshape(n), precision.reshape(n, tile, tile)
    updated = pl.pallas_call(
        functools.partial(finish_direct, n, tile, scale),
        out_shape=jax.ShapeDtypeStruct((n, tile, tile), jnp.float32),
        in_specs=[smem, smem, vmem, vmem],
        out_specs=vmem,
    )(place, flags, summed, tiles)

    def turned_tile(i, place, flags):
        d = jnp.where(i == 0, n - DIRECT[TURNED[0]], jnp.where(i == 1, n - DIRECT[TURNED[1]], n - DIRECT[TURNED[2]]))
        return lax.rem(place[0] + d, n), 0, 0

    one = pl.BlockSpec((1, tile, tile), turned_tile)
    updated = pl.pallas_call(
        functools.partial(finish_turned, n, scale),
        out_shape=jax.ShapeDtypeStruct((n, tile, tile), jnp.float32),
        grid_spec=pltpu.PrefetchScalarGridSpec(
            num_scalar_prefetch=2,
            grid=(len(TURNED),),
            in_specs=[pl.BlockSpec((tile, tile), lambda i, place, flags: (0, 0))] * len(TURNED)
            + [one, pl.BlockSpec(memory_space=pl.ANY)],
            out_specs=one,
        ),
        input_output_aliases={3 + len(TURNED): 0},
    )(place, flags, *arrived, tiles, updated)
    return updated.reshape(precision.shape)


def solution(mesh):
    n = mesh.shape["blk"]
    grid = Mesh(mesh.devices.reshape(n, n, n), AXES)
    rows = ("y", "k")
    in_specs = (P(rows, "z"), P(rows, "z"), P(rows, "z"), P(rows, "z"))
    return jax.shard_map(
        functools.partial(local, n), mesh=grid, in_specs=in_specs, out_specs=P(rows, "z"), check_vma=False
    )
```

time: 145 us -> 157 us (1.083)
  the two profiles are of different devices: /device:TPU:2 before, /device:TPU:1 now
where the time goes in v3:
time: 157 us; the launch traced here: 156 us
  waiting for transfers between devices  81.1 us (52%)
  starting transfers between devices  41.9 us (27%)
  Pallas kernels  14.4 us (9%)
  between operations  13.5 us (9%)
  local copies, waits for them, and re-layouts  4.7 us (3%)
    reduce_scatter x1, waiting for transfers between devices, local(): lax.psum_scatter(partial, AXES, scatter_dimension=0, axis_index_groups=di...  48.6 us
    ppermute x8, starting transfers between devices, moved(): return lax.ppermute(a, AXES, [(index(*i), index(*to(*i))) for i in ids])  41.9 us
    ppermute x8, waiting for transfers between devices, moved(): return lax.ppermute(a, AXES, [(index(*i), index(*to(*i))) for i in ids])  27 us
    pallas_call x1, Pallas kernels, local(): pl.pallas_call(functools.partial(products, tile, depth), out_shape=jax.Sh...  8.88 us
    all_gather x1, waiting for transfers between devices, local(): rows = lax.all_gather(own, 'k', axis=0, tiled=True)  5.52 us
    pallas_call x1, Pallas kernels, local(): pl.pallas_call(functools.partial(finish_turned, n, scale), out_shape=jax....  3.37 us
  transfers between devices with their start and end apart: 10, of which 5 were waited for; matrix products, arithmetic and copies ran while one was open for 0% of the time, Pallas kernels for 1%

profile of v3, /device:TPU:1, one launch (start us, length us, event | category | flops | bytes accessed | tf_op | source)
XLA Modules:
  0.0 156.3 jit_solution(14557128539483606043)
XLA Ops:
  6.5 0.9 constant_dynamic-update-slice_fusion.1
  7.5 0.9 constant_dynamic-update-slice_fusion
  8.4 0.0 copy-start
  8.4 0.7 copy-done
  9.1 0.0 all-gather.2.cloned.1.call-update
  9.1 0.0 reduce-scatter.2.cloned.1.call-start
  9.2 10.5 %collective-permute-start.4 = (bf16[128,1024]{1,0:T(8,128)(2,1)}, bf16[128,1024]{1,0:T(8,128)(2,1)S(1)}, u32[]{:S(2)}, u32[]{:S(2)}) collective-permute-start(bf16[128,1024]{1,0:T(8,128)(2,1)} %copy-done), channel_id=1, source_target_pairs={{0,32},{1,39},{2,38},{3,37},{4,36},{5,35},{6,34},{7,33},{8,40},{9,... | collective-permute-start | bytes 786440 | tf_op jit(solution)/shard_map/ppermute | solution.py:79
  19.6 1.9 %collective-permute-start.3 = (bf16[128,1024]{1,0:T(8,128)(2,1)}, bf16[128,1024]{1,0:T(8,128)(2,1)S(1)}, u32[]{:S(2)}, u32[]{:S(2)}) collective-permute-start(bf16[128,1024]{1,0:T(8,128)(2,1)} %copy-done), channel_id=1, source_target_pairs={{0,40},{1,47},{2,46},{3,45},{4,44},{5,43},{6,42},{7,41},{8,48},{9,... | collective-permute-start | bytes 786440 | tf_op jit(solution)/shard_map/ppermute | solution.py:79
  21.6 7.0 %collective-permute-start.2 = (bf16[128,1024]{1,0:T(8,128)(2,1)}, bf16[128,1024]{1,0:T(8,128)(2,1)S(1)}, u32[]{:S(2)}, u32[]{:S(2)}) collective-permute-start(bf16[128,1024]{1,0:T(8,128)(2,1)} %copy-done), channel_id=1, source_target_pairs={{0,48},{1,55},{2,54},{3,53},{4,52},{5,51},{6,50},{7,49},{8,56},{9,... | collective-permute-start | bytes 786440 | tf_op jit(solution)/shard_map/ppermute | solution.py:79
  28.6 1.9 %collective-permute-start.1 = (bf16[128,1024]{1,0:T(8,128)(2,1)}, bf16[128,1024]{1,0:T(8,128)(2,1)S(1)}, u32[]{:S(2)}, u32[]{:S(2)}) collective-permute-start(bf16[128,1024]{1,0:T(8,128)(2,1)} %copy-done), channel_id=1, source_target_pairs={{0,8},{1,15},{2,14},{3,13},{4,12},{5,11},{6,10},{7,9},{8,16},{9,23... | collective-permute-start | bytes 786440 | tf_op jit(solution)/shard_map/ppermute | solution.py:79
  30.5 2.6 %collective-permute-start = (bf16[128,1024]{1,0:T(8,128)(2,1)}, bf16[128,1024]{1,0:T(8,128)(2,1)S(1)}, u32[]{:S(2)}, u32[]{:S(2)}) collective-permute-start(bf16[128,1024]{1,0:T(8,128)(2,1)} %copy-done), channel_id=1, source_target_pairs={{0,0},{1,7},{2,6},{3,5},{4,4},{5,3},{6,2},{7,1},{8,8},{9,15},{10,1... | collective-permute-start | bytes 786440 | tf_op jit(solution)/shard_map/ppermute | solution.py:79
  33.1 0.6 pad_add_fusion.place
  33.8 0.0 collective-permute-done.4.refs_4_
  33.8 14.8 %collective-permute-done.3.refs_3_ = bf16[128,1024]{1,0:T(8,128)(2,1)S(1)} collective-permute-done((bf16[128,1024]{1,0:T(8,128)(2,1)}, bf16[128,1024]{1,0:T(8,128)(2,1)S(1)}, u32[]{:S(2)}, u32[]{:S(2)}) %collective-permute-start.3) | collective-permute-done | bytes 262176 | tf_op jit(solution)/shard_map/ppermute | solution.py:79
  48.6 12.0 %collective-permute-done.2.refs_2_ = bf16[128,1024]{1,0:T(8,128)(2,1)S(1)} collective-permute-done((bf16[128,1024]{1,0:T(8,128)(2,1)}, bf16[128,1024]{1,0:T(8,128)(2,1)S(1)}, u32[]{:S(2)}, u32[]{:S(2)}) %collective-permute-start.2) | collective-permute-done | bytes 262176 | tf_op jit(solution)/shard_map/ppermute | solution.py:79
  60.6 0.0 collective-permute-done.1.refs_1_
  60.6 0.2 collective-permute-done.refs_0_
  60.8 5.5 %all-gather.2.cloned.1.call-done.panel = bf16[1024,1024]{1,0:T(8,128)(2,1)} async-done(((bf16[128,1024]{1,0:T(8,128)(2,1)}), bf16[1024,1024]{1,0:T(8,128)(2,1)}) %all-gather.2.cloned.1.call-update) | async-done | bytes 2097168 | tf_op jit(solution)/shard_map/all_gather | solution.py:82
  66.3 8.9 %shard_map.46 = f32[8,5,128,128]{3,2,1,0:T(8,128)} custom-call(s32[3]{0:T(128)} %pad_add_fusion.place, bf16[1024,1024]{1,0:T(8,128)(2,1)} %all-gather.2.cloned.1.call-done.panel, bf16[128,1024]{1,0:T(8,128)(2,1)} %copy-done.5, bf16[128,1024]{1,0:T(8,128)(2,1)} %copy-done.4, bf16[128,1024]{1,0:T(8,128)(2,1)} %copy-done.3, bf16[128,1024]{1,0:T(8,128)(2,1)} %copy-done.2, ...), custom_call_target="tpu_custom_call" | custom-call | flops 1342177280 | bytes 5242880 | tf_op jit(solution)/shard_map/pallas_call | solution.py:85
  75.2 0.0 reduce-scatter.2.cloned.1.call-update
  75.2 48.6 %reduce-scatter.2.cloned.1.call-done = f32[1,5,128,128]{3,2,1,0:T(8,128)} async-done(((f32[8,5,128,128]{3,2,1,0:T(8,128)}), f32[1,5,128,128]{3,2,1,0:T(8,128)}) %reduce-scatter.2.cloned.1.call-update) | async-done | bytes 327696 | tf_op jit(solution)/shard_map/reduce_scatter | solution.py:104
  123.8 0.9 slice_bitcast_fusion
  124.7 6.9 %collective-permute-start.7 = (f32[128,128]{1,0:T(8,128)S(1)}, f32[128,128]{1,0:T(8,128)S(1)}, u32[]{:S(2)}, u32[]{:S(2)}) collective-permute-start(f32[128,128]{1,0:T(8,128)S(1)} %get-tuple-element.5), channel_id=1, source_target_pairs={{0,24},{1,31},{2,30},{3,29},{4,28},{5,27},{6,26},{7,25},{8,32},{9,... | collective-permute-start | bytes 196616 | tf_op jit(solution)/shard_map/ppermute | solution.py:79
  131.6 4.8 %collective-permute-start.6 = (f32[128,128]{1,0:T(8,128)S(1)}, f32[128,128]{1,0:T(8,128)S(1)}, u32[]{:S(2)}, u32[]{:S(2)}) collective-permute-start(f32[128,128]{1,0:T(8,128)S(1)} %get-tuple-element.6), channel_id=1, source_target_pairs={{0,16},{1,23},{2,22},{3,21},{4,20},{5,19},{6,18},{7,17},{8,24},{9,... | collective-permute-start | bytes 196616 | tf_op jit(solution)/shard_map/ppermute | solution.py:79
  136.5 6.2 %collective-permute-start.5 = (f32[128,128]{1,0:T(8,128)S(1)}, f32[128,128]{1,0:T(8,128)S(1)}, u32[]{:S(2)}, u32[]{:S(2)}) collective-permute-start(f32[128,128]{1,0:T(8,128)S(1)} %get-tuple-element.7), channel_id=1, source_target_pairs={{0,56},{1,63},{2,62},{3,61},{4,60},{5,59},{6,58},{7,57},{8,0},{9,7... | collective-permute-start | bytes 196616 | tf_op jit(solution)/shard_map/ppermute | solution.py:79
  142.7 2.1 %shard_map.47.refs_4_ = f32[8,128,128]{2,1,0:T(8,128)} custom-call(s32[3]{0:T(128)} %pad_add_fusion.place, s32[8]{0:T(128)} %bitcast.16, f32[5,128,128]{2,1,0:T(8,128)} %bitcast.15, f32[8,128,128]{2,1,0:T(8,128)} %bitcast.13), custom_call_target="tpu_custom_call" | custom-call | tf_op jit(solution)/shard_map/pallas_call | solution.py:110
  144.8 0.0 collective-permute-done.7.refs_2_
  144.8 0.0 collective-permute-done.5.refs_0_
  144.8 0.6 copy-done.6
  145.4 0.0 copy-done.7
  145.4 0.6 copy-done.8
  146.1 3.4 %shard_map.48 = f32[8,128,128]{2,1,0:T(8,128)} custom-call(s32[3]{0:T(128)} %pad_add_fusion.place, s32[8]{0:T(128)} %bitcast.17, f32[128,128]{1,0:T(8,128)} %copy-done.8, f32[128,128]{1,0:T(8,128)} %copy-done.7, f32[128,128]{1,0:T(8,128)} %copy-done.6, f32[8,128,128]{2,1,0:T(8,128)} %bitcast.14, ...), custom_call_target="tpu_custom_call", output_to_operand_aliasing={{}: (6, {})} | custom-call | tf_op jit(solution)/shard_map/pallas_call | solution.py:122
  (15 shorter events, 0.0 us)
Async XLA Ops:
  6.5 59.7 %all-gather.2.cloned.1.call-start = ((), (), s32[]{:S(2)}) async-start(), calls=%async_computation.1 | async-start | bytes 2359296 | tf_op jit(solution)/shard_map/all_gather | solution.py:82
  8.4 0.7 copy-start
  9.1 114.7 %reduce-scatter.2.cloned.1.call-start = ((), (), s32[]{:S(2)}) async-start(), calls=%async_computation.2 | async-start | bytes 2949120 | tf_op jit(solution)/shard_map/reduce_scatter | solution.py:104
  9.2 24.6 %collective-permute-start.4 = (bf16[128,1024]{1,0:T(8,128)(2,1)}, bf16[128,1024]{1,0:T(8,128)(2,1)S(1)}, u32[]{:S(2)}, u32[]{:S(2)}) collective-permute-start(bf16[128,1024]{1,0:T(8,128)(2,1)} %copy-done), channel_id=1, source_target_pairs={{0,32},{1,39},{2,38},{3,37},{4,36},{5,35},{6,34},{7,33},{8,40},{9,... | collective-permute-start | bytes 786440 | tf_op jit(solution)/shard_map/ppermute | solution.py:79
  19.6 28.9 %collective-permute-start.3 = (bf16[128,1024]{1,0:T(8,128)(2,1)}, bf16[128,1024]{1,0:T(8,128)(2,1)S(1)}, u32[]{:S(2)}, u32[]{:S(2)}) collective-permute-start(bf16[128,1024]{1,0:T(8,128)(2,1)} %copy-done), channel_id=1, source_target_pairs={{0,40},{1,47},{2,46},{3,45},{4,44},{5,43},{6,42},{7,41},{8,48},{9,... | collective-permute-start | bytes 786440 | tf_op jit(solution)/shard_map/ppermute | solution.py:79
  21.6 39.0 %collective-permute-start.2 = (bf16[128,1024]{1,0:T(8,128)(2,1)}, bf16[128,1024]{1,0:T(8,128)(2,1)S(1)}, u32[]{:S(2)}, u32[]{:S(2)}) collective-permute-start(bf16[128,1024]{1,0:T(8,128)(2,1)} %copy-done), channel_id=1, source_target_pairs={{0,48},{1,55},{2,54},{3,53},{4,52},{5,51},{6,50},{7,49},{8,56},{9,... | collective-permute-start | bytes 786440 | tf_op jit(solution)/shard_map/ppermute | solution.py:79
  28.6 32.0 %collective-permute-start.1 = (bf16[128,1024]{1,0:T(8,128)(2,1)}, bf16[128,1024]{1,0:T(8,128)(2,1)S(1)}, u32[]{:S(2)}, u32[]{:S(2)}) collective-permute-start(bf16[128,1024]{1,0:T(8,128)(2,1)} %copy-done), channel_id=1, source_target_pairs={{0,8},{1,15},{2,14},{3,13},{4,12},{5,11},{6,10},{7,9},{8,16},{9,23... | collective-permute-start | bytes 786440 | tf_op jit(solution)/shard_map/ppermute | solution.py:79
  30.5 30.2 %collective-permute-start = (bf16[128,1024]{1,0:T(8,128)(2,1)}, bf16[128,1024]{1,0:T(8,128)(2,1)S(1)}, u32[]{:S(2)}, u32[]{:S(2)}) collective-permute-start(bf16[128,1024]{1,0:T(8,128)(2,1)} %copy-done), channel_id=1, source_target_pairs={{0,0},{1,7},{2,6},{3,5},{4,4},{5,3},{6,2},{7,1},{8,8},{9,15},{10,1... | collective-permute-start | bytes 786440 | tf_op jit(solution)/shard_map/ppermute | solution.py:79
  33.8 32.5 %copy-start.1 = (bf16[128,1024]{1,0:T(8,128)(2,1)}, bf16[128,1024]{1,0:T(8,128)(2,1)S(1)}, u32[]{:S(2)}) copy-start(bf16[128,1024]{1,0:T(8,128)(2,1)S(1)} %collective-permute-done.4.refs_4_) | copy-start | bytes 786436
  48.6 17.7 %copy-start.2 = (bf16[128,1024]{1,0:T(8,128)(2,1)}, bf16[128,1024]{1,0:T(8,128)(2,1)S(1)}, u32[]{:S(2)}) copy-start(bf16[128,1024]{1,0:T(8,128)(2,1)S(1)} %collective-permute-done.3.refs_3_) | copy-start | bytes 786436
  60.6 5.7 %copy-start.3 = (bf16[128,1024]{1,0:T(8,128)(2,1)}, bf16[128,1024]{1,0:T(8,128)(2,1)S(1)}, u32[]{:S(2)}) copy-start(bf16[128,1024]{1,0:T(8,128)(2,1)S(1)} %collective-permute-done.2.refs_2_) | copy-start | bytes 786436
  60.6 5.7 %copy-start.4 = (bf16[128,1024]{1,0:T(8,128)(2,1)}, bf16[128,1024]{1,0:T(8,128)(2,1)S(1)}, u32[]{:S(2)}) copy-start(bf16[128,1024]{1,0:T(8,128)(2,1)S(1)} %collective-permute-done.1.refs_1_) | copy-start | bytes 786436
  60.8 5.5 %copy-start.5 = (bf16[128,1024]{1,0:T(8,128)(2,1)}, bf16[128,1024]{1,0:T(8,128)(2,1)S(1)}, u32[]{:S(2)}) copy-start(bf16[128,1024]{1,0:T(8,128)(2,1)S(1)} %collective-permute-done.refs_0_) | copy-start | bytes 786436
  124.7 20.1 %collective-permute-start.7 = (f32[128,128]{1,0:T(8,128)S(1)}, f32[128,128]{1,0:T(8,128)S(1)}, u32[]{:S(2)}, u32[]{:S(2)}) collective-permute-start(f32[128,128]{1,0:T(8,128)S(1)} %get-tuple-element.5), channel_id=1, source_target_pairs={{0,24},{1,31},{2,30},{3,29},{4,28},{5,27},{6,26},{7,25},{8,32},{9,... | collective-permute-start | bytes 196616 | tf_op jit(solution)/shard_map/ppermute | solution.py:79
  131.6 13.2 %collective-permute-start.6 = (f32[128,128]{1,0:T(8,128)S(1)}, f32[128,128]{1,0:T(8,128)S(1)}, u32[]{:S(2)}, u32[]{:S(2)}) collective-permute-start(f32[128,128]{1,0:T(8,128)S(1)} %get-tuple-element.6), channel_id=1, source_target_pairs={{0,16},{1,23},{2,22},{3,21},{4,20},{5,19},{6,18},{7,17},{8,24},{9,... | collective-permute-start | bytes 196616 | tf_op jit(solution)/shard_map/ppermute | solution.py:79
  136.5 8.4 %collective-permute-start.5 = (f32[128,128]{1,0:T(8,128)S(1)}, f32[128,128]{1,0:T(8,128)S(1)}, u32[]{:S(2)}, u32[]{:S(2)}) collective-permute-start(f32[128,128]{1,0:T(8,128)S(1)} %get-tuple-element.7), channel_id=1, source_target_pairs={{0,56},{1,63},{2,62},{3,61},{4,60},{5,59},{6,58},{7,57},{8,0},{9,7... | collective-permute-start | bytes 196616 | tf_op jit(solution)/shard_map/ppermute | solution.py:79
  144.8 0.6 copy-start.6
  144.8 0.6 copy-start.7
  145.4 0.6 copy-start.8
Sparse Core Ops, SparseCore 0:
  9.5 56.7 all-gather.1
  75.3 48.4 reduce-scatter.1

commit v4 on v1

v4 whole, which is shorter than its diff:
```python
import functools

import jax
import jax.numpy as jnp
from jax import lax
from jax.experimental import pallas as pl
from jax.experimental.pallas import tpu as pltpu
from jax.sharding import Mesh, PartitionSpec as P

STEP = 1.0
LASSO = 0.1
RIDGE = 0.5
AXES = ("z", "y", "k")
OFFSETS = (0, 7, 2, 3, 4)
TURNED = (1, 2, 3)
CHUNKS = 4
MIB = 2**20


def join(a_ref, b_ref, out_ref):
    half = a_ref.shape[1]
    out_ref[:, :half] = a_ref[...]
    out_ref[:, half:] = b_ref[...]


def products(n, tile, depth, rows_ref, *refs):
    count = len(OFFSETS)
    columns, (out_ref, rows, picked, made, row_sems, column_sems, out_sems) = refs[:count], refs[count:]
    k = lax.axis_index("k")
    per = n // CHUNKS
    loads = []
    for i, ref in enumerate(columns):
        at = pl.ds(i * tile, tile)
        for h in range(2):
            here, there = pl.ds(h * depth, depth), pl.ds((1 - h) * depth, depth)
            loads.append(pltpu.make_async_copy(ref.at[:, there], picked.at[at, here], column_sems.at[i, h]))
    chunks = [
        pltpu.make_async_copy(rows_ref.at[pl.ds(c * per * tile, per * tile)], rows.at[c], row_sems.at[c])
        for c in range(CHUNKS)
    ]
    for copy in loads + chunks:
        copy.start()
    for copy in loads:
        copy.wait()
    stores = []
    for c in range(CHUNKS):
        chunks[c].wait()
        part = lax.dot_general(
            rows[c], picked[...], (((1,), (1,)), ((), ())), preferred_element_type=jnp.float32
        )
        for e in range(per):
            j = c * per + e
            for i in range(count):
                made[j, i] = part[e * tile:(e + 1) * tile, i * tile:(i + 1) * tile]
            m = lax.rem(j + k, n)
            stores.append(pltpu.make_async_copy(made.at[j], out_ref.at[m], out_sems.at[j]))
            stores[-1].start()
    for copy in stores:
        copy.wait()


def finish(n, tile, scale, active_ref, own, mirrored, *refs):
    arrived, (precision_ref, out_ref) = refs[:-2], refs[-2:]
    z, y, k = (lax.axis_index(a) for a in AXES)
    row = lax.broadcasted_iota(jnp.int32, (tile, tile), 0)
    column = lax.broadcasted_iota(jnp.int32, (tile, tile), 1)

    def put(d, total):
        t = lax.rem(y + d, n)
        w = precision_ref[t]
        gradient = total * scale + RIDGE * w
        if d == 0:
            on_diag = (row == column) & (lax.rem(2 * k - z + n, n) == 0)
            inverse = jnp.where(on_diag, 1.0 / jnp.where(on_diag, w, 1.0), 0.0)
            stepped = w - STEP * (gradient - inverse)
        else:
            stepped = w - STEP * gradient
        shrunk = jnp.where(
            stepped > 0, jnp.maximum(stepped - STEP * LASSO, 0.0), jnp.minimum(stepped + STEP * LASSO, 0.0)
        )
        if d == 0:
            shrunk = jnp.where(on_diag, stepped, shrunk)
        out_ref[t] = shrunk * active_ref[t].astype(jnp.float32)

    put(0, own[0].T)
    for i in range(1, len(OFFSETS)):
        put(OFFSETS[i], mirrored[i])
    for i, ref in zip(TURNED, arrived):
        put(n - OFFSETS[i], ref[...].T)


def local(n, resid, samples, precision, active):
    tile, depth = resid.shape
    vmem, smem, anywhere = (pl.BlockSpec(memory_space=s) for s in (pltpu.VMEM, pltpu.SMEM, pl.ANY))
    count = len(OFFSETS)

    def moved(a, to):
        def index(z, y, k):
            return (z % n * n + y % n) * n + k % n

        ids = [(z, y, k) for z in range(n) for y in range(n) for k in range(n)]
        return lax.ppermute(a, AXES, [(index(*i), index(*to(*i))) for i in ids])

    own = pl.pallas_call(
        join,
        out_shape=jax.ShapeDtypeStruct((tile, 2 * depth), resid.dtype),
        in_specs=[vmem, vmem],
        out_specs=vmem,
        compiler_params=pltpu.CompilerParams(vmem_limit_bytes=60 * MIB),
    )(resid, samples)
    rows = lax.all_gather(own, "k", axis=0, tiled=True)
    columns = [own] + [moved(own, lambda z, y, k, d=d: (z, y - d, k)) for d in OFFSETS[1:]]
    partial = pl.pallas_call(
        functools.partial(products, n, tile, depth),
        out_shape=jax.ShapeDtypeStruct((n, count, tile, tile), jnp.float32),
        in_specs=[anywhere] * (1 + count),
        out_specs=anywhere,
        scratch_shapes=[
            pltpu.VMEM((CHUNKS, n // CHUNKS * tile, 2 * depth), jnp.bfloat16),
            pltpu.VMEM((count * tile, 2 * depth), jnp.bfloat16),
            pltpu.VMEM((n, count, tile, tile), jnp.float32),
            pltpu.SemaphoreType.DMA((CHUNKS,)),
            pltpu.SemaphoreType.DMA((count, 2)),
            pltpu.SemaphoreType.DMA((n,)),
        ],
        compiler_params=pltpu.CompilerParams(vmem_limit_bytes=60 * MIB),
        cost_estimate=pl.CostEstimate(
            flops=4 * n * count * tile * tile * depth, bytes_accessed=6 * MIB, transcendentals=0
        ),
    )(rows, *columns)
    summed = lax.psum_scatter(partial, "z", scatter_dimension=0, tiled=True)[0]
    mirrored = moved(summed, lambda z, y, k: (z, y, z - k))
    arrived = [moved(summed[i], lambda z, y, k, d=OFFSETS[i]: (z, y + d, k)) for i in TURNED]
    updated = pl.pallas_call(
        functools.partial(finish, n, tile, 0.5 / (depth * n)),
        out_shape=jax.ShapeDtypeStruct((n, tile, tile), jnp.float32),
        in_specs=[smem] + [vmem] * (3 + len(TURNED)),
        out_specs=vmem,
        compiler_params=pltpu.CompilerParams(vmem_limit_bytes=16 * MIB),
    )(active.reshape(n), summed, mirrored, *arrived, precision.reshape(n, tile, tile))
    return updated.reshape(precision.shape)


def solution(mesh):
    n = mesh.shape["blk"]
    grid = Mesh(mesh.devices.reshape(n, n, n), AXES)
    rows = ("y", "k")
    in_specs = (P(rows, "z"), P(rows, "z"), P(rows, "z"), P(rows, "z"))
    return jax.shard_map(
        functools.partial(local, n), mesh=grid, in_specs=in_specs, out_specs=P(rows, "z"), check_vma=False
    )
```

time: 145 us -> 144 us (level)
  the two profiles are of different devices: /device:TPU:2 before, /device:TPU:58 now
where the time goes in v4:
time: 144 us
  waiting for transfers between devices  86.4 us (60%)
  starting transfers between devices  32.3 us (22%)
  between operations  13.5 us (9%)
  Pallas kernels  9.11 us (6%)
  local copies, waits for them, and re-layouts  2.75 us (2%)
    reduce_scatter x1, waiting for transfers between devices, local(): summed = lax.psum_scatter(partial, 'z', scatter_dimension=0, tiled=True)[0]  55.3 us
    ppermute x8, starting transfers between devices, moved(): return lax.ppermute(a, AXES, [(index(*i), index(*to(*i))) for i in ids])  32.3 us
    ppermute x8, waiting for transfers between devices, moved(): return lax.ppermute(a, AXES, [(index(*i), index(*to(*i))) for i in ids])  31 us
    pallas_call x1, Pallas kernels, local(): pl.pallas_call(functools.partial(products, n, tile, depth), out_shape=jax...  5.81 us
  transfers between devices with their start and end apart: 10, of which 5 were waited for; matrix products, arithmetic and copies ran while one was open for 1% of the time, Pallas kernels for 0%

profile of v4, /device:TPU:58, one launch (start us, length us, event | category | flops | bytes accessed | tf_op | source)
XLA Modules:
  0.0 144.1 jit_solution(7524085358477503200)
XLA Ops:
  6.5 1.7 %shard_map.46.refs_0_ = bf16[128,1024]{1,0:T(8,128)(2,1)} custom-call(bf16[128,512]{1,0:T(8,128)(2,1)} %a_ref.1, bf16[128,512]{1,0:T(8,128)(2,1)} %b_ref.1), custom_call_target="tpu_custom_call" | custom-call | tf_op jit(solution)/shard_map/pallas_call | solution.py:104
  8.2 0.0 all-gather.2.cloned.1.call-update
  8.2 0.0 reduce-scatter.2.cloned.1.call-start
  8.3 4.7 %collective-permute-start.3 = (bf16[128,1024]{1,0:T(8,128)(2,1)}, bf16[128,1024]{1,0:T(8,128)(2,1)S(1)}, u32[]{:S(2)}, u32[]{:S(2)}) collective-permute-start(bf16[128,1024]{1,0:T(8,128)(2,1)} %shard_map.46.refs_0_), channel_id=1, source_target_pairs={{0,32},{1,33},{2,34},{3,35},{4,36},{5,37},{6,38},{7,39},{8,40},{9,... | collective-permute-start | bytes 786440 | tf_op jit(solution)/shard_map/ppermute | solution.py:102
  13.0 2.1 %collective-permute-start.2 = (bf16[128,1024]{1,0:T(8,128)(2,1)}, bf16[128,1024]{1,0:T(8,128)(2,1)S(1)}, u32[]{:S(2)}, u32[]{:S(2)}) collective-permute-start(bf16[128,1024]{1,0:T(8,128)(2,1)} %shard_map.46.refs_0_), channel_id=1, source_target_pairs={{0,40},{1,41},{2,42},{3,43},{4,44},{5,45},{6,46},{7,47},{8,48},{9,... | collective-permute-start | bytes 786440 | tf_op jit(solution)/shard_map/ppermute | solution.py:102
  15.2 6.2 %collective-permute-start.1 = (bf16[128,1024]{1,0:T(8,128)(2,1)}, bf16[128,1024]{1,0:T(8,128)(2,1)S(1)}, u32[]{:S(2)}, u32[]{:S(2)}) collective-permute-start(bf16[128,1024]{1,0:T(8,128)(2,1)} %shard_map.46.refs_0_), channel_id=1, source_target_pairs={{0,48},{1,49},{2,50},{3,51},{4,52},{5,53},{6,54},{7,55},{8,56},{9,... | collective-permute-start | bytes 786440 | tf_op jit(solution)/shard_map/ppermute | solution.py:102
  21.3 3.8 %collective-permute-start = (bf16[128,1024]{1,0:T(8,128)(2,1)}, bf16[128,1024]{1,0:T(8,128)(2,1)S(1)}, u32[]{:S(2)}, u32[]{:S(2)}) collective-permute-start(bf16[128,1024]{1,0:T(8,128)(2,1)} %shard_map.46.refs_0_), channel_id=1, source_target_pairs={{0,8},{1,9},{2,10},{3,11},{4,12},{5,13},{6,14},{7,15},{8,16},{9,17... | collective-permute-start | bytes 786440 | tf_op jit(solution)/shard_map/ppermute | solution.py:102
  25.1 5.8 %collective-permute-done.3.refs_4_ = bf16[128,1024]{1,0:T(8,128)(2,1)S(1)} collective-permute-done((bf16[128,1024]{1,0:T(8,128)(2,1)}, bf16[128,1024]{1,0:T(8,128)(2,1)S(1)}, u32[]{:S(2)}, u32[]{:S(2)}) %collective-permute-start.3) | collective-permute-done | bytes 262176 | tf_op jit(solution)/shard_map/ppermute | solution.py:102
  31.0 19.7 %collective-permute-done.2.refs_3_ = bf16[128,1024]{1,0:T(8,128)(2,1)S(1)} collective-permute-done((bf16[128,1024]{1,0:T(8,128)(2,1)}, bf16[128,1024]{1,0:T(8,128)(2,1)S(1)}, u32[]{:S(2)}, u32[]{:S(2)}) %collective-permute-start.2) | collective-permute-done | bytes 262176 | tf_op jit(solution)/shard_map/ppermute | solution.py:102
  50.7 0.0 collective-permute-done.1.refs_2_
  50.7 0.0 collective-permute-done.refs_1_
  50.7 0.0 all-gather.2.cloned.1.call-done.rows_ref
  50.7 0.7 copy-done.4
  51.4 0.1 copy-done.5
  51.5 0.1 copy-done.6
  51.6 5.8 %shard_map.47 = f32[8,5,128,128]{3,2,1,0:T(8,128)} custom-call(bf16[1024,1024]{1,0:T(8,128)(2,1)} %all-gather.2.cloned.1.call-done.rows_ref, bf16[128,1024]{1,0:T(8,128)(2,1)} %shard_map.46.refs_0_, bf16[128,1024]{1,0:T(8,128)(2,1)} %copy-done.6, bf16[128,1024]{1,0:T(8,128)(2,1)} %copy-done.5, bf16[128,1024]{1,0:T(8,128)(2,1)} %copy-done.4, ...), custom_call_target="tpu_custom_call" | custom-call | flops 1342177280 | bytes 6291456 | tf_op jit(solution)/shard_map/pallas_call | solution.py:113
  57.4 0.0 copy-start.1
  57.4 0.0 copy-start.2
  57.4 0.0 reduce-scatter.2.cloned.1.call-update
  57.4 55.3 %reduce-scatter.2.cloned.1.call-done = f32[1,5,128,128]{3,2,1,0:T(8,128)} async-done(((f32[8,5,128,128]{3,2,1,0:T(8,128)}), f32[1,5,128,128]{3,2,1,0:T(8,128)}) %reduce-scatter.2.cloned.1.call-update) | async-done | bytes 327696 | tf_op jit(solution)/shard_map/reduce_scatter | solution.py:131
  112.8 3.9 %collective-permute-start.4 = (f32[5,128,128]{2,1,0:T(8,128)}, f32[5,128,128]{2,1,0:T(8,128)S(1)}, u32[]{:S(2)}, u32[]{:S(2)}) collective-permute-start(f32[5,128,128]{2,1,0:T(8,128)} %bitcast.10), channel_id=1, source_target_pairs={{0,0},{1,7},{2,6},{3,5},{4,4},{5,3},{6,2},{7,1},{8,8},{9,15},{10,1... | collective-permute-start | bytes 983048 | tf_op jit(solution)/shard_map/ppermute | solution.py:102
  116.7 0.9 slice_bitcast_fusion
  117.6 4.2 %collective-permute-start.7 = (f32[128,128]{1,0:T(8,128)S(1)}, f32[128,128]{1,0:T(8,128)S(1)}, u32[]{:S(2)}, u32[]{:S(2)}) collective-permute-start(f32[128,128]{1,0:T(8,128)S(1)} %get-tuple-element.5), channel_id=1, source_target_pairs={{0,24},{1,25},{2,26},{3,27},{4,28},{5,29},{6,30},{7,31},{8,32},{9,... | collective-permute-start | bytes 196616 | tf_op jit(solution)/shard_map/ppermute | solution.py:102
  121.8 5.5 %collective-permute-start.6 = (f32[128,128]{1,0:T(8,128)S(1)}, f32[128,128]{1,0:T(8,128)S(1)}, u32[]{:S(2)}, u32[]{:S(2)}) collective-permute-start(f32[128,128]{1,0:T(8,128)S(1)} %get-tuple-element.6), channel_id=1, source_target_pairs={{0,16},{1,17},{2,18},{3,19},{4,20},{5,21},{6,22},{7,23},{8,24},{9,... | collective-permute-start | bytes 196616 | tf_op jit(solution)/shard_map/ppermute | solution.py:102
  127.2 1.9 %collective-permute-start.5 = (f32[128,128]{1,0:T(8,128)S(1)}, f32[128,128]{1,0:T(8,128)S(1)}, u32[]{:S(2)}, u32[]{:S(2)}) collective-permute-start(f32[128,128]{1,0:T(8,128)S(1)} %get-tuple-element.7), channel_id=1, source_target_pairs={{0,56},{1,57},{2,58},{3,59},{4,60},{5,61},{6,62},{7,63},{8,0},{9,1... | collective-permute-start | bytes 196616 | tf_op jit(solution)/shard_map/ppermute | solution.py:102
  129.2 0.0 collective-permute-done.7.refs_2_
  129.2 0.3 collective-permute-done.6.refs_1_
  129.5 5.1 %collective-permute-done.5.refs_0_ = f32[128,128]{1,0:T(8,128)S(1)} collective-permute-done((f32[128,128]{1,0:T(8,128)S(1)}, f32[128,128]{1,0:T(8,128)S(1)}, u32[]{:S(2)}, u32[]{:S(2)}) %collective-permute-start.5) | collective-permute-done | bytes 65568 | tf_op jit(solution)/shard_map/ppermute | solution.py:102
  134.6 0.0 collective-permute-done.4.mirrored
  134.6 0.0 copy-done.1
  134.6 1.0 copy-done
  135.6 1.6 %shard_map.48 = f32[8,128,128]{2,1,0:T(8,128)} custom-call(s32[8]{0:T(128)S(1)} %bitcast.13, f32[5,128,128]{2,1,0:T(8,128)S(1)} %bitcast.11, f32[5,128,128]{2,1,0:T(8,128)S(1)} %collective-permute-done.4.mirrored, f32[128,128]{1,0:T(8,128)S(1)} %collective-permute-done.5.refs_0_, f32[128,128]{1,0:T(8,128)S(1)} %collective-permute-done.6.refs_1_, ...), custom_call_target="tpu_custom_call" | custom-call | tf_op jit(solution)/shard_map/pallas_call | solution.py:134
  (8 shorter events, 0.0 us)
Async XLA Ops:
  6.5 44.2 %all-gather.2.cloned.1.call-start = ((), (), s32[]{:S(2)}) async-start(), calls=%async_computation.1 | async-start | bytes 2359296 | tf_op jit(solution)/shard_map/all_gather | solution.py:111
  8.2 104.5 %reduce-scatter.2.cloned.1.call-start = ((), (), s32[]{:S(2)}) async-start(), calls=%async_computation.2 | async-start | bytes 2949120 | tf_op jit(solution)/shard_map/reduce_scatter | solution.py:131
  8.3 22.7 %collective-permute-start.3 = (bf16[128,1024]{1,0:T(8,128)(2,1)}, bf16[128,1024]{1,0:T(8,128)(2,1)S(1)}, u32[]{:S(2)}, u32[]{:S(2)}) collective-permute-start(bf16[128,1024]{1,0:T(8,128)(2,1)} %shard_map.46.refs_0_), channel_id=1, source_target_pairs={{0,32},{1,33},{2,34},{3,35},{4,36},{5,37},{6,38},{7,39},{8,40},{9,... | collective-permute-start | bytes 786440 | tf_op jit(solution)/shard_map/ppermute | solution.py:102
  13.0 37.6 %collective-permute-start.2 = (bf16[128,1024]{1,0:T(8,128)(2,1)}, bf16[128,1024]{1,0:T(8,128)(2,1)S(1)}, u32[]{:S(2)}, u32[]{:S(2)}) collective-permute-start(bf16[128,1024]{1,0:T(8,128)(2,1)} %shard_map.46.refs_0_), channel_id=1, source_target_pairs={{0,40},{1,41},{2,42},{3,43},{4,44},{5,45},{6,46},{7,47},{8,48},{9,... | collective-permute-start | bytes 786440 | tf_op jit(solution)/shard_map/ppermute | solution.py:102
  15.2 35.5 %collective-permute-start.1 = (bf16[128,1024]{1,0:T(8,128)(2,1)}, bf16[128,1024]{1,0:T(8,128)(2,1)S(1)}, u32[]{:S(2)}, u32[]{:S(2)}) collective-permute-start(bf16[128,1024]{1,0:T(8,128)(2,1)} %shard_map.46.refs_0_), channel_id=1, source_target_pairs={{0,48},{1,49},{2,50},{3,51},{4,52},{5,53},{6,54},{7,55},{8,56},{9,... | collective-permute-start | bytes 786440 | tf_op jit(solution)/shard_map/ppermute | solution.py:102
  21.3 29.3 %collective-permute-start = (bf16[128,1024]{1,0:T(8,128)(2,1)}, bf16[128,1024]{1,0:T(8,128)(2,1)S(1)}, u32[]{:S(2)}, u32[]{:S(2)}) collective-permute-start(bf16[128,1024]{1,0:T(8,128)(2,1)} %shard_map.46.refs_0_), channel_id=1, source_target_pairs={{0,8},{1,9},{2,10},{3,11},{4,12},{5,13},{6,14},{7,15},{8,16},{9,17... | collective-permute-start | bytes 786440 | tf_op jit(solution)/shard_map/ppermute | solution.py:102
  31.0 19.8 %copy-start.3 = (bf16[128,1024]{1,0:T(8,128)(2,1)}, bf16[128,1024]{1,0:T(8,128)(2,1)S(1)}, u32[]{:S(2)}) copy-start(bf16[128,1024]{1,0:T(8,128)(2,1)S(1)} %collective-permute-done.3.refs_4_) | copy-start | bytes 786436
  50.7 0.7 copy-start.4
  50.7 0.8 copy-start.5
  50.7 0.9 copy-start.6
  57.4 77.2 %copy-start.1 = (f32[1,1,8,128,128]{4,3,2,1,0:T(8,128)S(1)}, f32[1,1,8,128,128]{4,3,2,1,0:T(8,128)}, u32[]{:S(2)}) copy-start(f32[1,1,8,128,128]{4,3,2,1,0:T(8,128)} %param.6) | copy-start | bytes 1572868
  57.4 77.2 %copy-start.2 = (s32[1,1,8]{2,1,0:T(1,128)S(1)}, s32[1,1,8]{2,1,0:T(1,128)}, u32[]{:S(2)}) copy-start(s32[1,1,8]{2,1,0:T(1,128)} %param.7) | copy-start | bytes 100
  112.8 21.9 %collective-permute-start.4 = (f32[5,128,128]{2,1,0:T(8,128)}, f32[5,128,128]{2,1,0:T(8,128)S(1)}, u32[]{:S(2)}, u32[]{:S(2)}) collective-permute-start(f32[5,128,128]{2,1,0:T(8,128)} %bitcast.10), channel_id=1, source_target_pairs={{0,0},{1,7},{2,6},{3,5},{4,4},{5,3},{6,2},{7,1},{8,8},{9,15},{10,1... | collective-permute-start | bytes 983048 | tf_op jit(solution)/shard_map/ppermute | solution.py:102
  117.6 11.6 %collective-permute-start.7 = (f32[128,128]{1,0:T(8,128)S(1)}, f32[128,128]{1,0:T(8,128)S(1)}, u32[]{:S(2)}, u32[]{:S(2)}) collective-permute-start(f32[128,128]{1,0:T(8,128)S(1)} %get-tuple-element.5), channel_id=1, source_target_pairs={{0,24},{1,25},{2,26},{3,27},{4,28},{5,29},{6,30},{7,31},{8,32},{9,... | collective-permute-start | bytes 196616 | tf_op jit(solution)/shard_map/ppermute | solution.py:102
  121.8 7.8 %collective-permute-start.6 = (f32[128,128]{1,0:T(8,128)S(1)}, f32[128,128]{1,0:T(8,128)S(1)}, u32[]{:S(2)}, u32[]{:S(2)}) collective-permute-start(f32[128,128]{1,0:T(8,128)S(1)} %get-tuple-element.6), channel_id=1, source_target_pairs={{0,16},{1,17},{2,18},{3,19},{4,20},{5,21},{6,22},{7,23},{8,24},{9,... | collective-permute-start | bytes 196616 | tf_op jit(solution)/shard_map/ppermute | solution.py:102
  127.2 7.4 %collective-permute-start.5 = (f32[128,128]{1,0:T(8,128)S(1)}, f32[128,128]{1,0:T(8,128)S(1)}, u32[]{:S(2)}, u32[]{:S(2)}) collective-permute-start(f32[128,128]{1,0:T(8,128)S(1)} %get-tuple-element.7), channel_id=1, source_target_pairs={{0,56},{1,57},{2,58},{3,59},{4,60},{5,61},{6,62},{7,63},{8,0},{9,1... | collective-permute-start | bytes 196616 | tf_op jit(solution)/shard_map/ppermute | solution.py:102
  134.6 1.0 copy-start
Sparse Core Ops, SparseCore 0:
  9.5 33.2 all-gather.1
  57.6 55.1 reduce-scatter.1

commit v5 on v4

--- a/solution.py
+++ b/solution.py
@@ -11,8 +11,8 @@
 LASSO = 0.1
 RIDGE = 0.5
 AXES = ("z", "y", "k")
-OFFSETS = (0, 7, 2, 3, 4)
-TURNED = (1, 2, 3)
+EARLY = (0, 7, 4)
+LATE = (2, 3)
 CHUNKS = 4
 MIB = 2**20
 
@@ -23,8 +23,7 @@
     out_ref[:, half:] = b_ref[...]
 
 
-def products(n, tile, depth, rows_ref, *refs):
-    count = len(OFFSETS)
+def products(n, tile, depth, count, rows_ref, *refs):
     columns, (out_ref, rows, picked, made, row_sems, column_sems, out_sems) = refs[:count], refs[count:]
     k = lax.axis_index("k")
     per = n // CHUNKS
@@ -59,7 +58,14 @@
         copy.wait()
 
 
-def finish(n, tile, scale, active_ref, own, mirrored, *refs):
+def added(parts_ref, out_ref, *each):
+    for i, ref in enumerate(each):
+        total = jnp.sum(parts_ref[:, i], axis=0)
+        out_ref[i] = total
+        ref[...] = total
+
+
+def finish(n, tile, scale, active_ref, own, early, late, *refs):
     arrived, (precision_ref, out_ref) = refs[:-2], refs[-2:]
     z, y, k = (lax.axis_index(a) for a in AXES)
     row = lax.broadcasted_iota(jnp.int32, (tile, tile), 0)
@@ -83,16 +89,17 @@
         out_ref[t] = shrunk * active_ref[t].astype(jnp.float32)
 
     put(0, own[0].T)
-    for i in range(1, len(OFFSETS)):
-        put(OFFSETS[i], mirrored[i])
-    for i, ref in zip(TURNED, arrived):
-        put(n - OFFSETS[i], ref[...].T)
+    for i in range(1, len(EARLY)):
+        put(EARLY[i], early[i])
+    for i in range(len(LATE)):
+        put(LATE[i], late[i])
+    for d, ref in zip((EARLY[1],) + LATE, arrived):
+        put(n - d, ref[...].T)
 
 
 def local(n, resid, samples, precision, active):
     tile, depth = resid.shape
     vmem, smem, anywhere = (pl.BlockSpec(memory_space=s) for s in (pltpu.VMEM, pltpu.SMEM, pl.ANY))
-    count = len(OFFSETS)
 
     def moved(a, to):
         def index(z, y, k):
@@ -100,6 +107,25 @@
 
         ids = [(z, y, k) for z in range(n) for y in range(n) for k in range(n)]
         return lax.ppermute(a, AXES, [(index(*i), index(*to(*i))) for i in ids])
+
+    def multiplied(rows, columns, flops):
+        count = len(columns)
+        return pl.pallas_call(
+            functools.partial(products, n, tile, depth, count),
+            out_shape=jax.ShapeDtypeStruct((n, count, tile, tile), jnp.float32),
+            in_specs=[anywhere] * (1 + count),
+            out_specs=anywhere,
+            scratch_shapes=[
+                pltpu.VMEM((CHUNKS, n // CHUNKS * tile, 2 * depth), jnp.bfloat16),
+                pltpu.VMEM((count * tile, 2 * depth), jnp.bfloat16),
+                pltpu.VMEM((n, count, tile, tile), jnp.float32),
+                pltpu.SemaphoreType.DMA((CHUNKS,)),
+                pltpu.SemaphoreType.DMA((count, 2)),
+                pltpu.SemaphoreType.DMA((n,)),
+            ],
+            compiler_params=pltpu.CompilerParams(vmem_limit_bytes=60 * MIB),
+            cost_estimate=pl.CostEstimate(flops=flops, bytes_accessed=4 * MIB, transcendentals=0),
+        )(rows, *columns)
 
     own = pl.pallas_call(
         join,
@@ -109,35 +135,33 @@
         compiler_params=pltpu.CompilerParams(vmem_limit_bytes=60 * MIB),
     )(resid, samples)
     rows = lax.all_gather(own, "k", axis=0, tiled=True)
-    columns = [own] + [moved(own, lambda z, y, k, d=d: (z, y - d, k)) for d in OFFSETS[1:]]
-    partial = pl.pallas_call(
-        functools.partial(products, n, tile, depth),
-        out_shape=jax.ShapeDtypeStruct((n, count, tile, tile), jnp.float32),
-        in_specs=[anywhere] * (1 + count),
-        out_specs=anywhere,
-        scratch_shapes=[
-            pltpu.VMEM((CHUNKS, n // CHUNKS * tile, 2 * depth), jnp.bfloat16),
-            pltpu.VMEM((count * tile, 2 * depth), jnp.bfloat16),
-            pltpu.VMEM((n, count, tile, tile), jnp.float32),
-            pltpu.SemaphoreType.DMA((CHUNKS,)),
-            pltpu.SemaphoreType.DMA((count, 2)),
-            pltpu.SemaphoreType.DMA((n,)),
-        ],
-        compiler_params=pltpu.CompilerParams(vmem_limit_bytes=60 * MIB),
-        cost_estimate=pl.CostEstimate(
-            flops=4 * n * count * tile * tile * depth, bytes_accessed=6 * MIB, transcendentals=0
-        ),
-    )(rows, *columns)
-    summed = lax.psum_scatter(partial, "z", scatter_dimension=0, tiled=True)[0]
-    mirrored = moved(summed, lambda z, y, k: (z, y, z - k))
-    arrived = [moved(summed[i], lambda z, y, k, d=OFFSETS[i]: (z, y + d, k)) for i in TURNED]
+    panel = {d: moved(own, lambda z, y, k, d=d: (z, y - d, k)) for d in EARLY[1:] + LATE}
+    panel[0] = own
+    once = 4 * n * tile * tile * depth
+    early = lax.psum_scatter(
+        multiplied(rows, [panel[d] for d in EARLY], once), "z", scatter_dimension=0, tiled=True
+    )[0]
+    weight = 600 * once
+    parts = lax.all_to_all(multiplied(rows, [panel[d] for d in LATE], weight), "z", 0, 0, tiled=True)
+    square = jax.ShapeDtypeStruct((tile, tile), jnp.float32)
+    late, *each = pl.pallas_call(
+        added,
+        out_shape=[jax.ShapeDtypeStruct((len(LATE), tile, tile), jnp.float32)] + [square] * len(LATE),
+        in_specs=[vmem],
+        out_specs=[vmem] * (1 + len(LATE)),
+        compiler_params=pltpu.CompilerParams(vmem_limit_bytes=16 * MIB),
+    )(parts)
+    late = moved(late, lambda z, y, k: (z, y, z - k))
+    arrived = [moved(a, lambda z, y, k, d=d: (z, y + d, k)) for a, d in zip(each, LATE)]
+    arrived = [moved(early[1], lambda z, y, k: (z, y + EARLY[1], k))] + arrived
+    mirrored = moved(early, lambda z, y, k: (z, y, z - k))
     updated = pl.pallas_call(
         functools.partial(finish, n, tile, 0.5 / (depth * n)),
         out_shape=jax.ShapeDtypeStruct((n, tile, tile), jnp.float32),
-        in_specs=[smem] + [vmem] * (3 + len(TURNED)),
+        in_specs=[smem] + [vmem] * (4 + len(arrived)),
         out_specs=vmem,
         compiler_params=pltpu.CompilerParams(vmem_limit_bytes=16 * MIB),
-    )(active.reshape(n), summed, mirrored, *arrived, precision.reshape(n, tile, tile))
+    )(active.reshape(n), early, mirrored, late, *arrived, precision.reshape(n, tile, tile))
     return updated.reshape(precision.shape)
 
 

time: 144 us -> 144 us (level)
  the two profiles are of different devices: /device:TPU:58 before, /device:TPU:2 now
where the time goes in v5:
time: 144 us; the launch traced here: 143 us
  blocking collectives  46.7 us (32%)
  starting transfers between devices  36.7 us (25%)
  waiting for transfers between devices  31.9 us (22%)
  between operations  13.6 us (9%)
  Pallas kernels  11.9 us (8%)
  local copies, waits for them, and re-layouts  2.5 us (2%)
    all_to_all x1, blocking collectives, local(): lax.all_to_all(multiplied(rows, [panel[d] for d in LATE], weight), 'z', 0...  46.7 us
    ppermute x9, starting transfers between devices, moved(): return lax.ppermute(a, AXES, [(index(*i), index(*to(*i))) for i in ids])  36.7 us
    ppermute x9, waiting for transfers between devices, moved(): return lax.ppermute(a, AXES, [(index(*i), index(*to(*i))) for i in ids])  21 us
    all_gather x1, waiting for transfers between devices, local(): rows = lax.all_gather(own, 'k', axis=0, tiled=True)  10.8 us
    pallas_call x2, Pallas kernels, multiplied(): pl.pallas_call(functools.partial(products, n, tile, depth, count), out_sh...  8.53 us
  transfers between devices with their start and end apart: 11, of which 4 were waited for; matrix products, arithmetic and copies ran while one was open for 1% of the time, Pallas kernels for 6%

profile of v5, /device:TPU:2, one launch (start us, length us, event | category | flops | bytes accessed | tf_op | source)
XLA Modules:
  0.0 143.2 jit_solution(11055826958338779325)
XLA Ops:
  6.5 1.7 %shard_map.46.refs_0_ = bf16[128,1024]{1,0:T(8,128)(2,1)} custom-call(bf16[128,512]{1,0:T(8,128)(2,1)} %a_ref.1, bf16[128,512]{1,0:T(8,128)(2,1)} %b_ref.1), custom_call_target="tpu_custom_call" | custom-call | tf_op jit(solution)/shard_map/pallas_call | solution.py:130
  8.2 0.0 all-gather.2.cloned.1.call-update
  8.2 0.0 reduce-scatter.2.cloned.1.call-start
  8.3 3.5 %collective-permute-start = (bf16[128,1024]{1,0:T(8,128)(2,1)}, bf16[128,1024]{1,0:T(8,128)(2,1)S(1)}, u32[]{:S(2)}, u32[]{:S(2)}) collective-permute-start(bf16[128,1024]{1,0:T(8,128)(2,1)} %shard_map.46.refs_0_), channel_id=1, source_target_pairs={{0,8},{1,9},{2,10},{3,11},{4,12},{5,13},{6,14},{7,15},{8,16},{9,17... | collective-permute-start | bytes 786440 | tf_op jit(solution)/shard_map/ppermute | solution.py:109
  11.8 6.8 %collective-permute-start.1 = (bf16[128,1024]{1,0:T(8,128)(2,1)}, bf16[128,1024]{1,0:T(8,128)(2,1)S(1)}, u32[]{:S(2)}, u32[]{:S(2)}) collective-permute-start(bf16[128,1024]{1,0:T(8,128)(2,1)} %shard_map.46.refs_0_), channel_id=1, source_target_pairs={{0,32},{1,33},{2,34},{3,35},{4,36},{5,37},{6,38},{7,39},{8,40},{9,... | collective-permute-start | bytes 786440 | tf_op jit(solution)/shard_map/ppermute | solution.py:109
  18.6 3.1 %collective-permute-start.3 = (bf16[128,1024]{1,0:T(8,128)(2,1)}, bf16[128,1024]{1,0:T(8,128)(2,1)S(1)}, u32[]{:S(2)}, u32[]{:S(2)}) collective-permute-start(bf16[128,1024]{1,0:T(8,128)(2,1)} %shard_map.46.refs_0_), channel_id=1, source_target_pairs={{0,48},{1,49},{2,50},{3,51},{4,52},{5,53},{6,54},{7,55},{8,56},{9,... | collective-permute-start | bytes 786440 | tf_op jit(solution)/shard_map/ppermute | solution.py:109
  21.8 3.6 %collective-permute-start.4 = (bf16[128,1024]{1,0:T(8,128)(2,1)}, bf16[128,1024]{1,0:T(8,128)(2,1)S(1)}, u32[]{:S(2)}, u32[]{:S(2)}) collective-permute-start(bf16[128,1024]{1,0:T(8,128)(2,1)} %shard_map.46.refs_0_), channel_id=1, source_target_pairs={{0,40},{1,41},{2,42},{3,43},{4,44},{5,45},{6,46},{7,47},{8,48},{9,... | collective-permute-start | bytes 786440 | tf_op jit(solution)/shard_map/ppermute | solution.py:109
  25.4 0.0 collective-permute-done.refs_1_
  25.4 7.2 %collective-permute-done.1.refs_2_ = bf16[128,1024]{1,0:T(8,128)(2,1)S(1)} collective-permute-done((bf16[128,1024]{1,0:T(8,128)(2,1)}, bf16[128,1024]{1,0:T(8,128)(2,1)S(1)}, u32[]{:S(2)}, u32[]{:S(2)}) %collective-permute-start.1) | collective-permute-done | bytes 262176 | tf_op jit(solution)/shard_map/ppermute | solution.py:109
  32.6 10.8 %all-gather.2.cloned.1.call-done.rows_ref = bf16[1024,1024]{1,0:T(8,128)(2,1)} async-done(((bf16[128,1024]{1,0:T(8,128)(2,1)}), bf16[1024,1024]{1,0:T(8,128)(2,1)}) %all-gather.2.cloned.1.call-update) | async-done | bytes 2097168 | tf_op jit(solution)/shard_map/all_gather | solution.py:137
  43.4 4.4 %shard_map.47 = f32[8,3,128,128]{3,2,1,0:T(8,128)} custom-call(bf16[1024,1024]{1,0:T(8,128)(2,1)} %all-gather.2.cloned.1.call-done.rows_ref, bf16[128,1024]{1,0:T(8,128)(2,1)} %shard_map.46.refs_0_, bf16[128,1024]{1,0:T(8,128)(2,1)} %copy-done.3, bf16[128,1024]{1,0:T(8,128)(2,1)} %copy-done.4), custom_call_target="tpu_custom_call" | custom-call | flops 268435456 | bytes 4194304 | tf_op jit(solution)/shard_map/pallas_call | solution.py:113
  47.8 0.0 reduce-scatter.2.cloned.1.call-update
  47.8 0.0 collective-permute-done.3.refs_0_
  47.9 10.2 %collective-permute-done.4.refs_1_ = bf16[128,1024]{1,0:T(8,128)(2,1)S(1)} collective-permute-done((bf16[128,1024]{1,0:T(8,128)(2,1)}, bf16[128,1024]{1,0:T(8,128)(2,1)S(1)}, u32[]{:S(2)}, u32[]{:S(2)}) %collective-permute-start.4) | collective-permute-done | bytes 262176 | tf_op jit(solution)/shard_map/ppermute | solution.py:109
  58.1 0.7 copy-done.6
  58.8 4.1 %shard_map.48 = f32[8,2,128,128]{3,2,1,0:T(8,128)} custom-call(bf16[1024,1024]{1,0:T(8,128)(2,1)} %all-gather.2.cloned.1.call-done.rows_ref, bf16[128,1024]{1,0:T(8,128)(2,1)} %copy-done.5, bf16[128,1024]{1,0:T(8,128)(2,1)} %copy-done.6), custom_call_target="tpu_custom_call" | custom-call | flops 161061273600 | bytes 4194304 | tf_op jit(solution)/shard_map/pallas_call | solution.py:113
  62.9 0.0 copy-start
  62.9 0.0 copy-start.2
  63.0 46.7 %all_to_all.5.parts_ref = f32[8,2,128,128]{3,2,1,0:T(8,128)S(1)} all-to-all(f32[8,2,128,128]{3,2,1,0:T(8,128)} %shard_map.48), channel_id=1, replica_groups=mesh['z'=8,'y'=8,'k'=8] {'z'}, dimensions={0} | all-to-all | bytes 2097152 | tf_op jit(solution)/shard_map/all_to_all | solution.py:145
  109.7 0.1 shard_map.49
  109.7 4.0 %collective-permute-start.5 = (f32[2,128,128]{2,1,0:T(8,128)S(1)}, f32[2,128,128]{2,1,0:T(8,128)S(1)}, u32[]{:S(2)}, u32[]{:S(2)}) collective-permute-start(f32[2,128,128]{2,1,0:T(8,128)S(1)} %get-tuple-element.8), channel_id=1, source_target_pairs={{0,0},{1,7},{2,6},{3,5},{4,4},{5,3},{6,2},{7,1},{8,8},{9,15},{10,1... | collective-permute-start | bytes 393224 | tf_op jit(solution)/shard_map/ppermute | solution.py:109
  113.7 1.9 %collective-permute-start.7 = (f32[128,128]{1,0:T(8,128)S(1)}, f32[128,128]{1,0:T(8,128)S(1)}, u32[]{:S(2)}, u32[]{:S(2)}) collective-permute-start(f32[128,128]{1,0:T(8,128)S(1)} %get-tuple-element.9), channel_id=1, source_target_pairs={{0,16},{1,17},{2,18},{3,19},{4,20},{5,21},{6,22},{7,23},{8,24},{9,... | collective-permute-start | bytes 196616 | tf_op jit(solution)/shard_map/ppermute | solution.py:109
  115.6 7.8 %collective-permute-start.8 = (f32[128,128]{1,0:T(8,128)S(1)}, f32[128,128]{1,0:T(8,128)S(1)}, u32[]{:S(2)}, u32[]{:S(2)}) collective-permute-start(f32[128,128]{1,0:T(8,128)S(1)} %get-tuple-element.10), channel_id=1, source_target_pairs={{0,24},{1,25},{2,26},{3,27},{4,28},{5,29},{6,30},{7,31},{8,32},{9,... | collective-permute-start | bytes 196616 | tf_op jit(solution)/shard_map/ppermute | solution.py:109
  123.4 0.0 reduce-scatter.2.cloned.1.call-done
  123.4 3.4 %collective-permute-start.2 = (f32[3,128,128]{2,1,0:T(8,128)}, f32[3,128,128]{2,1,0:T(8,128)S(1)}, u32[]{:S(2)}, u32[]{:S(2)}) collective-permute-start(f32[3,128,128]{2,1,0:T(8,128)} %bitcast.7), channel_id=1, source_target_pairs={{0,0},{1,7},{2,6},{3,5},{4,4},{5,3},{6,2},{7,1},{8,8},{9,15},{10,1... | collective-permute-start | bytes 589832 | tf_op jit(solution)/shard_map/ppermute | solution.py:109
  126.9 0.9 slice_bitcast_fusion
  127.7 2.5 %collective-permute-start.6 = (f32[128,128]{1,0:T(8,128)S(1)}, f32[128,128]{1,0:T(8,128)S(1)}, u32[]{:S(2)}, u32[]{:S(2)}) collective-permute-start(f32[128,128]{1,0:T(8,128)S(1)} %slice_bitcast_fusion), channel_id=1, source_target_pairs={{0,56},{1,57},{2,58},{3,59},{4,60},{5,61},{6,62},{7,63},{8,0},{9,1... | collective-permute-start | bytes 196616 | tf_op jit(solution)/shard_map/ppermute | solution.py:109
  130.3 0.0 collective-permute-done.7.refs_1_
  130.3 0.0 collective-permute-done.5.late
  130.3 3.6 %collective-permute-done.6.refs_0_ = f32[128,128]{1,0:T(8,128)S(1)} collective-permute-done((f32[128,128]{1,0:T(8,128)S(1)}, f32[128,128]{1,0:T(8,128)S(1)}, u32[]{:S(2)}, u32[]{:S(2)}) %collective-permute-start.6) | collective-permute-done | bytes 65568 | tf_op jit(solution)/shard_map/ppermute | solution.py:109
  133.9 0.9 copy-done.1
  134.8 1.6 %shard_map.50 = f32[8,128,128]{2,1,0:T(8,128)} custom-call(s32[8]{0:T(128)S(1)} %bitcast.9, f32[3,128,128]{2,1,0:T(8,128)S(1)} %bitcast.8, f32[3,128,128]{2,1,0:T(8,128)S(1)} %collective-permute-done.2.early, f32[2,128,128]{2,1,0:T(8,128)S(1)} %collective-permute-done.5.late, f32[128,128]{1,0:T(8,128)S(1)} %collective-permute-done.6.refs_0_, ...), custom_call_target="tpu_custom_call" | custom-call | tf_op jit(solution)/shard_map/pallas_call | solution.py:158
  (13 shorter events, 0.0 us)
Async XLA Ops:
  6.5 36.9 %all-gather.2.cloned.1.call-start = ((), (), s32[]{:S(2)}) async-start(), calls=%async_computation.2 | async-start | bytes 2359296 | tf_op jit(solution)/shard_map/all_gather | solution.py:137
  8.2 115.2 %reduce-scatter.2.cloned.1.call-start = ((), (), s32[]{:S(2)}) async-start(), calls=%async_computation.3 | async-start | bytes 1769472 | tf_op jit(solution)/shard_map/reduce_scatter | solution.py:141
  8.3 17.1 %collective-permute-start = (bf16[128,1024]{1,0:T(8,128)(2,1)}, bf16[128,1024]{1,0:T(8,128)(2,1)S(1)}, u32[]{:S(2)}, u32[]{:S(2)}) collective-permute-start(bf16[128,1024]{1,0:T(8,128)(2,1)} %shard_map.46.refs_0_), channel_id=1, source_target_pairs={{0,8},{1,9},{2,10},{3,11},{4,12},{5,13},{6,14},{7,15},{8,16},{9,17... | collective-permute-start | bytes 786440 | tf_op jit(solution)/shard_map/ppermute | solution.py:109
  11.8 20.8 %collective-permute-start.1 = (bf16[128,1024]{1,0:T(8,128)(2,1)}, bf16[128,1024]{1,0:T(8,128)(2,1)S(1)}, u32[]{:S(2)}, u32[]{:S(2)}) collective-permute-start(bf16[128,1024]{1,0:T(8,128)(2,1)} %shard_map.46.refs_0_), channel_id=1, source_target_pairs={{0,32},{1,33},{2,34},{3,35},{4,36},{5,37},{6,38},{7,39},{8,40},{9,... | collective-permute-start | bytes 786440 | tf_op jit(solution)/shard_map/ppermute | solution.py:109
  18.6 29.2 %collective-permute-start.3 = (bf16[128,1024]{1,0:T(8,128)(2,1)}, bf16[128,1024]{1,0:T(8,128)(2,1)S(1)}, u32[]{:S(2)}, u32[]{:S(2)}) collective-permute-start(bf16[128,1024]{1,0:T(8,128)(2,1)} %shard_map.46.refs_0_), channel_id=1, source_target_pairs={{0,48},{1,49},{2,50},{3,51},{4,52},{5,53},{6,54},{7,55},{8,56},{9,... | collective-permute-start | bytes 786440 | tf_op jit(solution)/shard_map/ppermute | solution.py:109
  21.8 36.3 %collective-permute-start.4 = (bf16[128,1024]{1,0:T(8,128)(2,1)}, bf16[128,1024]{1,0:T(8,128)(2,1)S(1)}, u32[]{:S(2)}, u32[]{:S(2)}) collective-permute-start(bf16[128,1024]{1,0:T(8,128)(2,1)} %shard_map.46.refs_0_), channel_id=1, source_target_pairs={{0,40},{1,41},{2,42},{3,43},{4,44},{5,45},{6,46},{7,47},{8,48},{9,... | collective-permute-start | bytes 786440 | tf_op jit(solution)/shard_map/ppermute | solution.py:109
  25.4 18.0 %copy-start.3 = (bf16[128,1024]{1,0:T(8,128)(2,1)}, bf16[128,1024]{1,0:T(8,128)(2,1)S(1)}, u32[]{:S(2)}) copy-start(bf16[128,1024]{1,0:T(8,128)(2,1)S(1)} %collective-permute-done.refs_1_) | copy-start | bytes 786436
  32.6 10.8 %copy-start.4 = (bf16[128,1024]{1,0:T(8,128)(2,1)}, bf16[128,1024]{1,0:T(8,128)(2,1)S(1)}, u32[]{:S(2)}) copy-start(bf16[128,1024]{1,0:T(8,128)(2,1)S(1)} %collective-permute-done.1.refs_2_) | copy-start | bytes 786436
  47.8 10.2 %copy-start.5 = (bf16[128,1024]{1,0:T(8,128)(2,1)}, bf16[128,1024]{1,0:T(8,128)(2,1)S(1)}, u32[]{:S(2)}) copy-start(bf16[128,1024]{1,0:T(8,128)(2,1)S(1)} %collective-permute-done.3.refs_0_) | copy-start | bytes 786436
  58.1 0.7 copy-start.6
  62.9 70.9 %copy-start = (f32[1,1,8,128,128]{4,3,2,1,0:T(8,128)S(1)}, f32[1,1,8,128,128]{4,3,2,1,0:T(8,128)}, u32[]{:S(2)}) copy-start(f32[1,1,8,128,128]{4,3,2,1,0:T(8,128)} %param.6) | copy-start | bytes 1572868
  62.9 70.9 %copy-start.2 = (s32[1,1,8]{2,1,0:T(1,128)S(1)}, s32[1,1,8]{2,1,0:T(1,128)}, u32[]{:S(2)}) copy-start(s32[1,1,8]{2,1,0:T(1,128)} %param.7) | copy-start | bytes 100
  109.7 20.6 %collective-permute-start.5 = (f32[2,128,128]{2,1,0:T(8,128)S(1)}, f32[2,128,128]{2,1,0:T(8,128)S(1)}, u32[]{:S(2)}, u32[]{:S(2)}) collective-permute-start(f32[2,128,128]{2,1,0:T(8,128)S(1)} %get-tuple-element.8), channel_id=1, source_target_pairs={{0,0},{1,7},{2,6},{3,5},{4,4},{5,3},{6,2},{7,1},{8,8},{9,15},{10,1... | collective-permute-start | bytes 393224 | tf_op jit(solution)/shard_map/ppermute | solution.py:109
  113.7 16.6 %collective-permute-start.7 = (f32[128,128]{1,0:T(8,128)S(1)}, f32[128,128]{1,0:T(8,128)S(1)}, u32[]{:S(2)}, u32[]{:S(2)}) collective-permute-start(f32[128,128]{1,0:T(8,128)S(1)} %get-tuple-element.9), channel_id=1, source_target_pairs={{0,16},{1,17},{2,18},{3,19},{4,20},{5,21},{6,22},{7,23},{8,24},{9,... | collective-permute-start | bytes 196616 | tf_op jit(solution)/shard_map/ppermute | solution.py:109
  115.6 14.6 %collective-permute-start.8 = (f32[128,128]{1,0:T(8,128)S(1)}, f32[128,128]{1,0:T(8,128)S(1)}, u32[]{:S(2)}, u32[]{:S(2)}) collective-permute-start(f32[128,128]{1,0:T(8,128)S(1)} %get-tuple-element.10), channel_id=1, source_target_pairs={{0,24},{1,25},{2,26},{3,27},{4,28},{5,29},{6,30},{7,31},{8,32},{9,... | collective-permute-start | bytes 196616 | tf_op jit(solution)/shard_map/ppermute | solution.py:109
  123.4 10.4 %collective-permute-start.2 = (f32[3,128,128]{2,1,0:T(8,128)}, f32[3,128,128]{2,1,0:T(8,128)S(1)}, u32[]{:S(2)}, u32[]{:S(2)}) collective-permute-start(f32[3,128,128]{2,1,0:T(8,128)} %bitcast.7), channel_id=1, source_target_pairs={{0,0},{1,7},{2,6},{3,5},{4,4},{5,3},{6,2},{7,1},{8,8},{9,15},{10,1... | collective-permute-start | bytes 589832 | tf_op jit(solution)/shard_map/ppermute | solution.py:109
  127.7 6.1 %collective-permute-start.6 = (f32[128,128]{1,0:T(8,128)S(1)}, f32[128,128]{1,0:T(8,128)S(1)}, u32[]{:S(2)}, u32[]{:S(2)}) collective-permute-start(f32[128,128]{1,0:T(8,128)S(1)} %slice_bitcast_fusion), channel_id=1, source_target_pairs={{0,56},{1,57},{2,58},{3,59},{4,60},{5,61},{6,62},{7,63},{8,0},{9,1... | collective-permute-start | bytes 196616 | tf_op jit(solution)/shard_map/ppermute | solution.py:109
  133.9 0.9 copy-start.1
Sparse Core Ops, SparseCore 0:
  9.5 33.8 all-gather.1
  48.0 60.2 reduce-scatter.1

commit v6 on v4

--- a/solution.py
+++ b/solution.py
@@ -11,7 +11,7 @@
 LASSO = 0.1
 RIDGE = 0.5
 AXES = ("z", "y", "k")
-OFFSETS = (0, 7, 2, 3, 4)
+OFFSETS = (0, 7, 6, 3, 4)
 TURNED = (1, 2, 3)
 CHUNKS = 4
 MIB = 2**20
@@ -82,7 +82,7 @@
             shrunk = jnp.where(on_diag, stepped, shrunk)
         out_ref[t] = shrunk * active_ref[t].astype(jnp.float32)
 
-    put(0, own[0].T)
+    put(0, own[...].T)
     for i in range(1, len(OFFSETS)):
         put(OFFSETS[i], mirrored[i])
     for i, ref in zip(TURNED, arrived):
@@ -137,7 +137,7 @@
         in_specs=[smem] + [vmem] * (3 + len(TURNED)),
         out_specs=vmem,
         compiler_params=pltpu.CompilerParams(vmem_limit_bytes=16 * MIB),
-    )(active.reshape(n), summed, mirrored, *arrived, precision.reshape(n, tile, tile))
+    )(active.reshape(n), summed[0], mirrored, *arrived, precision.reshape(n, tile, tile))
     return updated.reshape(precision.shape)
 
 

time: 144 us -> 133 us (0.924)
  the two profiles are of different devices: /device:TPU:58 before, /device:TPU:26 now
where the time goes in v6:
time: 133 us
  waiting for transfers between devices  76.7 us (58%)
  starting transfers between devices  31.4 us (24%)
  between operations  13.5 us (10%)
  Pallas kernels  9.09 us (7%)
  local copies, waits for them, and re-layouts  1.83 us (1%)
    reduce_scatter x1, waiting for transfers between devices, local(): summed = lax.psum_scatter(partial, 'z', scatter_dimension=0, tiled=True)[0]  52.4 us
    ppermute x8, starting transfers between devices, moved(): return lax.ppermute(a, AXES, [(index(*i), index(*to(*i))) for i in ids])  31.3 us
    ppermute x8, waiting for transfers between devices, moved(): return lax.ppermute(a, AXES, [(index(*i), index(*to(*i))) for i in ids])  24.3 us
    pallas_call x1, Pallas kernels, local(): pl.pallas_call(functools.partial(products, n, tile, depth), out_shape=jax...  5.79 us
  transfers between devices with their start and end apart: 10, of which 5 were waited for; matrix products, arithmetic and copies ran while one was open for 1% of the time, Pallas kernels for 0%

profile of v6, /device:TPU:26, one launch (start us, length us, event | category | flops | bytes accessed | tf_op | source)
XLA Modules:
  0.0 132.5 jit_solution(16027393678108010780)
XLA Ops:
  6.5 0.0 all-gather.2.cloned.1.call-start
  6.5 1.7 %shard_map.46.refs_0_ = bf16[128,1024]{1,0:T(8,128)(2,1)} custom-call(bf16[128,512]{1,0:T(8,128)(2,1)} %a_ref.1, bf16[128,512]{1,0:T(8,128)(2,1)} %b_ref.1), custom_call_target="tpu_custom_call" | custom-call | tf_op jit(solution)/shard_map/pallas_call | solution.py:104
  8.2 0.0 all-gather.2.cloned.1.call-update
  8.2 0.0 reduce-scatter.2.cloned.1.call-start
  8.3 5.0 %collective-permute-start.3 = (bf16[128,1024]{1,0:T(8,128)(2,1)}, bf16[128,1024]{1,0:T(8,128)(2,1)S(1)}, u32[]{:S(2)}, u32[]{:S(2)}) collective-permute-start(bf16[128,1024]{1,0:T(8,128)(2,1)} %shard_map.46.refs_0_), channel_id=1, source_target_pairs={{0,32},{1,33},{2,34},{3,35},{4,36},{5,37},{6,38},{7,39},{8,40},{9,... | collective-permute-start | bytes 786440 | tf_op jit(solution)/shard_map/ppermute | solution.py:102
  13.3 4.8 %collective-permute-start.2 = (bf16[128,1024]{1,0:T(8,128)(2,1)}, bf16[128,1024]{1,0:T(8,128)(2,1)S(1)}, u32[]{:S(2)}, u32[]{:S(2)}) collective-permute-start(bf16[128,1024]{1,0:T(8,128)(2,1)} %shard_map.46.refs_0_), channel_id=1, source_target_pairs={{0,40},{1,41},{2,42},{3,43},{4,44},{5,45},{6,46},{7,47},{8,48},{9,... | collective-permute-start | bytes 786440 | tf_op jit(solution)/shard_map/ppermute | solution.py:102
  18.2 3.9 %collective-permute-start.1 = (bf16[128,1024]{1,0:T(8,128)(2,1)}, bf16[128,1024]{1,0:T(8,128)(2,1)S(1)}, u32[]{:S(2)}, u32[]{:S(2)}) collective-permute-start(bf16[128,1024]{1,0:T(8,128)(2,1)} %shard_map.46.refs_0_), channel_id=1, source_target_pairs={{0,16},{1,17},{2,18},{3,19},{4,20},{5,21},{6,22},{7,23},{8,24},{9,... | collective-permute-start | bytes 786440 | tf_op jit(solution)/shard_map/ppermute | solution.py:102
  22.1 2.6 %collective-permute-start = (bf16[128,1024]{1,0:T(8,128)(2,1)}, bf16[128,1024]{1,0:T(8,128)(2,1)S(1)}, u32[]{:S(2)}, u32[]{:S(2)}) collective-permute-start(bf16[128,1024]{1,0:T(8,128)(2,1)} %shard_map.46.refs_0_), channel_id=1, source_target_pairs={{0,8},{1,9},{2,10},{3,11},{4,12},{5,13},{6,14},{7,15},{8,16},{9,17... | collective-permute-start | bytes 786440 | tf_op jit(solution)/shard_map/ppermute | solution.py:102
  24.7 4.2 %collective-permute-done.3.refs_4_ = bf16[128,1024]{1,0:T(8,128)(2,1)S(1)} collective-permute-done((bf16[128,1024]{1,0:T(8,128)(2,1)}, bf16[128,1024]{1,0:T(8,128)(2,1)S(1)}, u32[]{:S(2)}, u32[]{:S(2)}) %collective-permute-start.3) | collective-permute-done | bytes 262176 | tf_op jit(solution)/shard_map/ppermute | solution.py:102
  28.8 14.7 %collective-permute-done.2.refs_3_ = bf16[128,1024]{1,0:T(8,128)(2,1)S(1)} collective-permute-done((bf16[128,1024]{1,0:T(8,128)(2,1)}, bf16[128,1024]{1,0:T(8,128)(2,1)S(1)}, u32[]{:S(2)}, u32[]{:S(2)}) %collective-permute-start.2) | collective-permute-done | bytes 262176 | tf_op jit(solution)/shard_map/ppermute | solution.py:102
  43.6 0.0 collective-permute-done.1.refs_2_
  43.6 0.0 collective-permute-done.refs_1_
  43.6 0.0 copy-start.5
  43.6 0.0 all-gather.2.cloned.1.call-done.rows_ref
  43.6 0.7 copy-done.3
  44.3 0.1 copy-done.4
  44.4 0.1 copy-done.5
  44.5 5.8 %shard_map.47 = f32[8,5,128,128]{3,2,1,0:T(8,128)} custom-call(bf16[1024,1024]{1,0:T(8,128)(2,1)} %all-gather.2.cloned.1.call-done.rows_ref, bf16[128,1024]{1,0:T(8,128)(2,1)} %shard_map.46.refs_0_, bf16[128,1024]{1,0:T(8,128)(2,1)} %copy-done.5, bf16[128,1024]{1,0:T(8,128)(2,1)} %copy-done.4, bf16[128,1024]{1,0:T(8,128)(2,1)} %copy-done.3, ...), custom_call_target="tpu_custom_call" | custom-call | flops 1342177280 | bytes 6291456 | tf_op jit(solution)/shard_map/pallas_call | solution.py:113
  50.3 0.0 copy-start
  50.3 0.0 copy-start.1
  50.3 0.0 reduce-scatter.2.cloned.1.call-update
  50.3 52.4 %reduce-scatter.2.cloned.1.call-done = f32[1,5,128,128]{3,2,1,0:T(8,128)} async-done(((f32[8,5,128,128]{3,2,1,0:T(8,128)}), f32[1,5,128,128]{3,2,1,0:T(8,128)}) %reduce-scatter.2.cloned.1.call-update) | async-done | bytes 327696 | tf_op jit(solution)/shard_map/reduce_scatter | solution.py:131
  102.7 4.0 %collective-permute-start.4 = (f32[5,128,128]{2,1,0:T(8,128)}, f32[5,128,128]{2,1,0:T(8,128)S(1)}, u32[]{:S(2)}, u32[]{:S(2)}) collective-permute-start(f32[5,128,128]{2,1,0:T(8,128)} %bitcast.14), channel_id=1, source_target_pairs={{0,0},{1,7},{2,6},{3,5},{4,4},{5,3},{6,2},{7,1},{8,8},{9,15},{10,1... | collective-permute-start | bytes 983048 | tf_op jit(solution)/shard_map/ppermute | solution.py:102
  106.7 1.0 slice_bitcast_fusion
  107.7 4.7 %collective-permute-start.7 = (f32[128,128]{1,0:T(8,128)S(1)}, f32[128,128]{1,0:T(8,128)S(1)}, u32[]{:S(2)}, u32[]{:S(2)}) collective-permute-start(f32[128,128]{1,0:T(8,128)S(1)} %get-tuple-element.5), channel_id=1, source_target_pairs={{0,24},{1,25},{2,26},{3,27},{4,28},{5,29},{6,30},{7,31},{8,32},{9,... | collective-permute-start | bytes 196616 | tf_op jit(solution)/shard_map/ppermute | solution.py:102
  112.3 4.4 %collective-permute-start.6 = (f32[128,128]{1,0:T(8,128)S(1)}, f32[128,128]{1,0:T(8,128)S(1)}, u32[]{:S(2)}, u32[]{:S(2)}) collective-permute-start(f32[128,128]{1,0:T(8,128)S(1)} %get-tuple-element.6), channel_id=1, source_target_pairs={{0,48},{1,49},{2,50},{3,51},{4,52},{5,53},{6,54},{7,55},{8,56},{9,... | collective-permute-start | bytes 196616 | tf_op jit(solution)/shard_map/ppermute | solution.py:102
  116.7 1.9 %collective-permute-start.5 = (f32[128,128]{1,0:T(8,128)S(1)}, f32[128,128]{1,0:T(8,128)S(1)}, u32[]{:S(2)}, u32[]{:S(2)}) collective-permute-start(f32[128,128]{1,0:T(8,128)S(1)} %get-tuple-element.7), channel_id=1, source_target_pairs={{0,56},{1,57},{2,58},{3,59},{4,60},{5,61},{6,62},{7,63},{8,0},{9,1... | collective-permute-start | bytes 196616 | tf_op jit(solution)/shard_map/ppermute | solution.py:102
  118.6 0.0 collective-permute-done.7.refs_2_
  118.7 2.2 %collective-permute-done.6.refs_1_ = f32[128,128]{1,0:T(8,128)S(1)} collective-permute-done((f32[128,128]{1,0:T(8,128)S(1)}, f32[128,128]{1,0:T(8,128)S(1)}, u32[]{:S(2)}, u32[]{:S(2)}) %collective-permute-start.6) | collective-permute-done | bytes 65568 | tf_op jit(solution)/shard_map/ppermute | solution.py:102
  120.8 3.3 %collective-permute-done.5.refs_0_ = f32[128,128]{1,0:T(8,128)S(1)} collective-permute-done((f32[128,128]{1,0:T(8,128)S(1)}, f32[128,128]{1,0:T(8,128)S(1)}, u32[]{:S(2)}, u32[]{:S(2)}) %collective-permute-start.5) | collective-permute-done | bytes 65568 | tf_op jit(solution)/shard_map/ppermute | solution.py:102
  124.1 0.0 collective-permute-done.4.mirrored
  124.1 1.6 %shard_map.48 = f32[8,128,128]{2,1,0:T(8,128)} custom-call(s32[8]{0:T(128)S(1)} %bitcast.13, f32[128,128]{1,0:T(8,128)S(1)} %get-tuple-element.8.own, f32[5,128,128]{2,1,0:T(8,128)S(1)} %collective-permute-done.4.mirrored, f32[128,128]{1,0:T(8,128)S(1)} %collective-permute-done.5.refs_0_, f32[128,128]{1,0:T(8,128)S(1)} %collective-permute-done.6.refs_1_, ...), custom_call_target="tpu_custom_call" | custom-call | tf_op jit(solution)/shard_map/pallas_call | solution.py:134
  (6 shorter events, 0.0 us)
Async XLA Ops:
  6.5 37.1 %all-gather.2.cloned.1.call-start = ((), (), s32[]{:S(2)}) async-start(), calls=%async_computation.1 | async-start | bytes 2359296 | tf_op jit(solution)/shard_map/all_gather | solution.py:111
  8.2 94.5 %reduce-scatter.2.cloned.1.call-start = ((), (), s32[]{:S(2)}) async-start(), calls=%async_computation.2 | async-start | bytes 2949120 | tf_op jit(solution)/shard_map/reduce_scatter | solution.py:131
  8.3 20.5 %collective-permute-start.3 = (bf16[128,1024]{1,0:T(8,128)(2,1)}, bf16[128,1024]{1,0:T(8,128)(2,1)S(1)}, u32[]{:S(2)}, u32[]{:S(2)}) collective-permute-start(bf16[128,1024]{1,0:T(8,128)(2,1)} %shard_map.46.refs_0_), channel_id=1, source_target_pairs={{0,32},{1,33},{2,34},{3,35},{4,36},{5,37},{6,38},{7,39},{8,40},{9,... | collective-permute-start | bytes 786440 | tf_op jit(solution)/shard_map/ppermute | solution.py:102
  13.3 30.2 %collective-permute-start.2 = (bf16[128,1024]{1,0:T(8,128)(2,1)}, bf16[128,1024]{1,0:T(8,128)(2,1)S(1)}, u32[]{:S(2)}, u32[]{:S(2)}) collective-permute-start(bf16[128,1024]{1,0:T(8,128)(2,1)} %shard_map.46.refs_0_), channel_id=1, source_target_pairs={{0,40},{1,41},{2,42},{3,43},{4,44},{5,45},{6,46},{7,47},{8,48},{9,... | collective-permute-start | bytes 786440 | tf_op jit(solution)/shard_map/ppermute | solution.py:102
  18.2 25.4 %collective-permute-start.1 = (bf16[128,1024]{1,0:T(8,128)(2,1)}, bf16[128,1024]{1,0:T(8,128)(2,1)S(1)}, u32[]{:S(2)}, u32[]{:S(2)}) collective-permute-start(bf16[128,1024]{1,0:T(8,128)(2,1)} %shard_map.46.refs_0_), channel_id=1, source_target_pairs={{0,16},{1,17},{2,18},{3,19},{4,20},{5,21},{6,22},{7,23},{8,24},{9,... | collective-permute-start | bytes 786440 | tf_op jit(solution)/shard_map/ppermute | solution.py:102
  22.1 21.5 %collective-permute-start = (bf16[128,1024]{1,0:T(8,128)(2,1)}, bf16[128,1024]{1,0:T(8,128)(2,1)S(1)}, u32[]{:S(2)}, u32[]{:S(2)}) collective-permute-start(bf16[128,1024]{1,0:T(8,128)(2,1)} %shard_map.46.refs_0_), channel_id=1, source_target_pairs={{0,8},{1,9},{2,10},{3,11},{4,12},{5,13},{6,14},{7,15},{8,16},{9,17... | collective-permute-start | bytes 786440 | tf_op jit(solution)/shard_map/ppermute | solution.py:102
  28.8 14.8 %copy-start.2 = (bf16[128,1024]{1,0:T(8,128)(2,1)}, bf16[128,1024]{1,0:T(8,128)(2,1)S(1)}, u32[]{:S(2)}) copy-start(bf16[128,1024]{1,0:T(8,128)(2,1)S(1)} %collective-permute-done.3.refs_4_) | copy-start | bytes 786436
  43.6 0.7 copy-start.3
  43.6 0.8 copy-start.4
  43.6 0.9 copy-start.5
  50.3 73.8 %copy-start = (f32[1,1,8,128,128]{4,3,2,1,0:T(8,128)S(1)}, f32[1,1,8,128,128]{4,3,2,1,0:T(8,128)}, u32[]{:S(2)}) copy-start(f32[1,1,8,128,128]{4,3,2,1,0:T(8,128)} %param.6) | copy-start | bytes 1572868
  50.3 73.8 %copy-start.1 = (s32[1,1,8]{2,1,0:T(1,128)S(1)}, s32[1,1,8]{2,1,0:T(1,128)}, u32[]{:S(2)}) copy-start(s32[1,1,8]{2,1,0:T(1,128)} %param.7) | copy-start | bytes 100
  102.7 21.4 %collective-permute-start.4 = (f32[5,128,128]{2,1,0:T(8,128)}, f32[5,128,128]{2,1,0:T(8,128)S(1)}, u32[]{:S(2)}, u32[]{:S(2)}) collective-permute-start(f32[5,128,128]{2,1,0:T(8,128)} %bitcast.14), channel_id=1, source_target_pairs={{0,0},{1,7},{2,6},{3,5},{4,4},{5,3},{6,2},{7,1},{8,8},{9,15},{10,1... | collective-permute-start | bytes 983048 | tf_op jit(solution)/shard_map/ppermute | solution.py:102
  107.7 11.0 %collective-permute-start.7 = (f32[128,128]{1,0:T(8,128)S(1)}, f32[128,128]{1,0:T(8,128)S(1)}, u32[]{:S(2)}, u32[]{:S(2)}) collective-permute-start(f32[128,128]{1,0:T(8,128)S(1)} %get-tuple-element.5), channel_id=1, source_target_pairs={{0,24},{1,25},{2,26},{3,27},{4,28},{5,29},{6,30},{7,31},{8,32},{9,... | collective-permute-start | bytes 196616 | tf_op jit(solution)/shard_map/ppermute | solution.py:102
  112.3 8.5 %collective-permute-start.6 = (f32[128,128]{1,0:T(8,128)S(1)}, f32[128,128]{1,0:T(8,128)S(1)}, u32[]{:S(2)}, u32[]{:S(2)}) collective-permute-start(f32[128,128]{1,0:T(8,128)S(1)} %get-tuple-element.6), channel_id=1, source_target_pairs={{0,48},{1,49},{2,50},{3,51},{4,52},{5,53},{6,54},{7,55},{8,56},{9,... | collective-permute-start | bytes 196616 | tf_op jit(solution)/shard_map/ppermute | solution.py:102
  116.7 7.4 %collective-permute-start.5 = (f32[128,128]{1,0:T(8,128)S(1)}, f32[128,128]{1,0:T(8,128)S(1)}, u32[]{:S(2)}, u32[]{:S(2)}) collective-permute-start(f32[128,128]{1,0:T(8,128)S(1)} %get-tuple-element.7), channel_id=1, source_target_pairs={{0,56},{1,57},{2,58},{3,59},{4,60},{5,61},{6,62},{7,63},{8,0},{9,1... | collective-permute-start | bytes 196616 | tf_op jit(solution)/shard_map/ppermute | solution.py:102
Sparse Core Ops, SparseCore 0:
  9.5 33.5 all-gather.1
  50.5 52.2 reduce-scatter.1

commit v7 on v6

--- a/solution.py
+++ b/solution.py
@@ -11,9 +11,9 @@
 LASSO = 0.1
 RIDGE = 0.5
 AXES = ("z", "y", "k")
-OFFSETS = (0, 7, 6, 3, 4)
-TURNED = (1, 2, 3)
-CHUNKS = 4
+OFFSETS = (0, 7, 6, 4, 3)
+TURNED = (1, 2, 4)
+CHUNKS = 2
 MIB = 2**20
 
 
@@ -25,22 +25,27 @@
 
 def products(n, tile, depth, rows_ref, *refs):
     count = len(OFFSETS)
-    columns, (out_ref, rows, picked, made, row_sems, column_sems, out_sems) = refs[:count], refs[count:]
+    columns, (out_ref, rows, picked, made, own_sems, row_sems, out_sems) = refs[:count - 1], refs[count - 1:]
     k = lax.axis_index("k")
     per = n // CHUNKS
-    loads = []
-    for i, ref in enumerate(columns):
-        at = pl.ds(i * tile, tile)
-        for h in range(2):
-            here, there = pl.ds(h * depth, depth), pl.ds((1 - h) * depth, depth)
-            loads.append(pltpu.make_async_copy(ref.at[:, there], picked.at[at, here], column_sems.at[i, h]))
     chunks = [
         pltpu.make_async_copy(rows_ref.at[pl.ds(c * per * tile, per * tile)], rows.at[c], row_sems.at[c])
         for c in range(CHUNKS)
     ]
-    for copy in loads + chunks:
+    here = [
+        pltpu.make_async_copy(
+            rows_ref.at[pl.ds(pl.multiple_of(k * tile, tile), tile), pl.ds((1 - h) * depth, depth)],
+            picked.at[pl.ds(0, tile), pl.ds(h * depth, depth)],
+            own_sems.at[h],
+        )
+        for h in range(2)
+    ]
+    for copy in here + chunks:
         copy.start()
-    for copy in loads:
+    for i, ref in enumerate(columns, 1):
+        picked[i * tile:(i + 1) * tile, :depth] = ref[:, depth:]
+        picked[i * tile:(i + 1) * tile, depth:] = ref[:, :depth]
+    for copy in here:
         copy.wait()
     stores = []
     for c in range(CHUNKS):
@@ -59,7 +64,7 @@
         copy.wait()
 
 
-def finish(n, tile, scale, active_ref, own, mirrored, *refs):
+def finish(n, tile, scale, active_ref, mirrored, *refs):
     arrived, (precision_ref, out_ref) = refs[:-2], refs[-2:]
     z, y, k = (lax.axis_index(a) for a in AXES)
     row = lax.broadcasted_iota(jnp.int32, (tile, tile), 0)
@@ -82,16 +87,15 @@
             shrunk = jnp.where(on_diag, stepped, shrunk)
         out_ref[t] = shrunk * active_ref[t].astype(jnp.float32)
 
-    put(0, own[...].T)
-    for i in range(1, len(OFFSETS)):
-        put(OFFSETS[i], mirrored[i])
+    for i, d in enumerate(OFFSETS):
+        put(d, mirrored[i])
     for i, ref in zip(TURNED, arrived):
         put(n - OFFSETS[i], ref[...].T)
 
 
 def local(n, resid, samples, precision, active):
     tile, depth = resid.shape
-    vmem, smem, anywhere = (pl.BlockSpec(memory_space=s) for s in (pltpu.VMEM, pltpu.SMEM, pl.ANY))
+    vmem, smem, far = (pl.BlockSpec(memory_space=s) for s in (pltpu.VMEM, pltpu.SMEM, pltpu.HBM))
     count = len(OFFSETS)
 
     def moved(a, to):
@@ -109,21 +113,21 @@
         compiler_params=pltpu.CompilerParams(vmem_limit_bytes=60 * MIB),
     )(resid, samples)
     rows = lax.all_gather(own, "k", axis=0, tiled=True)
-    columns = [own] + [moved(own, lambda z, y, k, d=d: (z, y - d, k)) for d in OFFSETS[1:]]
+    columns = [moved(own, lambda z, y, k, d=d: (z, y - d, k)) for d in OFFSETS[1:]]
     partial = pl.pallas_call(
         functools.partial(products, n, tile, depth),
         out_shape=jax.ShapeDtypeStruct((n, count, tile, tile), jnp.float32),
-        in_specs=[anywhere] * (1 + count),
-        out_specs=anywhere,
+        in_specs=[far] + [vmem] * (count - 1),
+        out_specs=far,
         scratch_shapes=[
             pltpu.VMEM((CHUNKS, n // CHUNKS * tile, 2 * depth), jnp.bfloat16),
             pltpu.VMEM((count * tile, 2 * depth), jnp.bfloat16),
             pltpu.VMEM((n, count, tile, tile), jnp.float32),
+            pltpu.SemaphoreType.DMA((2,)),
             pltpu.SemaphoreType.DMA((CHUNKS,)),
-            pltpu.SemaphoreType.DMA((count, 2)),
             pltpu.SemaphoreType.DMA((n,)),
         ],
-        compiler_params=pltpu.CompilerParams(vmem_limit_bytes=60 * MIB),
+        compiler_params=pltpu.CompilerParams(vmem_limit_bytes=52 * MIB),
         cost_estimate=pl.CostEstimate(
             flops=4 * n * count * tile * tile * depth, bytes_accessed=6 * MIB, transcendentals=0
         ),
@@ -134,10 +138,10 @@
     updated = pl.pallas_call(
         functools.partial(finish, n, tile, 0.5 / (depth * n)),
         out_shape=jax.ShapeDtypeStruct((n, tile, tile), jnp.float32),
-        in_specs=[smem] + [vmem] * (3 + len(TURNED)),
+        in_specs=[smem] + [vmem] * (2 + len(TURNED)),
         out_specs=vmem,
         compiler_params=pltpu.CompilerParams(vmem_limit_bytes=16 * MIB),
-    )(active.reshape(n), summed[0], mirrored, *arrived, precision.reshape(n, tile, tile))
+    )(active.reshape(n), mirrored, *arrived, precision.reshape(n, tile, tile))
     return updated.reshape(precision.shape)
 
 

time: 133 us -> 134 us (level)
  waiting for transfers between devices: 76.7 us -> 79.5 us
    ppermute x8, waiting for transfers between devices: 24.3 us -> 27.6 us  [moved(): return lax.ppermute(a, AXES, [(index(*i), index(*to(*i))) for i in ids])]
  transfers between devices with their start and end apart: 10 -> 10, of which waited for: 5 -> 7; matrix products, arithmetic and copies ran while one was open for 1% -> 1% of each run, Pallas kernels for 0% -> 0%
where the time goes in v7:
time: 134 us; the launch traced here: 133 us
  waiting for transfers between devices  79.5 us (59%)
  starting transfers between devices  31.2 us (23%)
  between operations  13.5 us (10%)
  Pallas kernels  8.16 us (6%)
    reduce_scatter x1, waiting for transfers between devices, local(): summed = lax.psum_scatter(partial, 'z', scatter_dimension=0, tiled=True)[0]  51.8 us
    ppermute x8, starting transfers between devices, moved(): return lax.ppermute(a, AXES, [(index(*i), index(*to(*i))) for i in ids])  31.1 us
    ppermute x8, waiting for transfers between devices, moved(): return lax.ppermute(a, AXES, [(index(*i), index(*to(*i))) for i in ids])  27.6 us
    pallas_call x1, Pallas kernels, local(): pl.pallas_call(functools.partial(products, n, tile, depth), out_shape=jax...  4.9 us
  transfers between devices with their start and end apart: 10, of which 7 were waited for; matrix products, arithmetic and copies ran while one was open for 1% of the time, Pallas kernels for 0%

profile of v7, /device:TPU:26, one launch (start us, length us, event | category | flops | bytes accessed | tf_op | source)
XLA Modules:
  0.0 133.3 jit_solution(3715572265721275641)
XLA Ops:
  6.5 0.0 all-gather.2.cloned.1.call-start
  6.5 1.7 %shard_map.46 = bf16[128,1024]{1,0:T(8,128)(2,1)} custom-call(bf16[128,512]{1,0:T(8,128)(2,1)} %a_ref.1, bf16[128,512]{1,0:T(8,128)(2,1)} %b_ref.1), custom_call_target="tpu_custom_call" | custom-call | tf_op jit(solution)/shard_map/pallas_call | solution.py:108
  8.2 0.0 all-gather.2.cloned.1.call-update
  8.2 0.0 reduce-scatter.2.cloned.1.call-start
  8.3 2.1 %collective-permute-start.3 = (bf16[128,1024]{1,0:T(8,128)(2,1)}, bf16[128,1024]{1,0:T(8,128)(2,1)S(1)}, u32[]{:S(2)}, u32[]{:S(2)}) collective-permute-start(bf16[128,1024]{1,0:T(8,128)(2,1)} %shard_map.46), channel_id=1, source_target_pairs={{0,40},{1,41},{2,42},{3,43},{4,44},{5,45},{6,46},{7,47},{8,48},{9,... | collective-permute-start | bytes 786440 | tf_op jit(solution)/shard_map/ppermute | solution.py:106
  10.4 7.7 %collective-permute-start.2 = (bf16[128,1024]{1,0:T(8,128)(2,1)}, bf16[128,1024]{1,0:T(8,128)(2,1)S(1)}, u32[]{:S(2)}, u32[]{:S(2)}) collective-permute-start(bf16[128,1024]{1,0:T(8,128)(2,1)} %shard_map.46), channel_id=1, source_target_pairs={{0,32},{1,33},{2,34},{3,35},{4,36},{5,37},{6,38},{7,39},{8,40},{9,... | collective-permute-start | bytes 786440 | tf_op jit(solution)/shard_map/ppermute | solution.py:106
  18.2 3.9 %collective-permute-start.1 = (bf16[128,1024]{1,0:T(8,128)(2,1)}, bf16[128,1024]{1,0:T(8,128)(2,1)S(1)}, u32[]{:S(2)}, u32[]{:S(2)}) collective-permute-start(bf16[128,1024]{1,0:T(8,128)(2,1)} %shard_map.46), channel_id=1, source_target_pairs={{0,16},{1,17},{2,18},{3,19},{4,20},{5,21},{6,22},{7,23},{8,24},{9,... | collective-permute-start | bytes 786440 | tf_op jit(solution)/shard_map/ppermute | solution.py:106
  22.1 2.6 %collective-permute-start = (bf16[128,1024]{1,0:T(8,128)(2,1)}, bf16[128,1024]{1,0:T(8,128)(2,1)S(1)}, u32[]{:S(2)}, u32[]{:S(2)}) collective-permute-start(bf16[128,1024]{1,0:T(8,128)(2,1)} %shard_map.46), channel_id=1, source_target_pairs={{0,8},{1,9},{2,10},{3,11},{4,12},{5,13},{6,14},{7,15},{8,16},{9,17... | collective-permute-start | bytes 786440 | tf_op jit(solution)/shard_map/ppermute | solution.py:106
  24.7 7.4 %collective-permute-done.3.refs_3_ = bf16[128,1024]{1,0:T(8,128)(2,1)S(1)} collective-permute-done((bf16[128,1024]{1,0:T(8,128)(2,1)}, bf16[128,1024]{1,0:T(8,128)(2,1)S(1)}, u32[]{:S(2)}, u32[]{:S(2)}) %collective-permute-start.3) | collective-permute-done | bytes 262176 | tf_op jit(solution)/shard_map/ppermute | solution.py:106
  32.1 6.7 %collective-permute-done.2.refs_2_ = bf16[128,1024]{1,0:T(8,128)(2,1)S(1)} collective-permute-done((bf16[128,1024]{1,0:T(8,128)(2,1)}, bf16[128,1024]{1,0:T(8,128)(2,1)S(1)}, u32[]{:S(2)}, u32[]{:S(2)}) %collective-permute-start.2) | collective-permute-done | bytes 262176 | tf_op jit(solution)/shard_map/ppermute | solution.py:106
  38.8 2.6 %collective-permute-done.1.refs_1_ = bf16[128,1024]{1,0:T(8,128)(2,1)S(1)} collective-permute-done((bf16[128,1024]{1,0:T(8,128)(2,1)}, bf16[128,1024]{1,0:T(8,128)(2,1)S(1)}, u32[]{:S(2)}, u32[]{:S(2)}) %collective-permute-start.1) | collective-permute-done | bytes 262176 | tf_op jit(solution)/shard_map/ppermute | solution.py:106
  41.4 5.4 %collective-permute-done.refs_0_ = bf16[128,1024]{1,0:T(8,128)(2,1)S(1)} collective-permute-done((bf16[128,1024]{1,0:T(8,128)(2,1)}, bf16[128,1024]{1,0:T(8,128)(2,1)S(1)}, u32[]{:S(2)}, u32[]{:S(2)}) %collective-permute-start) | collective-permute-done | bytes 262176 | tf_op jit(solution)/shard_map/ppermute | solution.py:106
  46.9 0.0 all-gather.2.cloned.1.call-done.rows_ref
  46.9 4.9 %shard_map.47 = f32[8,5,128,128]{3,2,1,0:T(8,128)} custom-call(bf16[1024,1024]{1,0:T(8,128)(2,1)} %all-gather.2.cloned.1.call-done.rows_ref, bf16[128,1024]{1,0:T(8,128)(2,1)S(1)} %collective-permute-done.refs_0_, bf16[128,1024]{1,0:T(8,128)(2,1)S(1)} %collective-permute-done.1.refs_1_, bf16[128,1024]{1,0:T(8,128)(2,1)S(1)} %collective-permute-done.2.refs_2_, ...), custom_call_target="tpu_custom_call" | custom-call | flops 1342177280 | bytes 6291456 | tf_op jit(solution)/shard_map/pallas_call | solution.py:117
  51.8 0.0 copy-start
  51.8 0.0 copy-start.1
  51.8 0.0 reduce-scatter.2.cloned.1.call-update
  51.8 51.8 %reduce-scatter.2.cloned.1.call-done = f32[1,5,128,128]{3,2,1,0:T(8,128)} async-done(((f32[8,5,128,128]{3,2,1,0:T(8,128)}), f32[1,5,128,128]{3,2,1,0:T(8,128)}) %reduce-scatter.2.cloned.1.call-update) | async-done | bytes 327696 | tf_op jit(solution)/shard_map/reduce_scatter | solution.py:135
  103.7 4.0 %collective-permute-start.4 = (f32[5,128,128]{2,1,0:T(8,128)}, f32[5,128,128]{2,1,0:T(8,128)S(1)}, u32[]{:S(2)}, u32[]{:S(2)}) collective-permute-start(f32[5,128,128]{2,1,0:T(8,128)} %bitcast.12), channel_id=1, source_target_pairs={{0,0},{1,7},{2,6},{3,5},{4,4},{5,3},{6,2},{7,1},{8,8},{9,15},{10,1... | collective-permute-start | bytes 983048 | tf_op jit(solution)/shard_map/ppermute | solution.py:106
  107.7 0.9 slice_bitcast_fusion
  108.6 4.6 %collective-permute-start.7 = (f32[128,128]{1,0:T(8,128)S(1)}, f32[128,128]{1,0:T(8,128)S(1)}, u32[]{:S(2)}, u32[]{:S(2)}) collective-permute-start(f32[128,128]{1,0:T(8,128)S(1)} %get-tuple-element.5), channel_id=1, source_target_pairs={{0,24},{1,25},{2,26},{3,27},{4,28},{5,29},{6,30},{7,31},{8,32},{9,... | collective-permute-start | bytes 196616 | tf_op jit(solution)/shard_map/ppermute | solution.py:106
  113.3 4.2 %collective-permute-start.6 = (f32[128,128]{1,0:T(8,128)S(1)}, f32[128,128]{1,0:T(8,128)S(1)}, u32[]{:S(2)}, u32[]{:S(2)}) collective-permute-start(f32[128,128]{1,0:T(8,128)S(1)} %get-tuple-element.6), channel_id=1, source_target_pairs={{0,48},{1,49},{2,50},{3,51},{4,52},{5,53},{6,54},{7,55},{8,56},{9,... | collective-permute-start | bytes 196616 | tf_op jit(solution)/shard_map/ppermute | solution.py:106
  117.5 1.9 %collective-permute-start.5 = (f32[128,128]{1,0:T(8,128)S(1)}, f32[128,128]{1,0:T(8,128)S(1)}, u32[]{:S(2)}, u32[]{:S(2)}) collective-permute-start(f32[128,128]{1,0:T(8,128)S(1)} %get-tuple-element.7), channel_id=1, source_target_pairs={{0,56},{1,57},{2,58},{3,59},{4,60},{5,61},{6,62},{7,63},{8,0},{9,1... | collective-permute-start | bytes 196616 | tf_op jit(solution)/shard_map/ppermute | solution.py:106
  119.4 0.0 collective-permute-done.7.refs_2_
  119.4 2.2 %collective-permute-done.6.refs_1_ = f32[128,128]{1,0:T(8,128)S(1)} collective-permute-done((f32[128,128]{1,0:T(8,128)S(1)}, f32[128,128]{1,0:T(8,128)S(1)}, u32[]{:S(2)}, u32[]{:S(2)}) %collective-permute-start.6) | collective-permute-done | bytes 65568 | tf_op jit(solution)/shard_map/ppermute | solution.py:106
  121.7 3.2 %collective-permute-done.5.refs_0_ = f32[128,128]{1,0:T(8,128)S(1)} collective-permute-done((f32[128,128]{1,0:T(8,128)S(1)}, f32[128,128]{1,0:T(8,128)S(1)}, u32[]{:S(2)}, u32[]{:S(2)}) %collective-permute-start.5) | collective-permute-done | bytes 65568 | tf_op jit(solution)/shard_map/ppermute | solution.py:106
  124.8 0.0 collective-permute-done.4.mirrored
  124.8 0.0 copy-done
  124.8 0.0 copy-done.1
  124.9 1.6 %shard_map.48 = f32[8,128,128]{2,1,0:T(8,128)} custom-call(s32[8]{0:T(128)S(1)} %bitcast.11, f32[5,128,128]{2,1,0:T(8,128)S(1)} %collective-permute-done.4.mirrored, f32[128,128]{1,0:T(8,128)S(1)} %collective-permute-done.5.refs_0_, f32[128,128]{1,0:T(8,128)S(1)} %collective-permute-done.6.refs_1_, f32[128,128]{1,0:T(8,128)S(1)} %collective-permute-done.7.refs_2_, ...), custom_call_target="tpu_custom_call" | custom-call | tf_op jit(solution)/shard_map/pallas_call | solution.py:138
Async XLA Ops:
  6.5 40.3 %all-gather.2.cloned.1.call-start = ((), (), s32[]{:S(2)}) async-start(), calls=%async_computation.1 | async-start | bytes 2359296 | tf_op jit(solution)/shard_map/all_gather | solution.py:115
  8.2 95.4 %reduce-scatter.2.cloned.1.call-start = ((), (), s32[]{:S(2)}) async-start(), calls=%async_computation.2 | async-start | bytes 2949120 | tf_op jit(solution)/shard_map/reduce_scatter | solution.py:135
  8.3 23.8 %collective-permute-start.3 = (bf16[128,1024]{1,0:T(8,128)(2,1)}, bf16[128,1024]{1,0:T(8,128)(2,1)S(1)}, u32[]{:S(2)}, u32[]{:S(2)}) collective-permute-start(bf16[128,1024]{1,0:T(8,128)(2,1)} %shard_map.46), channel_id=1, source_target_pairs={{0,40},{1,41},{2,42},{3,43},{4,44},{5,45},{6,46},{7,47},{8,48},{9,... | collective-permute-start | bytes 786440 | tf_op jit(solution)/shard_map/ppermute | solution.py:106
  10.4 28.4 %collective-permute-start.2 = (bf16[128,1024]{1,0:T(8,128)(2,1)}, bf16[128,1024]{1,0:T(8,128)(2,1)S(1)}, u32[]{:S(2)}, u32[]{:S(2)}) collective-permute-start(bf16[128,1024]{1,0:T(8,128)(2,1)} %shard_map.46), channel_id=1, source_target_pairs={{0,32},{1,33},{2,34},{3,35},{4,36},{5,37},{6,38},{7,39},{8,40},{9,... | collective-permute-start | bytes 786440 | tf_op jit(solution)/shard_map/ppermute | solution.py:106
  18.2 23.3 %collective-permute-start.1 = (bf16[128,1024]{1,0:T(8,128)(2,1)}, bf16[128,1024]{1,0:T(8,128)(2,1)S(1)}, u32[]{:S(2)}, u32[]{:S(2)}) collective-permute-start(bf16[128,1024]{1,0:T(8,128)(2,1)} %shard_map.46), channel_id=1, source_target_pairs={{0,16},{1,17},{2,18},{3,19},{4,20},{5,21},{6,22},{7,23},{8,24},{9,... | collective-permute-start | bytes 786440 | tf_op jit(solution)/shard_map/ppermute | solution.py:106
  22.1 24.8 %collective-permute-start = (bf16[128,1024]{1,0:T(8,128)(2,1)}, bf16[128,1024]{1,0:T(8,128)(2,1)S(1)}, u32[]{:S(2)}, u32[]{:S(2)}) collective-permute-start(bf16[128,1024]{1,0:T(8,128)(2,1)} %shard_map.46), channel_id=1, source_target_pairs={{0,8},{1,9},{2,10},{3,11},{4,12},{5,13},{6,14},{7,15},{8,16},{9,17... | collective-permute-start | bytes 786440 | tf_op jit(solution)/shard_map/ppermute | solution.py:106
  51.8 73.1 %copy-start = (f32[1,1,8,128,128]{4,3,2,1,0:T(8,128)S(1)}, f32[1,1,8,128,128]{4,3,2,1,0:T(8,128)}, u32[]{:S(2)}) copy-start(f32[1,1,8,128,128]{4,3,2,1,0:T(8,128)} %param.6) | copy-start | bytes 1572868
  51.8 73.1 %copy-start.1 = (s32[1,1,8]{2,1,0:T(1,128)S(1)}, s32[1,1,8]{2,1,0:T(1,128)}, u32[]{:S(2)}) copy-start(s32[1,1,8]{2,1,0:T(1,128)} %param.7) | copy-start | bytes 100
  103.7 21.2 %collective-permute-start.4 = (f32[5,128,128]{2,1,0:T(8,128)}, f32[5,128,128]{2,1,0:T(8,128)S(1)}, u32[]{:S(2)}, u32[]{:S(2)}) collective-permute-start(f32[5,128,128]{2,1,0:T(8,128)} %bitcast.12), channel_id=1, source_target_pairs={{0,0},{1,7},{2,6},{3,5},{4,4},{5,3},{6,2},{7,1},{8,8},{9,15},{10,1... | collective-permute-start | bytes 983048 | tf_op jit(solution)/shard_map/ppermute | solution.py:106
  108.6 10.8 %collective-permute-start.7 = (f32[128,128]{1,0:T(8,128)S(1)}, f32[128,128]{1,0:T(8,128)S(1)}, u32[]{:S(2)}, u32[]{:S(2)}) collective-permute-start(f32[128,128]{1,0:T(8,128)S(1)} %get-tuple-element.5), channel_id=1, source_target_pairs={{0,24},{1,25},{2,26},{3,27},{4,28},{5,29},{6,30},{7,31},{8,32},{9,... | collective-permute-start | bytes 196616 | tf_op jit(solution)/shard_map/ppermute | solution.py:106
  113.3 8.4 %collective-permute-start.6 = (f32[128,128]{1,0:T(8,128)S(1)}, f32[128,128]{1,0:T(8,128)S(1)}, u32[]{:S(2)}, u32[]{:S(2)}) collective-permute-start(f32[128,128]{1,0:T(8,128)S(1)} %get-tuple-element.6), channel_id=1, source_target_pairs={{0,48},{1,49},{2,50},{3,51},{4,52},{5,53},{6,54},{7,55},{8,56},{9,... | collective-permute-start | bytes 196616 | tf_op jit(solution)/shard_map/ppermute | solution.py:106
  117.5 7.4 %collective-permute-start.5 = (f32[128,128]{1,0:T(8,128)S(1)}, f32[128,128]{1,0:T(8,128)S(1)}, u32[]{:S(2)}, u32[]{:S(2)}) collective-permute-start(f32[128,128]{1,0:T(8,128)S(1)} %get-tuple-element.7), channel_id=1, source_target_pairs={{0,56},{1,57},{2,58},{3,59},{4,60},{5,61},{6,62},{7,63},{8,0},{9,1... | collective-permute-start | bytes 196616 | tf_op jit(solution)/shard_map/ppermute | solution.py:106
Sparse Core Ops, SparseCore 0:
  9.5 33.5 all-gather.1
  51.9 51.6 reduce-scatter.1

commit v8 on v7

--- a/solution.py
+++ b/solution.py
@@ -11,8 +11,8 @@
 LASSO = 0.1
 RIDGE = 0.5
 AXES = ("z", "y", "k")
-OFFSETS = (0, 7, 6, 4, 3)
-TURNED = (1, 2, 4)
+OFFSETS = (0, 7, 6, 3, 4)
+TURNED = (1, 2, 3)
 CHUNKS = 2
 MIB = 2**20
 

time: 134 us -> 131 us (0.978)
  waiting for transfers between devices: 79.5 us -> 76.8 us
    ppermute x8, waiting for transfers between devices: 27.6 us -> 24.3 us  [moved(): return lax.ppermute(a, AXES, [(index(*i), index(*to(*i))) for i in ids])]
  transfers between devices with their start and end apart: 10 -> 10, of which waited for: 7 -> 5; matrix products, arithmetic and copies ran while one was open for 1% -> 1% of each run, Pallas kernels for 0% -> 0%
where the time goes in v8:
time: 131 us; the launch traced here: 130 us
  waiting for transfers between devices  76.8 us (59%)
  starting transfers between devices  31.1 us (24%)
  between operations  13.5 us (10%)
  Pallas kernels  8.16 us (6%)
    reduce_scatter x1, waiting for transfers between devices, local(): summed = lax.psum_scatter(partial, 'z', scatter_dimension=0, tiled=True)[0]  52.4 us
    ppermute x8, starting transfers between devices, moved(): return lax.ppermute(a, AXES, [(index(*i), index(*to(*i))) for i in ids])  31.1 us
    ppermute x8, waiting for transfers between devices, moved(): return lax.ppermute(a, AXES, [(index(*i), index(*to(*i))) for i in ids])  24.3 us
    pallas_call x1, Pallas kernels, local(): pl.pallas_call(functools.partial(products, n, tile, depth), out_shape=jax...  4.9 us
  transfers between devices with their start and end apart: 10, of which 5 were waited for; matrix products, arithmetic and copies ran while one was open for 1% of the time, Pallas kernels for 0%

profile of v8, /device:TPU:26, one launch (start us, length us, event | category | flops | bytes accessed | tf_op | source)
XLA Modules:
  0.0 130.5 jit_solution(12784346609321996714)
XLA Ops:
  6.5 0.0 all-gather.2.cloned.1.call-start
  6.5 1.7 %shard_map.46 = bf16[128,1024]{1,0:T(8,128)(2,1)} custom-call(bf16[128,512]{1,0:T(8,128)(2,1)} %a_ref.1, bf16[128,512]{1,0:T(8,128)(2,1)} %b_ref.1), custom_call_target="tpu_custom_call" | custom-call | tf_op jit(solution)/shard_map/pallas_call | solution.py:108
  8.2 0.0 all-gather.2.cloned.1.call-update
  8.2 0.0 reduce-scatter.2.cloned.1.call-start
  8.3 5.0 %collective-permute-start.3 = (bf16[128,1024]{1,0:T(8,128)(2,1)}, bf16[128,1024]{1,0:T(8,128)(2,1)S(1)}, u32[]{:S(2)}, u32[]{:S(2)}) collective-permute-start(bf16[128,1024]{1,0:T(8,128)(2,1)} %shard_map.46), channel_id=1, source_target_pairs={{0,32},{1,33},{2,34},{3,35},{4,36},{5,37},{6,38},{7,39},{8,40},{9,... | collective-permute-start | bytes 786440 | tf_op jit(solution)/shard_map/ppermute | solution.py:106
  13.3 4.8 %collective-permute-start.2 = (bf16[128,1024]{1,0:T(8,128)(2,1)}, bf16[128,1024]{1,0:T(8,128)(2,1)S(1)}, u32[]{:S(2)}, u32[]{:S(2)}) collective-permute-start(bf16[128,1024]{1,0:T(8,128)(2,1)} %shard_map.46), channel_id=1, source_target_pairs={{0,40},{1,41},{2,42},{3,43},{4,44},{5,45},{6,46},{7,47},{8,48},{9,... | collective-permute-start | bytes 786440 | tf_op jit(solution)/shard_map/ppermute | solution.py:106
  18.2 3.9 %collective-permute-start.1 = (bf16[128,1024]{1,0:T(8,128)(2,1)}, bf16[128,1024]{1,0:T(8,128)(2,1)S(1)}, u32[]{:S(2)}, u32[]{:S(2)}) collective-permute-start(bf16[128,1024]{1,0:T(8,128)(2,1)} %shard_map.46), channel_id=1, source_target_pairs={{0,16},{1,17},{2,18},{3,19},{4,20},{5,21},{6,22},{7,23},{8,24},{9,... | collective-permute-start | bytes 786440 | tf_op jit(solution)/shard_map/ppermute | solution.py:106
  22.1 2.6 %collective-permute-start = (bf16[128,1024]{1,0:T(8,128)(2,1)}, bf16[128,1024]{1,0:T(8,128)(2,1)S(1)}, u32[]{:S(2)}, u32[]{:S(2)}) collective-permute-start(bf16[128,1024]{1,0:T(8,128)(2,1)} %shard_map.46), channel_id=1, source_target_pairs={{0,8},{1,9},{2,10},{3,11},{4,12},{5,13},{6,14},{7,15},{8,16},{9,17... | collective-permute-start | bytes 786440 | tf_op jit(solution)/shard_map/ppermute | solution.py:106
  24.7 4.2 %collective-permute-done.3.refs_3_ = bf16[128,1024]{1,0:T(8,128)(2,1)S(1)} collective-permute-done((bf16[128,1024]{1,0:T(8,128)(2,1)}, bf16[128,1024]{1,0:T(8,128)(2,1)S(1)}, u32[]{:S(2)}, u32[]{:S(2)}) %collective-permute-start.3) | collective-permute-done | bytes 262176 | tf_op jit(solution)/shard_map/ppermute | solution.py:106
  28.8 14.7 %collective-permute-done.2.refs_2_ = bf16[128,1024]{1,0:T(8,128)(2,1)S(1)} collective-permute-done((bf16[128,1024]{1,0:T(8,128)(2,1)}, bf16[128,1024]{1,0:T(8,128)(2,1)S(1)}, u32[]{:S(2)}, u32[]{:S(2)}) %collective-permute-start.2) | collective-permute-done | bytes 262176 | tf_op jit(solution)/shard_map/ppermute | solution.py:106
  43.6 0.0 collective-permute-done.1.refs_1_
  43.6 0.0 collective-permute-done.refs_0_
  43.6 0.0 all-gather.2.cloned.1.call-done.rows_ref
  43.6 4.9 %shard_map.47 = f32[8,5,128,128]{3,2,1,0:T(8,128)} custom-call(bf16[1024,1024]{1,0:T(8,128)(2,1)} %all-gather.2.cloned.1.call-done.rows_ref, bf16[128,1024]{1,0:T(8,128)(2,1)S(1)} %collective-permute-done.refs_0_, bf16[128,1024]{1,0:T(8,128)(2,1)S(1)} %collective-permute-done.1.refs_1_, bf16[128,1024]{1,0:T(8,128)(2,1)S(1)} %collective-permute-done.2.refs_2_, ...), custom_call_target="tpu_custom_call" | custom-call | flops 1342177280 | bytes 6291456 | tf_op jit(solution)/shard_map/pallas_call | solution.py:117
  48.5 0.0 copy-start
  48.5 0.0 copy-start.1
  48.5 0.0 reduce-scatter.2.cloned.1.call-update
  48.6 52.4 %reduce-scatter.2.cloned.1.call-done = f32[1,5,128,128]{3,2,1,0:T(8,128)} async-done(((f32[8,5,128,128]{3,2,1,0:T(8,128)}), f32[1,5,128,128]{3,2,1,0:T(8,128)}) %reduce-scatter.2.cloned.1.call-update) | async-done | bytes 327696 | tf_op jit(solution)/shard_map/reduce_scatter | solution.py:135
  100.9 3.9 %collective-permute-start.4 = (f32[5,128,128]{2,1,0:T(8,128)}, f32[5,128,128]{2,1,0:T(8,128)S(1)}, u32[]{:S(2)}, u32[]{:S(2)}) collective-permute-start(f32[5,128,128]{2,1,0:T(8,128)} %bitcast.12), channel_id=1, source_target_pairs={{0,0},{1,7},{2,6},{3,5},{4,4},{5,3},{6,2},{7,1},{8,8},{9,15},{10,1... | collective-permute-start | bytes 983048 | tf_op jit(solution)/shard_map/ppermute | solution.py:106
  104.9 0.9 slice_bitcast_fusion
  105.8 4.6 %collective-permute-start.7 = (f32[128,128]{1,0:T(8,128)S(1)}, f32[128,128]{1,0:T(8,128)S(1)}, u32[]{:S(2)}, u32[]{:S(2)}) collective-permute-start(f32[128,128]{1,0:T(8,128)S(1)} %get-tuple-element.5), channel_id=1, source_target_pairs={{0,24},{1,25},{2,26},{3,27},{4,28},{5,29},{6,30},{7,31},{8,32},{9,... | collective-permute-start | bytes 196616 | tf_op jit(solution)/shard_map/ppermute | solution.py:106
  110.4 4.3 %collective-permute-start.6 = (f32[128,128]{1,0:T(8,128)S(1)}, f32[128,128]{1,0:T(8,128)S(1)}, u32[]{:S(2)}, u32[]{:S(2)}) collective-permute-start(f32[128,128]{1,0:T(8,128)S(1)} %get-tuple-element.6), channel_id=1, source_target_pairs={{0,48},{1,49},{2,50},{3,51},{4,52},{5,53},{6,54},{7,55},{8,56},{9,... | collective-permute-start | bytes 196616 | tf_op jit(solution)/shard_map/ppermute | solution.py:106
  114.7 1.9 %collective-permute-start.5 = (f32[128,128]{1,0:T(8,128)S(1)}, f32[128,128]{1,0:T(8,128)S(1)}, u32[]{:S(2)}, u32[]{:S(2)}) collective-permute-start(f32[128,128]{1,0:T(8,128)S(1)} %get-tuple-element.7), channel_id=1, source_target_pairs={{0,56},{1,57},{2,58},{3,59},{4,60},{5,61},{6,62},{7,63},{8,0},{9,1... | collective-permute-start | bytes 196616 | tf_op jit(solution)/shard_map/ppermute | solution.py:106
  116.6 0.0 collective-permute-done.7.refs_2_
  116.6 2.3 %collective-permute-done.6.refs_1_ = f32[128,128]{1,0:T(8,128)S(1)} collective-permute-done((f32[128,128]{1,0:T(8,128)S(1)}, f32[128,128]{1,0:T(8,128)S(1)}, u32[]{:S(2)}, u32[]{:S(2)}) %collective-permute-start.6) | collective-permute-done | bytes 65568 | tf_op jit(solution)/shard_map/ppermute | solution.py:106
  118.9 3.1 %collective-permute-done.5.refs_0_ = f32[128,128]{1,0:T(8,128)S(1)} collective-permute-done((f32[128,128]{1,0:T(8,128)S(1)}, f32[128,128]{1,0:T(8,128)S(1)}, u32[]{:S(2)}, u32[]{:S(2)}) %collective-permute-start.5) | collective-permute-done | bytes 65568 | tf_op jit(solution)/shard_map/ppermute | solution.py:106
  122.0 0.0 collective-permute-done.4.mirrored
  122.0 0.0 copy-done
  122.1 0.0 copy-done.1
  122.1 1.6 %shard_map.48 = f32[8,128,128]{2,1,0:T(8,128)} custom-call(s32[8]{0:T(128)S(1)} %bitcast.11, f32[5,128,128]{2,1,0:T(8,128)S(1)} %collective-permute-done.4.mirrored, f32[128,128]{1,0:T(8,128)S(1)} %collective-permute-done.5.refs_0_, f32[128,128]{1,0:T(8,128)S(1)} %collective-permute-done.6.refs_1_, f32[128,128]{1,0:T(8,128)S(1)} %collective-permute-done.7.refs_2_, ...), custom_call_target="tpu_custom_call" | custom-call | tf_op jit(solution)/shard_map/pallas_call | solution.py:138
Async XLA Ops:
  6.5 37.0 %all-gather.2.cloned.1.call-start = ((), (), s32[]{:S(2)}) async-start(), calls=%async_computation.1 | async-start | bytes 2359296 | tf_op jit(solution)/shard_map/all_gather | solution.py:115
  8.2 92.7 %reduce-scatter.2.cloned.1.call-start = ((), (), s32[]{:S(2)}) async-start(), calls=%async_computation.2 | async-start | bytes 2949120 | tf_op jit(solution)/shard_map/reduce_scatter | solution.py:135
  8.3 20.5 %collective-permute-start.3 = (bf16[128,1024]{1,0:T(8,128)(2,1)}, bf16[128,1024]{1,0:T(8,128)(2,1)S(1)}, u32[]{:S(2)}, u32[]{:S(2)}) collective-permute-start(bf16[128,1024]{1,0:T(8,128)(2,1)} %shard_map.46), channel_id=1, source_target_pairs={{0,32},{1,33},{2,34},{3,35},{4,36},{5,37},{6,38},{7,39},{8,40},{9,... | collective-permute-start | bytes 786440 | tf_op jit(solution)/shard_map/ppermute | solution.py:106
  13.3 30.2 %collective-permute-start.2 = (bf16[128,1024]{1,0:T(8,128)(2,1)}, bf16[128,1024]{1,0:T(8,128)(2,1)S(1)}, u32[]{:S(2)}, u32[]{:S(2)}) collective-permute-start(bf16[128,1024]{1,0:T(8,128)(2,1)} %shard_map.46), channel_id=1, source_target_pairs={{0,40},{1,41},{2,42},{3,43},{4,44},{5,45},{6,46},{7,47},{8,48},{9,... | collective-permute-start | bytes 786440 | tf_op jit(solution)/shard_map/ppermute | solution.py:106
  18.2 25.4 %collective-permute-start.1 = (bf16[128,1024]{1,0:T(8,128)(2,1)}, bf16[128,1024]{1,0:T(8,128)(2,1)S(1)}, u32[]{:S(2)}, u32[]{:S(2)}) collective-permute-start(bf16[128,1024]{1,0:T(8,128)(2,1)} %shard_map.46), channel_id=1, source_target_pairs={{0,16},{1,17},{2,18},{3,19},{4,20},{5,21},{6,22},{7,23},{8,24},{9,... | collective-permute-start | bytes 786440 | tf_op jit(solution)/shard_map/ppermute | solution.py:106
  22.1 21.5 %collective-permute-start = (bf16[128,1024]{1,0:T(8,128)(2,1)}, bf16[128,1024]{1,0:T(8,128)(2,1)S(1)}, u32[]{:S(2)}, u32[]{:S(2)}) collective-permute-start(bf16[128,1024]{1,0:T(8,128)(2,1)} %shard_map.46), channel_id=1, source_target_pairs={{0,8},{1,9},{2,10},{3,11},{4,12},{5,13},{6,14},{7,15},{8,16},{9,17... | collective-permute-start | bytes 786440 | tf_op jit(solution)/shard_map/ppermute | solution.py:106
  48.5 73.5 %copy-start = (f32[1,1,8,128,128]{4,3,2,1,0:T(8,128)S(1)}, f32[1,1,8,128,128]{4,3,2,1,0:T(8,128)}, u32[]{:S(2)}) copy-start(f32[1,1,8,128,128]{4,3,2,1,0:T(8,128)} %param.6) | copy-start | bytes 1572868
  48.5 73.5 %copy-start.1 = (s32[1,1,8]{2,1,0:T(1,128)S(1)}, s32[1,1,8]{2,1,0:T(1,128)}, u32[]{:S(2)}) copy-start(s32[1,1,8]{2,1,0:T(1,128)} %param.7) | copy-start | bytes 100
  100.9 21.1 %collective-permute-start.4 = (f32[5,128,128]{2,1,0:T(8,128)}, f32[5,128,128]{2,1,0:T(8,128)S(1)}, u32[]{:S(2)}, u32[]{:S(2)}) collective-permute-start(f32[5,128,128]{2,1,0:T(8,128)} %bitcast.12), channel_id=1, source_target_pairs={{0,0},{1,7},{2,6},{3,5},{4,4},{5,3},{6,2},{7,1},{8,8},{9,15},{10,1... | collective-permute-start | bytes 983048 | tf_op jit(solution)/shard_map/ppermute | solution.py:106
  105.8 10.8 %collective-permute-start.7 = (f32[128,128]{1,0:T(8,128)S(1)}, f32[128,128]{1,0:T(8,128)S(1)}, u32[]{:S(2)}, u32[]{:S(2)}) collective-permute-start(f32[128,128]{1,0:T(8,128)S(1)} %get-tuple-element.5), channel_id=1, source_target_pairs={{0,24},{1,25},{2,26},{3,27},{4,28},{5,29},{6,30},{7,31},{8,32},{9,... | collective-permute-start | bytes 196616 | tf_op jit(solution)/shard_map/ppermute | solution.py:106
  110.4 8.5 %collective-permute-start.6 = (f32[128,128]{1,0:T(8,128)S(1)}, f32[128,128]{1,0:T(8,128)S(1)}, u32[]{:S(2)}, u32[]{:S(2)}) collective-permute-start(f32[128,128]{1,0:T(8,128)S(1)} %get-tuple-element.6), channel_id=1, source_target_pairs={{0,48},{1,49},{2,50},{3,51},{4,52},{5,53},{6,54},{7,55},{8,56},{9,... | collective-permute-start | bytes 196616 | tf_op jit(solution)/shard_map/ppermute | solution.py:106
  114.7 7.4 %collective-permute-start.5 = (f32[128,128]{1,0:T(8,128)S(1)}, f32[128,128]{1,0:T(8,128)S(1)}, u32[]{:S(2)}, u32[]{:S(2)}) collective-permute-start(f32[128,128]{1,0:T(8,128)S(1)} %get-tuple-element.7), channel_id=1, source_target_pairs={{0,56},{1,57},{2,58},{3,59},{4,60},{5,61},{6,62},{7,63},{8,0},{9,1... | collective-permute-start | bytes 196616 | tf_op jit(solution)/shard_map/ppermute | solution.py:106
Sparse Core Ops, SparseCore 0:
  9.5 33.5 all-gather.1
  48.7 52.2 reduce-scatter.1

commit v9 on v8

--- a/solution.py
+++ b/solution.py
@@ -11,8 +11,10 @@
 LASSO = 0.1
 RIDGE = 0.5
 AXES = ("z", "y", "k")
-OFFSETS = (0, 7, 6, 3, 4)
-TURNED = (1, 2, 3)
+EARLY = (0, 7, 6, 4)
+TURNED = (1, 2)
+LATE = 3
+SENT = (7, 6, 3, 4)
 CHUNKS = 2
 MIB = 2**20
 
@@ -23,9 +25,8 @@
     out_ref[:, half:] = b_ref[...]
 
 
-def products(n, tile, depth, rows_ref, *refs):
-    count = len(OFFSETS)
-    columns, (out_ref, rows, picked, made, own_sems, row_sems, out_sems) = refs[:count - 1], refs[count - 1:]
+def products(n, tile, depth, count, offset, rows_ref, *refs):
+    columns, (out_ref, rows, picked, made, own_sems, row_sems, out_sems) = refs[:count - offset], refs[count - offset:]
     k = lax.axis_index("k")
     per = n // CHUNKS
     chunks = [
@@ -38,11 +39,11 @@
             picked.at[pl.ds(0, tile), pl.ds(h * depth, depth)],
             own_sems.at[h],
         )
-        for h in range(2)
+        for h in range(2 * offset)
     ]
     for copy in here + chunks:
         copy.start()
-    for i, ref in enumerate(columns, 1):
+    for i, ref in enumerate(columns, offset):
         picked[i * tile:(i + 1) * tile, :depth] = ref[:, depth:]
         picked[i * tile:(i + 1) * tile, depth:] = ref[:, :depth]
     for copy in here:
@@ -64,7 +65,11 @@
         copy.wait()
 
 
-def finish(n, tile, scale, active_ref, mirrored, *refs):
+def added(parts_ref, out_ref):
+    out_ref[...] = jnp.sum(parts_ref[:, 0], axis=0)
+
+
+def finish(n, tile, scale, active_ref, mirrored, late, *refs):
     arrived, (precision_ref, out_ref) = refs[:-2], refs[-2:]
     z, y, k = (lax.axis_index(a) for a in AXES)
     row = lax.broadcasted_iota(jnp.int32, (tile, tile), 0)
@@ -87,16 +92,16 @@
             shrunk = jnp.where(on_diag, stepped, shrunk)
         out_ref[t] = shrunk * active_ref[t].astype(jnp.float32)
 
-    for i, d in enumerate(OFFSETS):
+    put(LATE, late[...])
+    for i, d in enumerate(EARLY):
         put(d, mirrored[i])
-    for i, ref in zip(TURNED, arrived):
-        put(n - OFFSETS[i], ref[...].T)
+    for d, ref in zip((LATE,) + tuple(EARLY[i] for i in TURNED), arrived):
+        put(n - d, ref[...].T)
 
 
 def local(n, resid, samples, precision, active):
     tile, depth = resid.shape
     vmem, smem, far = (pl.BlockSpec(memory_space=s) for s in (pltpu.VMEM, pltpu.SMEM, pltpu.HBM))
-    count = len(OFFSETS)
 
     def moved(a, to):
         def index(z, y, k):
@@ -113,35 +118,51 @@
         compiler_params=pltpu.CompilerParams(vmem_limit_bytes=60 * MIB),
     )(resid, samples)
     rows = lax.all_gather(own, "k", axis=0, tiled=True)
-    columns = [moved(own, lambda z, y, k, d=d: (z, y - d, k)) for d in OFFSETS[1:]]
-    partial = pl.pallas_call(
-        functools.partial(products, n, tile, depth),
-        out_shape=jax.ShapeDtypeStruct((n, count, tile, tile), jnp.float32),
-        in_specs=[far] + [vmem] * (count - 1),
-        out_specs=far,
-        scratch_shapes=[
-            pltpu.VMEM((CHUNKS, n // CHUNKS * tile, 2 * depth), jnp.bfloat16),
-            pltpu.VMEM((count * tile, 2 * depth), jnp.bfloat16),
-            pltpu.VMEM((n, count, tile, tile), jnp.float32),
-            pltpu.SemaphoreType.DMA((2,)),
-            pltpu.SemaphoreType.DMA((CHUNKS,)),
-            pltpu.SemaphoreType.DMA((n,)),
-        ],
-        compiler_params=pltpu.CompilerParams(vmem_limit_bytes=52 * MIB),
-        cost_estimate=pl.CostEstimate(
-            flops=4 * n * count * tile * tile * depth, bytes_accessed=6 * MIB, transcendentals=0
-        ),
-    )(rows, *columns)
-    summed = lax.psum_scatter(partial, "z", scatter_dimension=0, tiled=True)[0]
-    mirrored = moved(summed, lambda z, y, k: (z, y, z - k))
-    arrived = [moved(summed[i], lambda z, y, k, d=OFFSETS[i]: (z, y + d, k)) for i in TURNED]
+    panel = {d: moved(own, lambda z, y, k, d=d: (z, y - d, k)) for d in SENT}
+
+    def multiplied(columns, offset, flops):
+        count = len(columns) + offset
+        return pl.pallas_call(
+            functools.partial(products, n, tile, depth, count, offset),
+            out_shape=jax.ShapeDtypeStruct((n, count, tile, tile), jnp.float32),
+            in_specs=[far] + [vmem] * len(columns),
+            out_specs=far,
+            scratch_shapes=[
+                pltpu.VMEM((CHUNKS, n // CHUNKS * tile, 2 * depth), jnp.bfloat16),
+                pltpu.VMEM((count * tile, 2 * depth), jnp.bfloat16),
+                pltpu.VMEM((n, count, tile, tile), jnp.float32),
+                pltpu.SemaphoreType.DMA((2,)),
+                pltpu.SemaphoreType.DMA((CHUNKS,)),
+                pltpu.SemaphoreType.DMA((n,)),
+            ],
+            compiler_params=pltpu.CompilerParams(vmem_limit_bytes=52 * MIB),
+            cost_estimate=pl.CostEstimate(flops=flops, bytes_accessed=6 * MIB, transcendentals=0),
+        )(rows, *columns)
+
+    once = 4 * n * tile * tile * depth
+    early = lax.psum_scatter(
+        multiplied([panel[d] for d in EARLY[1:]], 1, once), "z", scatter_dimension=0, tiled=True
+    )[0]
+    weight = 600 * once
+    parts = lax.all_to_all(multiplied([panel[LATE]], 0, weight), "z", 0, 0, tiled=True)
+    late = pl.pallas_call(
+        added,
+        out_shape=jax.ShapeDtypeStruct((tile, tile), jnp.float32),
+        in_specs=[vmem],
+        out_specs=vmem,
+        compiler_params=pltpu.CompilerParams(vmem_limit_bytes=16 * MIB),
+    )(parts)
+    arrived = [moved(late, lambda z, y, k: (z, y + LATE, k))]
+    late = moved(late, lambda z, y, k: (z, y, z - k))
+    mirrored = moved(early, lambda z, y, k: (z, y, z - k))
+    arrived += [moved(early[i], lambda z, y, k, d=EARLY[i]: (z, y + d, k)) for i in TURNED]
     updated = pl.pallas_call(
         functools.partial(finish, n, tile, 0.5 / (depth * n)),
         out_shape=jax.ShapeDtypeStruct((n, tile, tile), jnp.float32),
-        in_specs=[smem] + [vmem] * (2 + len(TURNED)),
+        in_specs=[smem] + [vmem] * (3 + len(arrived)),
         out_specs=vmem,
         compiler_params=pltpu.CompilerParams(vmem_limit_bytes=16 * MIB),
-    )(active.reshape(n), mirrored, *arrived, precision.reshape(n, tile, tile))
+    )(active.reshape(n), mirrored, late, *arrived, precision.reshape(n, tile, tile))
     return updated.reshape(precision.shape)
 
 

time: 131 us -> 126 us (0.962)
  waiting for transfers between devices: 76.8 us -> 36.5 us
  blocking collectives: 0 us -> 31.2 us
  starting transfers between devices: 31.1 us -> 33.4 us
  Pallas kernels: 8.16 us -> 10.4 us
    reduce_scatter x1, waiting for transfers between devices: 52.4 us -> 12.1 us  [local(): lax.psum_scatter(multiplied([panel[d] for d in EARLY[1:]], 1, once), 'z',...]
    all_to_all x0 -> x1, blocking collectives: none -> 31.2 us  [local(): lax.all_to_all(multiplied([panel[LATE]], 0, weight), 'z', 0, 0, tiled=True)]
    ppermute x8 -> x9, starting transfers between devices: 31.1 us -> 33.4 us  [moved(): return lax.ppermute(a, AXES, [(index(*i), index(*to(*i))) for i in ids])]
    pallas_call x1 -> x3, Pallas kernels: 4.9 us -> 7.15 us  [the longest x2 7.12 us: multiplied(): pl.pallas_call(functools.partial(products, n, tile, depth, count, offset)...]
    ppermute x8 -> x9, waiting for transfers between devices: 24.3 us -> 24.4 us  [moved(): return lax.ppermute(a, AXES, [(index(*i), index(*to(*i))) for i in ids])]
  transfers between devices with their start and end apart: 10 -> 11, of which waited for: 5 -> 6; matrix products, arithmetic and copies ran while one was open for 1% -> 1% of each run, Pallas kernels for 0% -> 6%
where the time goes in v9:
time: 126 us
  waiting for transfers between devices  36.5 us (29%)
  starting transfers between devices  33.4 us (27%)
  blocking collectives  31.2 us (25%)
  between operations  13.5 us (11%)
  Pallas kernels  10.4 us (8%)
    ppermute x9, starting transfers between devices, moved(): return lax.ppermute(a, AXES, [(index(*i), index(*to(*i))) for i in ids])  33.4 us
    all_to_all x1, blocking collectives, local(): lax.all_to_all(multiplied([panel[LATE]], 0, weight), 'z', 0, 0, tiled=True)  31.2 us
    ppermute x9, waiting for transfers between devices, moved(): return lax.ppermute(a, AXES, [(index(*i), index(*to(*i))) for i in ids])  24.4 us
    reduce_scatter x1, waiting for transfers between devices, local(): lax.psum_scatter(multiplied([panel[d] for d in EARLY[1:]], 1, once), 'z',...  12.1 us
    pallas_call x2, Pallas kernels, multiplied(): pl.pallas_call(functools.partial(products, n, tile, depth, count, offset)...  7.12 us
  transfers between devices with their start and end apart: 11, of which 6 were waited for; matrix products, arithmetic and copies ran while one was open for 1% of the time, Pallas kernels for 6%

profile of v9, /device:TPU:26, one launch (start us, length us, event | category | flops | bytes accessed | tf_op | source)
XLA Modules:
  0.0 126.0 jit_solution(7592858081307394077)
XLA Ops:
  6.5 0.0 all-gather.2.cloned.1.call-start
  6.5 1.7 %shard_map.46 = bf16[128,1024]{1,0:T(8,128)(2,1)} custom-call(bf16[128,512]{1,0:T(8,128)(2,1)} %a_ref.1, bf16[128,512]{1,0:T(8,128)(2,1)} %b_ref.1), custom_call_target="tpu_custom_call" | custom-call | tf_op jit(solution)/shard_map/pallas_call | solution.py:113
  8.2 0.0 all-gather.2.cloned.1.call-update
  8.2 0.0 reduce-scatter.2.cloned.1.call-start
  8.3 5.0 %collective-permute-start.2 = (bf16[128,1024]{1,0:T(8,128)(2,1)}, bf16[128,1024]{1,0:T(8,128)(2,1)S(1)}, u32[]{:S(2)}, u32[]{:S(2)}) collective-permute-start(bf16[128,1024]{1,0:T(8,128)(2,1)} %shard_map.46), channel_id=1, source_target_pairs={{0,32},{1,33},{2,34},{3,35},{4,36},{5,37},{6,38},{7,39},{8,40},{9,... | collective-permute-start | bytes 786440 | tf_op jit(solution)/shard_map/ppermute | solution.py:111
  13.3 2.7 %collective-permute-start.1 = (bf16[128,1024]{1,0:T(8,128)(2,1)}, bf16[128,1024]{1,0:T(8,128)(2,1)S(1)}, u32[]{:S(2)}, u32[]{:S(2)}) collective-permute-start(bf16[128,1024]{1,0:T(8,128)(2,1)} %shard_map.46), channel_id=1, source_target_pairs={{0,16},{1,17},{2,18},{3,19},{4,20},{5,21},{6,22},{7,23},{8,24},{9,... | collective-permute-start | bytes 786440 | tf_op jit(solution)/shard_map/ppermute | solution.py:111
  16.0 3.5 %collective-permute-start = (bf16[128,1024]{1,0:T(8,128)(2,1)}, bf16[128,1024]{1,0:T(8,128)(2,1)S(1)}, u32[]{:S(2)}, u32[]{:S(2)}) collective-permute-start(bf16[128,1024]{1,0:T(8,128)(2,1)} %shard_map.46), channel_id=1, source_target_pairs={{0,8},{1,9},{2,10},{3,11},{4,12},{5,13},{6,14},{7,15},{8,16},{9,17... | collective-permute-start | bytes 786440 | tf_op jit(solution)/shard_map/ppermute | solution.py:111
  19.5 3.9 %collective-permute-start.4 = (bf16[128,1024]{1,0:T(8,128)(2,1)}, bf16[128,1024]{1,0:T(8,128)(2,1)S(1)}, u32[]{:S(2)}, u32[]{:S(2)}) collective-permute-start(bf16[128,1024]{1,0:T(8,128)(2,1)} %shard_map.46), channel_id=1, source_target_pairs={{0,40},{1,41},{2,42},{3,43},{4,44},{5,45},{6,46},{7,47},{8,48},{9,... | collective-permute-start | bytes 786440 | tf_op jit(solution)/shard_map/ppermute | solution.py:111
  23.5 4.2 %collective-permute-done.2.refs_2_ = bf16[128,1024]{1,0:T(8,128)(2,1)S(1)} collective-permute-done((bf16[128,1024]{1,0:T(8,128)(2,1)}, bf16[128,1024]{1,0:T(8,128)(2,1)S(1)}, u32[]{:S(2)}, u32[]{:S(2)}) %collective-permute-start.2) | collective-permute-done | bytes 262176 | tf_op jit(solution)/shard_map/ppermute | solution.py:111
  27.6 11.2 %collective-permute-done.1.refs_1_ = bf16[128,1024]{1,0:T(8,128)(2,1)S(1)} collective-permute-done((bf16[128,1024]{1,0:T(8,128)(2,1)}, bf16[128,1024]{1,0:T(8,128)(2,1)S(1)}, u32[]{:S(2)}, u32[]{:S(2)}) %collective-permute-start.1) | collective-permute-done | bytes 262176 | tf_op jit(solution)/shard_map/ppermute | solution.py:111
  38.8 4.6 %collective-permute-done.refs_0_ = bf16[128,1024]{1,0:T(8,128)(2,1)S(1)} collective-permute-done((bf16[128,1024]{1,0:T(8,128)(2,1)}, bf16[128,1024]{1,0:T(8,128)(2,1)S(1)}, u32[]{:S(2)}, u32[]{:S(2)}) %collective-permute-start) | collective-permute-done | bytes 262176 | tf_op jit(solution)/shard_map/ppermute | solution.py:111
  43.4 3.7 %shard_map.47 = f32[8,4,128,128]{3,2,1,0:T(8,128)} custom-call(bf16[1024,1024]{1,0:T(8,128)(2,1)} %all-gather.2.cloned.1.call-done.rows_ref, bf16[128,1024]{1,0:T(8,128)(2,1)S(1)} %collective-permute-done.refs_0_, bf16[128,1024]{1,0:T(8,128)(2,1)S(1)} %collective-permute-done.1.refs_1_, bf16[128,1024]{1,0:T(8,128)(2,1)S(1)} %collective-permute-done.2.refs_2_), custom_call_target="tpu_custom_call" | custom-call | flops 268435456 | bytes 6291456 | tf_op jit(solution)/shard_map/pallas_call | solution.py:125
  47.1 0.0 reduce-scatter.2.cloned.1.call-update
  47.1 0.0 collective-permute-done.4.refs_0_
  47.2 0.0 copy-start.1
  47.2 3.4 %shard_map.48 = f32[8,1,128,128]{3,2,1,0:T(8,128)S(1)} custom-call(bf16[1024,1024]{1,0:T(8,128)(2,1)} %all-gather.2.cloned.1.call-done.rows_ref, bf16[128,1024]{1,0:T(8,128)(2,1)S(1)} %collective-permute-done.4.refs_0_), custom_call_target="tpu_custom_call" | custom-call | flops 161061273600 | bytes 6291456 | tf_op jit(solution)/shard_map/pallas_call | solution.py:125
  50.6 0.0 copy-start
  50.6 31.2 %all_to_all.5.parts_ref = f32[8,1,128,128]{3,2,1,0:T(8,128)S(1)} all-to-all(f32[8,1,128,128]{3,2,1,0:T(8,128)S(1)} %shard_map.48), channel_id=1, replica_groups=mesh['z'=8,'y'=8,'k'=8] {'z'}, dimensions={0} | all-to-all | bytes 1048576 | tf_op jit(solution)/shard_map/all_to_all | solution.py:147
  81.8 2.8 %collective-permute-start.6 = (f32[128,128]{1,0:T(8,128)S(1)}, f32[128,128]{1,0:T(8,128)S(1)}, u32[]{:S(2)}, u32[]{:S(2)}) collective-permute-start(f32[128,128]{1,0:T(8,128)S(1)} %shard_map.49), channel_id=1, source_target_pairs={{0,24},{1,25},{2,26},{3,27},{4,28},{5,29},{6,30},{7,31},{8,32},{9,... | collective-permute-start | bytes 196616 | tf_op jit(solution)/shard_map/ppermute | solution.py:111
  84.6 4.1 %collective-permute-start.5 = (f32[128,128]{1,0:T(8,128)S(1)}, f32[128,128]{1,0:T(8,128)S(1)}, u32[]{:S(2)}, u32[]{:S(2)}) collective-permute-start(f32[128,128]{1,0:T(8,128)S(1)} %shard_map.49), channel_id=1, source_target_pairs={{0,0},{1,7},{2,6},{3,5},{4,4},{5,3},{6,2},{7,1},{8,8},{9,15},{10,1... | collective-permute-start | bytes 196616 | tf_op jit(solution)/shard_map/ppermute | solution.py:111
  88.7 12.1 %reduce-scatter.2.cloned.1.call-done = f32[1,4,128,128]{3,2,1,0:T(8,128)} async-done(((f32[8,4,128,128]{3,2,1,0:T(8,128)}), f32[1,4,128,128]{3,2,1,0:T(8,128)}) %reduce-scatter.2.cloned.1.call-update) | async-done | bytes 262160 | tf_op jit(solution)/shard_map/reduce_scatter | solution.py:143
  100.8 4.1 %collective-permute-start.3 = (f32[4,128,128]{2,1,0:T(8,128)}, f32[4,128,128]{2,1,0:T(8,128)S(1)}, u32[]{:S(2)}, u32[]{:S(2)}) collective-permute-start(f32[4,128,128]{2,1,0:T(8,128)} %bitcast.10), channel_id=1, source_target_pairs={{0,0},{1,7},{2,6},{3,5},{4,4},{5,3},{6,2},{7,1},{8,8},{9,15},{10,1... | collective-permute-start | bytes 786440 | tf_op jit(solution)/shard_map/ppermute | solution.py:111
  104.9 0.9 slice_bitcast_fusion
  105.8 4.0 %collective-permute-start.8 = (f32[128,128]{1,0:T(8,128)S(1)}, f32[128,128]{1,0:T(8,128)S(1)}, u32[]{:S(2)}, u32[]{:S(2)}) collective-permute-start(f32[128,128]{1,0:T(8,128)S(1)} %get-tuple-element.5), channel_id=1, source_target_pairs={{0,48},{1,49},{2,50},{3,51},{4,52},{5,53},{6,54},{7,55},{8,56},{9,... | collective-permute-start | bytes 196616 | tf_op jit(solution)/shard_map/ppermute | solution.py:111
  109.8 3.3 %collective-permute-start.7 = (f32[128,128]{1,0:T(8,128)S(1)}, f32[128,128]{1,0:T(8,128)S(1)}, u32[]{:S(2)}, u32[]{:S(2)}) collective-permute-start(f32[128,128]{1,0:T(8,128)S(1)} %get-tuple-element.6), channel_id=1, source_target_pairs={{0,56},{1,57},{2,58},{3,59},{4,60},{5,61},{6,62},{7,63},{8,0},{9,1... | collective-permute-start | bytes 196616 | tf_op jit(solution)/shard_map/ppermute | solution.py:111
  113.1 0.0 collective-permute-done.6.refs_0_
  113.1 0.0 collective-permute-done.5.late
  113.1 1.0 collective-permute-done.8.refs_2_
  114.1 3.5 %collective-permute-done.7.refs_1_ = f32[128,128]{1,0:T(8,128)S(1)} collective-permute-done((f32[128,128]{1,0:T(8,128)S(1)}, f32[128,128]{1,0:T(8,128)S(1)}, u32[]{:S(2)}, u32[]{:S(2)}) %collective-permute-start.7) | collective-permute-done | bytes 65568 | tf_op jit(solution)/shard_map/ppermute | solution.py:111
  117.6 0.0 collective-permute-done.3.mirrored
  117.6 0.0 copy-done.1
  117.6 1.6 %shard_map.50 = f32[8,128,128]{2,1,0:T(8,128)} custom-call(s32[8]{0:T(128)S(1)} %bitcast.9, f32[4,128,128]{2,1,0:T(8,128)S(1)} %collective-permute-done.3.mirrored, f32[128,128]{1,0:T(8,128)S(1)} %collective-permute-done.5.late, f32[128,128]{1,0:T(8,128)S(1)} %collective-permute-done.6.refs_0_, f32[128,128]{1,0:T(8,128)S(1)} %collective-permute-done.7.refs_1_, ...), custom_call_target="tpu_custom_call" | custom-call | tf_op jit(solution)/shard_map/pallas_call | solution.py:159
  (3 shorter events, 0.0 us)
Async XLA Ops:
  6.5 36.9 %all-gather.2.cloned.1.call-start = ((), (), s32[]{:S(2)}) async-start(), calls=%async_computation.2 | async-start | bytes 2359296 | tf_op jit(solution)/shard_map/all_gather | solution.py:120
  8.2 92.5 %reduce-scatter.2.cloned.1.call-start = ((), (), s32[]{:S(2)}) async-start(), calls=%async_computation.3 | async-start | bytes 2359296 | tf_op jit(solution)/shard_map/reduce_scatter | solution.py:143
  8.3 19.3 %collective-permute-start.2 = (bf16[128,1024]{1,0:T(8,128)(2,1)}, bf16[128,1024]{1,0:T(8,128)(2,1)S(1)}, u32[]{:S(2)}, u32[]{:S(2)}) collective-permute-start(bf16[128,1024]{1,0:T(8,128)(2,1)} %shard_map.46), channel_id=1, source_target_pairs={{0,32},{1,33},{2,34},{3,35},{4,36},{5,37},{6,38},{7,39},{8,40},{9,... | collective-permute-start | bytes 786440 | tf_op jit(solution)/shard_map/ppermute | solution.py:111
  13.3 25.5 %collective-permute-start.1 = (bf16[128,1024]{1,0:T(8,128)(2,1)}, bf16[128,1024]{1,0:T(8,128)(2,1)S(1)}, u32[]{:S(2)}, u32[]{:S(2)}) collective-permute-start(bf16[128,1024]{1,0:T(8,128)(2,1)} %shard_map.46), channel_id=1, source_target_pairs={{0,16},{1,17},{2,18},{3,19},{4,20},{5,21},{6,22},{7,23},{8,24},{9,... | collective-permute-start | bytes 786440 | tf_op jit(solution)/shard_map/ppermute | solution.py:111
  16.0 27.4 %collective-permute-start = (bf16[128,1024]{1,0:T(8,128)(2,1)}, bf16[128,1024]{1,0:T(8,128)(2,1)S(1)}, u32[]{:S(2)}, u32[]{:S(2)}) collective-permute-start(bf16[128,1024]{1,0:T(8,128)(2,1)} %shard_map.46), channel_id=1, source_target_pairs={{0,8},{1,9},{2,10},{3,11},{4,12},{5,13},{6,14},{7,15},{8,16},{9,17... | collective-permute-start | bytes 786440 | tf_op jit(solution)/shard_map/ppermute | solution.py:111
  19.5 27.6 %collective-permute-start.4 = (bf16[128,1024]{1,0:T(8,128)(2,1)}, bf16[128,1024]{1,0:T(8,128)(2,1)S(1)}, u32[]{:S(2)}, u32[]{:S(2)}) collective-permute-start(bf16[128,1024]{1,0:T(8,128)(2,1)} %shard_map.46), channel_id=1, source_target_pairs={{0,40},{1,41},{2,42},{3,43},{4,44},{5,45},{6,46},{7,47},{8,48},{9,... | collective-permute-start | bytes 786440 | tf_op jit(solution)/shard_map/ppermute | solution.py:111
  47.2 70.4 %copy-start.1 = (s32[1,1,8]{2,1,0:T(1,128)S(1)}, s32[1,1,8]{2,1,0:T(1,128)}, u32[]{:S(2)}) copy-start(s32[1,1,8]{2,1,0:T(1,128)} %param.7) | copy-start | bytes 100
  50.6 67.0 %copy-start = (f32[1,1,8,128,128]{4,3,2,1,0:T(8,128)S(1)}, f32[1,1,8,128,128]{4,3,2,1,0:T(8,128)}, u32[]{:S(2)}) copy-start(f32[1,1,8,128,128]{4,3,2,1,0:T(8,128)} %param.6) | copy-start | bytes 1572868
  81.8 31.3 %collective-permute-start.6 = (f32[128,128]{1,0:T(8,128)S(1)}, f32[128,128]{1,0:T(8,128)S(1)}, u32[]{:S(2)}, u32[]{:S(2)}) collective-permute-start(f32[128,128]{1,0:T(8,128)S(1)} %shard_map.49), channel_id=1, source_target_pairs={{0,24},{1,25},{2,26},{3,27},{4,28},{5,29},{6,30},{7,31},{8,32},{9,... | collective-permute-start | bytes 196616 | tf_op jit(solution)/shard_map/ppermute | solution.py:111
  84.6 28.5 %collective-permute-start.5 = (f32[128,128]{1,0:T(8,128)S(1)}, f32[128,128]{1,0:T(8,128)S(1)}, u32[]{:S(2)}, u32[]{:S(2)}) collective-permute-start(f32[128,128]{1,0:T(8,128)S(1)} %shard_map.49), channel_id=1, source_target_pairs={{0,0},{1,7},{2,6},{3,5},{4,4},{5,3},{6,2},{7,1},{8,8},{9,15},{10,1... | collective-permute-start | bytes 196616 | tf_op jit(solution)/shard_map/ppermute | solution.py:111
  100.8 16.8 %collective-permute-start.3 = (f32[4,128,128]{2,1,0:T(8,128)}, f32[4,128,128]{2,1,0:T(8,128)S(1)}, u32[]{:S(2)}, u32[]{:S(2)}) collective-permute-start(f32[4,128,128]{2,1,0:T(8,128)} %bitcast.10), channel_id=1, source_target_pairs={{0,0},{1,7},{2,6},{3,5},{4,4},{5,3},{6,2},{7,1},{8,8},{9,15},{10,1... | collective-permute-start | bytes 786440 | tf_op jit(solution)/shard_map/ppermute | solution.py:111
  105.8 8.3 %collective-permute-start.8 = (f32[128,128]{1,0:T(8,128)S(1)}, f32[128,128]{1,0:T(8,128)S(1)}, u32[]{:S(2)}, u32[]{:S(2)}) collective-permute-start(f32[128,128]{1,0:T(8,128)S(1)} %get-tuple-element.5), channel_id=1, source_target_pairs={{0,48},{1,49},{2,50},{3,51},{4,52},{5,53},{6,54},{7,55},{8,56},{9,... | collective-permute-start | bytes 196616 | tf_op jit(solution)/shard_map/ppermute | solution.py:111
  109.8 7.8 %collective-permute-start.7 = (f32[128,128]{1,0:T(8,128)S(1)}, f32[128,128]{1,0:T(8,128)S(1)}, u32[]{:S(2)}, u32[]{:S(2)}) collective-permute-start(f32[128,128]{1,0:T(8,128)S(1)} %get-tuple-element.6), channel_id=1, source_target_pairs={{0,56},{1,57},{2,58},{3,59},{4,60},{5,61},{6,62},{7,63},{8,0},{9,1... | collective-permute-start | bytes 196616 | tf_op jit(solution)/shard_map/ppermute | solution.py:111
Sparse Core Ops, SparseCore 0:
  9.5 33.5 all-gather.1
  47.3 53.4 reduce-scatter.1

commit v10 on v9

--- a/solution.py
+++ b/solution.py
@@ -11,10 +11,10 @@
 LASSO = 0.1
 RIDGE = 0.5
 AXES = ("z", "y", "k")
-EARLY = (0, 7, 6, 4)
+EARLY = (0, 7, 2, 4)
 TURNED = (1, 2)
-LATE = 3
-SENT = (7, 6, 3, 4)
+LATE = 5
+SENT = (7, 2, 5, 4)
 CHUNKS = 2
 MIB = 2**20
 

time: 126 us -> 128 us (1.016)
  the two profiles are of different devices: /device:TPU:26 before, /device:TPU:18 now
where the time goes in v10:
time: 128 us
  waiting for transfers between devices  36.6 us (29%)
  blocking collectives  33.8 us (26%)
  starting transfers between devices  32.4 us (25%)
  between operations  13.5 us (11%)
  Pallas kernels  10.4 us (8%)
    all_to_all x1, blocking collectives, local(): lax.all_to_all(multiplied([panel[LATE]], 0, weight), 'z', 0, 0, tiled=True)  33.8 us
    ppermute x9, starting transfers between devices, moved(): return lax.ppermute(a, AXES, [(index(*i), index(*to(*i))) for i in ids])  32.4 us
    ppermute x9, waiting for transfers between devices, moved(): return lax.ppermute(a, AXES, [(index(*i), index(*to(*i))) for i in ids])  21.3 us
    reduce_scatter x1, waiting for transfers between devices, local(): lax.psum_scatter(multiplied([panel[d] for d in EARLY[1:]], 1, once), 'z',...  10.5 us
    pallas_call x2, Pallas kernels, multiplied(): pl.pallas_call(functools.partial(products, n, tile, depth, count, offset)...  7.13 us
    all_gather x1, waiting for transfers between devices, local(): rows = lax.all_gather(own, 'k', axis=0, tiled=True)  4.84 us
  transfers between devices with their start and end apart: 11, of which 7 were waited for; matrix products, arithmetic and copies ran while one was open for 1% of the time, Pallas kernels for 6%

profile of v10, /device:TPU:18, one launch (start us, length us, event | category | flops | bytes accessed | tf_op | source)
XLA Modules:
  0.0 127.8 jit_solution(16613767934315697654)
XLA Ops:
  6.5 0.0 all-gather.2.cloned.1.call-start
  6.5 1.7 %shard_map.46 = bf16[128,1024]{1,0:T(8,128)(2,1)} custom-call(bf16[128,512]{1,0:T(8,128)(2,1)} %a_ref.1, bf16[128,512]{1,0:T(8,128)(2,1)} %b_ref.1), custom_call_target="tpu_custom_call" | custom-call | tf_op jit(solution)/shard_map/pallas_call | solution.py:113
  8.2 0.0 all-gather.2.cloned.1.call-update
  8.2 0.0 reduce-scatter.2.cloned.1.call-start
  8.3 5.9 %collective-permute-start.2 = (bf16[128,1024]{1,0:T(8,128)(2,1)}, bf16[128,1024]{1,0:T(8,128)(2,1)S(1)}, u32[]{:S(2)}, u32[]{:S(2)}) collective-permute-start(bf16[128,1024]{1,0:T(8,128)(2,1)} %shard_map.46), channel_id=1, source_target_pairs={{0,32},{1,33},{2,34},{3,35},{4,36},{5,37},{6,38},{7,39},{8,40},{9,... | collective-permute-start | bytes 786440 | tf_op jit(solution)/shard_map/ppermute | solution.py:111
  14.2 4.0 %collective-permute-start.1 = (bf16[128,1024]{1,0:T(8,128)(2,1)}, bf16[128,1024]{1,0:T(8,128)(2,1)S(1)}, u32[]{:S(2)}, u32[]{:S(2)}) collective-permute-start(bf16[128,1024]{1,0:T(8,128)(2,1)} %shard_map.46), channel_id=1, source_target_pairs={{0,48},{1,49},{2,50},{3,51},{4,52},{5,53},{6,54},{7,55},{8,56},{9,... | collective-permute-start | bytes 786440 | tf_op jit(solution)/shard_map/ppermute | solution.py:111
  18.3 2.6 %collective-permute-start = (bf16[128,1024]{1,0:T(8,128)(2,1)}, bf16[128,1024]{1,0:T(8,128)(2,1)S(1)}, u32[]{:S(2)}, u32[]{:S(2)}) collective-permute-start(bf16[128,1024]{1,0:T(8,128)(2,1)} %shard_map.46), channel_id=1, source_target_pairs={{0,8},{1,9},{2,10},{3,11},{4,12},{5,13},{6,14},{7,15},{8,16},{9,17... | collective-permute-start | bytes 786440 | tf_op jit(solution)/shard_map/ppermute | solution.py:111
  20.9 3.4 %collective-permute-start.4 = (bf16[128,1024]{1,0:T(8,128)(2,1)}, bf16[128,1024]{1,0:T(8,128)(2,1)S(1)}, u32[]{:S(2)}, u32[]{:S(2)}) collective-permute-start(bf16[128,1024]{1,0:T(8,128)(2,1)} %shard_map.46), channel_id=1, source_target_pairs={{0,24},{1,25},{2,26},{3,27},{4,28},{5,29},{6,30},{7,31},{8,32},{9,... | collective-permute-start | bytes 786440 | tf_op jit(solution)/shard_map/ppermute | solution.py:111
  24.2 3.9 %collective-permute-done.2.refs_2_ = bf16[128,1024]{1,0:T(8,128)(2,1)S(1)} collective-permute-done((bf16[128,1024]{1,0:T(8,128)(2,1)}, bf16[128,1024]{1,0:T(8,128)(2,1)S(1)}, u32[]{:S(2)}, u32[]{:S(2)}) %collective-permute-start.2) | collective-permute-done | bytes 262176 | tf_op jit(solution)/shard_map/ppermute | solution.py:111
  28.2 10.1 %collective-permute-done.1.refs_1_ = bf16[128,1024]{1,0:T(8,128)(2,1)S(1)} collective-permute-done((bf16[128,1024]{1,0:T(8,128)(2,1)}, bf16[128,1024]{1,0:T(8,128)(2,1)S(1)}, u32[]{:S(2)}, u32[]{:S(2)}) %collective-permute-start.1) | collective-permute-done | bytes 262176 | tf_op jit(solution)/shard_map/ppermute | solution.py:111
  38.3 0.1 collective-permute-done.refs_0_
  38.4 4.8 %all-gather.2.cloned.1.call-done.rows_ref = bf16[1024,1024]{1,0:T(8,128)(2,1)} async-done(((bf16[128,1024]{1,0:T(8,128)(2,1)}), bf16[1024,1024]{1,0:T(8,128)(2,1)}) %all-gather.2.cloned.1.call-update) | async-done | bytes 2097168 | tf_op jit(solution)/shard_map/all_gather | solution.py:120
  43.2 3.7 %shard_map.47 = f32[8,4,128,128]{3,2,1,0:T(8,128)} custom-call(bf16[1024,1024]{1,0:T(8,128)(2,1)} %all-gather.2.cloned.1.call-done.rows_ref, bf16[128,1024]{1,0:T(8,128)(2,1)S(1)} %collective-permute-done.refs_0_, bf16[128,1024]{1,0:T(8,128)(2,1)S(1)} %collective-permute-done.1.refs_1_, bf16[128,1024]{1,0:T(8,128)(2,1)S(1)} %collective-permute-done.2.refs_2_), custom_call_target="tpu_custom_call" | custom-call | flops 268435456 | bytes 6291456 | tf_op jit(solution)/shard_map/pallas_call | solution.py:125
  47.0 0.0 reduce-scatter.2.cloned.1.call-update
  47.0 2.9 %collective-permute-done.4.refs_0_ = bf16[128,1024]{1,0:T(8,128)(2,1)S(1)} collective-permute-done((bf16[128,1024]{1,0:T(8,128)(2,1)}, bf16[128,1024]{1,0:T(8,128)(2,1)S(1)}, u32[]{:S(2)}, u32[]{:S(2)}) %collective-permute-start.4) | collective-permute-done | bytes 262176 | tf_op jit(solution)/shard_map/ppermute | solution.py:111
  49.9 3.4 %shard_map.48 = f32[8,1,128,128]{3,2,1,0:T(8,128)S(1)} custom-call(bf16[1024,1024]{1,0:T(8,128)(2,1)} %all-gather.2.cloned.1.call-done.rows_ref, bf16[128,1024]{1,0:T(8,128)(2,1)S(1)} %collective-permute-done.4.refs_0_), custom_call_target="tpu_custom_call" | custom-call | flops 161061273600 | bytes 6291456 | tf_op jit(solution)/shard_map/pallas_call | solution.py:125
  53.3 0.0 copy-start
  53.4 33.8 %all_to_all.5.parts_ref = f32[8,1,128,128]{3,2,1,0:T(8,128)S(1)} all-to-all(f32[8,1,128,128]{3,2,1,0:T(8,128)S(1)} %shard_map.48), channel_id=1, replica_groups=mesh['z'=8,'y'=8,'k'=8] {'z'}, dimensions={0} | all-to-all | bytes 1048576 | tf_op jit(solution)/shard_map/all_to_all | solution.py:147
  87.2 1.9 %collective-permute-start.6 = (f32[128,128]{1,0:T(8,128)S(1)}, f32[128,128]{1,0:T(8,128)S(1)}, u32[]{:S(2)}, u32[]{:S(2)}) collective-permute-start(f32[128,128]{1,0:T(8,128)S(1)} %shard_map.49), channel_id=1, source_target_pairs={{0,40},{1,41},{2,42},{3,43},{4,44},{5,45},{6,46},{7,47},{8,48},{9,... | collective-permute-start | bytes 196616 | tf_op jit(solution)/shard_map/ppermute | solution.py:111
  89.1 4.0 %collective-permute-start.5 = (f32[128,128]{1,0:T(8,128)S(1)}, f32[128,128]{1,0:T(8,128)S(1)}, u32[]{:S(2)}, u32[]{:S(2)}) collective-permute-start(f32[128,128]{1,0:T(8,128)S(1)} %shard_map.49), channel_id=1, source_target_pairs={{0,0},{1,7},{2,6},{3,5},{4,4},{5,3},{6,2},{7,1},{8,8},{9,15},{10,1... | collective-permute-start | bytes 196616 | tf_op jit(solution)/shard_map/ppermute | solution.py:111
  93.2 10.5 %reduce-scatter.2.cloned.1.call-done = f32[1,4,128,128]{3,2,1,0:T(8,128)} async-done(((f32[8,4,128,128]{3,2,1,0:T(8,128)}), f32[1,4,128,128]{3,2,1,0:T(8,128)}) %reduce-scatter.2.cloned.1.call-update) | async-done | bytes 262160 | tf_op jit(solution)/shard_map/reduce_scatter | solution.py:143
  103.7 3.5 %collective-permute-start.3 = (f32[4,128,128]{2,1,0:T(8,128)}, f32[4,128,128]{2,1,0:T(8,128)S(1)}, u32[]{:S(2)}, u32[]{:S(2)}) collective-permute-start(f32[4,128,128]{2,1,0:T(8,128)} %bitcast.10), channel_id=1, source_target_pairs={{0,0},{1,7},{2,6},{3,5},{4,4},{5,3},{6,2},{7,1},{8,8},{9,15},{10,1... | collective-permute-start | bytes 786440 | tf_op jit(solution)/shard_map/ppermute | solution.py:111
  107.2 0.9 slice_bitcast_fusion
  108.1 5.1 %collective-permute-start.8 = (f32[128,128]{1,0:T(8,128)S(1)}, f32[128,128]{1,0:T(8,128)S(1)}, u32[]{:S(2)}, u32[]{:S(2)}) collective-permute-start(f32[128,128]{1,0:T(8,128)S(1)} %get-tuple-element.5), channel_id=1, source_target_pairs={{0,16},{1,17},{2,18},{3,19},{4,20},{5,21},{6,22},{7,23},{8,24},{9,... | collective-permute-start | bytes 196616 | tf_op jit(solution)/shard_map/ppermute | solution.py:111
  113.2 1.9 %collective-permute-start.7 = (f32[128,128]{1,0:T(8,128)S(1)}, f32[128,128]{1,0:T(8,128)S(1)}, u32[]{:S(2)}, u32[]{:S(2)}) collective-permute-start(f32[128,128]{1,0:T(8,128)S(1)} %get-tuple-element.6), channel_id=1, source_target_pairs={{0,56},{1,57},{2,58},{3,59},{4,60},{5,61},{6,62},{7,63},{8,0},{9,1... | collective-permute-start | bytes 196616 | tf_op jit(solution)/shard_map/ppermute | solution.py:111
  115.1 0.0 collective-permute-done.6.refs_0_
  115.1 0.0 collective-permute-done.5.late
  115.1 0.0 collective-permute-done.8.refs_2_
  115.1 4.2 %collective-permute-done.7.refs_1_ = f32[128,128]{1,0:T(8,128)S(1)} collective-permute-done((f32[128,128]{1,0:T(8,128)S(1)}, f32[128,128]{1,0:T(8,128)S(1)}, u32[]{:S(2)}, u32[]{:S(2)}) %collective-permute-start.7) | collective-permute-done | bytes 65568 | tf_op jit(solution)/shard_map/ppermute | solution.py:111
  119.3 0.0 collective-permute-done.3.mirrored
  119.3 0.0 copy-done.1
  119.3 1.6 %shard_map.50 = f32[8,128,128]{2,1,0:T(8,128)} custom-call(s32[8]{0:T(128)S(1)} %bitcast.9, f32[4,128,128]{2,1,0:T(8,128)S(1)} %collective-permute-done.3.mirrored, f32[128,128]{1,0:T(8,128)S(1)} %collective-permute-done.5.late, f32[128,128]{1,0:T(8,128)S(1)} %collective-permute-done.6.refs_0_, f32[128,128]{1,0:T(8,128)S(1)} %collective-permute-done.7.refs_1_, ...), custom_call_target="tpu_custom_call" | custom-call | tf_op jit(solution)/shard_map/pallas_call | solution.py:159
  (3 shorter events, 0.0 us)
Async XLA Ops:
  6.5 36.7 %all-gather.2.cloned.1.call-start = ((), (), s32[]{:S(2)}) async-start(), calls=%async_computation.2 | async-start | bytes 2359296 | tf_op jit(solution)/shard_map/all_gather | solution.py:120
  8.2 95.4 %reduce-scatter.2.cloned.1.call-start = ((), (), s32[]{:S(2)}) async-start(), calls=%async_computation.3 | async-start | bytes 2359296 | tf_op jit(solution)/shard_map/reduce_scatter | solution.py:143
  8.3 19.9 %collective-permute-start.2 = (bf16[128,1024]{1,0:T(8,128)(2,1)}, bf16[128,1024]{1,0:T(8,128)(2,1)S(1)}, u32[]{:S(2)}, u32[]{:S(2)}) collective-permute-start(bf16[128,1024]{1,0:T(8,128)(2,1)} %shard_map.46), channel_id=1, source_target_pairs={{0,32},{1,33},{2,34},{3,35},{4,36},{5,37},{6,38},{7,39},{8,40},{9,... | collective-permute-start | bytes 786440 | tf_op jit(solution)/shard_map/ppermute | solution.py:111
  14.2 24.1 %collective-permute-start.1 = (bf16[128,1024]{1,0:T(8,128)(2,1)}, bf16[128,1024]{1,0:T(8,128)(2,1)S(1)}, u32[]{:S(2)}, u32[]{:S(2)}) collective-permute-start(bf16[128,1024]{1,0:T(8,128)(2,1)} %shard_map.46), channel_id=1, source_target_pairs={{0,48},{1,49},{2,50},{3,51},{4,52},{5,53},{6,54},{7,55},{8,56},{9,... | collective-permute-start | bytes 786440 | tf_op jit(solution)/shard_map/ppermute | solution.py:111
  18.3 20.1 %collective-permute-start = (bf16[128,1024]{1,0:T(8,128)(2,1)}, bf16[128,1024]{1,0:T(8,128)(2,1)S(1)}, u32[]{:S(2)}, u32[]{:S(2)}) collective-permute-start(bf16[128,1024]{1,0:T(8,128)(2,1)} %shard_map.46), channel_id=1, source_target_pairs={{0,8},{1,9},{2,10},{3,11},{4,12},{5,13},{6,14},{7,15},{8,16},{9,17... | collective-permute-start | bytes 786440 | tf_op jit(solution)/shard_map/ppermute | solution.py:111
  20.9 29.0 %collective-permute-start.4 = (bf16[128,1024]{1,0:T(8,128)(2,1)}, bf16[128,1024]{1,0:T(8,128)(2,1)S(1)}, u32[]{:S(2)}, u32[]{:S(2)}) collective-permute-start(bf16[128,1024]{1,0:T(8,128)(2,1)} %shard_map.46), channel_id=1, source_target_pairs={{0,24},{1,25},{2,26},{3,27},{4,28},{5,29},{6,30},{7,31},{8,32},{9,... | collective-permute-start | bytes 786440 | tf_op jit(solution)/shard_map/ppermute | solution.py:111
  49.9 69.4 %copy-start.1 = (s32[1,1,8]{2,1,0:T(1,128)S(1)}, s32[1,1,8]{2,1,0:T(1,128)}, u32[]{:S(2)}) copy-start(s32[1,1,8]{2,1,0:T(1,128)} %param.7) | copy-start | bytes 100
  53.3 66.0 %copy-start = (f32[1,1,8,128,128]{4,3,2,1,0:T(8,128)S(1)}, f32[1,1,8,128,128]{4,3,2,1,0:T(8,128)}, u32[]{:S(2)}) copy-start(f32[1,1,8,128,128]{4,3,2,1,0:T(8,128)} %param.6) | copy-start | bytes 1572868
  87.2 27.9 %collective-permute-start.6 = (f32[128,128]{1,0:T(8,128)S(1)}, f32[128,128]{1,0:T(8,128)S(1)}, u32[]{:S(2)}, u32[]{:S(2)}) collective-permute-start(f32[128,128]{1,0:T(8,128)S(1)} %shard_map.49), channel_id=1, source_target_pairs={{0,40},{1,41},{2,42},{3,43},{4,44},{5,45},{6,46},{7,47},{8,48},{9,... | collective-permute-start | bytes 196616 | tf_op jit(solution)/shard_map/ppermute | solution.py:111
  89.1 26.0 %collective-permute-start.5 = (f32[128,128]{1,0:T(8,128)S(1)}, f32[128,128]{1,0:T(8,128)S(1)}, u32[]{:S(2)}, u32[]{:S(2)}) collective-permute-start(f32[128,128]{1,0:T(8,128)S(1)} %shard_map.49), channel_id=1, source_target_pairs={{0,0},{1,7},{2,6},{3,5},{4,4},{5,3},{6,2},{7,1},{8,8},{9,15},{10,1... | collective-permute-start | bytes 196616 | tf_op jit(solution)/shard_map/ppermute | solution.py:111
  103.7 15.7 %collective-permute-start.3 = (f32[4,128,128]{2,1,0:T(8,128)}, f32[4,128,128]{2,1,0:T(8,128)S(1)}, u32[]{:S(2)}, u32[]{:S(2)}) collective-permute-start(f32[4,128,128]{2,1,0:T(8,128)} %bitcast.10), channel_id=1, source_target_pairs={{0,0},{1,7},{2,6},{3,5},{4,4},{5,3},{6,2},{7,1},{8,8},{9,15},{10,1... | collective-permute-start | bytes 786440 | tf_op jit(solution)/shard_map/ppermute | solution.py:111
  108.1 7.1 %collective-permute-start.8 = (f32[128,128]{1,0:T(8,128)S(1)}, f32[128,128]{1,0:T(8,128)S(1)}, u32[]{:S(2)}, u32[]{:S(2)}) collective-permute-start(f32[128,128]{1,0:T(8,128)S(1)} %get-tuple-element.5), channel_id=1, source_target_pairs={{0,16},{1,17},{2,18},{3,19},{4,20},{5,21},{6,22},{7,23},{8,24},{9,... | collective-permute-start | bytes 196616 | tf_op jit(solution)/shard_map/ppermute | solution.py:111
  113.2 6.2 %collective-permute-start.7 = (f32[128,128]{1,0:T(8,128)S(1)}, f32[128,128]{1,0:T(8,128)S(1)}, u32[]{:S(2)}, u32[]{:S(2)}) collective-permute-start(f32[128,128]{1,0:T(8,128)S(1)} %get-tuple-element.6), channel_id=1, source_target_pairs={{0,56},{1,57},{2,58},{3,59},{4,60},{5,61},{6,62},{7,63},{8,0},{9,1... | collective-permute-start | bytes 196616 | tf_op jit(solution)/shard_map/ppermute | solution.py:111
Sparse Core Ops, SparseCore 0:
  9.5 33.6 all-gather.1
  47.1 56.5 reduce-scatter.1

commit v11 on v9

--- a/solution.py
+++ b/solution.py
@@ -25,17 +25,23 @@
     out_ref[:, half:] = b_ref[...]
 
 
-def products(n, tile, depth, count, offset, rows_ref, *refs):
+def products(n, tile, depth, count, offset, resid_ref, samples_ref, *refs):
     columns, (out_ref, rows, picked, made, own_sems, row_sems, out_sems) = refs[:count - offset], refs[count - offset:]
     k = lax.axis_index("k")
     per = n // CHUNKS
+    halves = resid_ref, samples_ref
     chunks = [
-        pltpu.make_async_copy(rows_ref.at[pl.ds(c * per * tile, per * tile)], rows.at[c], row_sems.at[c])
+        pltpu.make_async_copy(
+            halves[h].at[pl.ds(c * per * tile, per * tile)],
+            rows.at[c, :, pl.ds(h * depth, depth)],
+            row_sems.at[c, h],
+        )
         for c in range(CHUNKS)
+        for h in range(2)
     ]
     here = [
         pltpu.make_async_copy(
-            rows_ref.at[pl.ds(pl.multiple_of(k * tile, tile), tile), pl.ds((1 - h) * depth, depth)],
+            halves[1 - h].at[pl.ds(pl.multiple_of(k * tile, tile), tile)],
             picked.at[pl.ds(0, tile), pl.ds(h * depth, depth)],
             own_sems.at[h],
         )
@@ -50,7 +56,8 @@
         copy.wait()
     stores = []
     for c in range(CHUNKS):
-        chunks[c].wait()
+        for h in range(2):
+            chunks[2 * c + h].wait()
         part = lax.dot_general(
             rows[c], picked[...], (((1,), (1,)), ((), ())), preferred_element_type=jnp.float32
         )
@@ -117,7 +124,7 @@
         out_specs=vmem,
         compiler_params=pltpu.CompilerParams(vmem_limit_bytes=60 * MIB),
     )(resid, samples)
-    rows = lax.all_gather(own, "k", axis=0, tiled=True)
+    halves = lax.all_gather((resid, samples), "k", axis=0, tiled=True)
     panel = {d: moved(own, lambda z, y, k, d=d: (z, y - d, k)) for d in SENT}
 
     def multiplied(columns, offset, flops):
@@ -125,19 +132,19 @@
         return pl.pallas_call(
             functools.partial(products, n, tile, depth, count, offset),
             out_shape=jax.ShapeDtypeStruct((n, count, tile, tile), jnp.float32),
-            in_specs=[far] + [vmem] * len(columns),
+            in_specs=[far, far] + [vmem] * len(columns),
             out_specs=far,
             scratch_shapes=[
                 pltpu.VMEM((CHUNKS, n // CHUNKS * tile, 2 * depth), jnp.bfloat16),
                 pltpu.VMEM((count * tile, 2 * depth), jnp.bfloat16),
                 pltpu.VMEM((n, count, tile, tile), jnp.float32),
                 pltpu.SemaphoreType.DMA((2,)),
-                pltpu.SemaphoreType.DMA((CHUNKS,)),
+                pltpu.SemaphoreType.DMA((CHUNKS, 2)),
                 pltpu.SemaphoreType.DMA((n,)),
             ],
             compiler_params=pltpu.CompilerParams(vmem_limit_bytes=52 * MIB),
             cost_estimate=pl.CostEstimate(flops=flops, bytes_accessed=6 * MIB, transcendentals=0),
-        )(rows, *columns)
+        )(*halves, *columns)
 
     once = 4 * n * tile * tile * depth
     early = lax.psum_scatter(

time: 126 us -> 155 us (1.23)
  the two profiles are of different devices: /device:TPU:26 before, /device:TPU:2 now
where the time goes in v11:
time: 155 us
  waiting for transfers between devices  58.2 us (38%)
  starting transfers between devices  41.1 us (27%)
  blocking collectives  28.6 us (18%)
  between operations  13.3 us (9%)
  Pallas kernels  10.2 us (7%)
  local copies, waits for them, and re-layouts  3.32 us (2%)
    ppermute x9, starting transfers between devices, moved(): return lax.ppermute(a, AXES, [(index(*i), index(*to(*i))) for i in ids])  41 us
    all_to_all x1, blocking collectives, local(): lax.all_to_all(multiplied([panel[LATE]], 0, weight), 'z', 0, 0, tiled=True)  28.6 us
    all_gather x2, waiting for transfers between devices, local(): halves = lax.all_gather((resid, samples), 'k', axis=0, tiled=True)  25.9 us
    ppermute x9, waiting for transfers between devices, moved(): return lax.ppermute(a, AXES, [(index(*i), index(*to(*i))) for i in ids])  20.6 us
    reduce_scatter x1, waiting for transfers between devices, local(): lax.psum_scatter(multiplied([panel[d] for d in EARLY[1:]], 1, once), 'z',...  10.3 us
    pallas_call x2, Pallas kernels, multiplied(): pl.pallas_call(functools.partial(products, n, tile, depth, count, offset)...  6.93 us
  transfers between devices with their start and end apart: 12, of which 6 were waited for; matrix products, arithmetic and copies ran while one was open for 1% of the time, Pallas kernels for 6%

profile of v11, /device:TPU:2, one launch (start us, length us, event | category | flops | bytes accessed | tf_op | source)
XLA Modules:
  0.0 154.6 jit_solution(2653406101844986225)
XLA Ops:
  6.5 0.7 all-gather.3.cloned.1.call-update
  7.3 0.0 all-gather.5.cloned.1.call-start
  7.3 0.7 all-gather.5.cloned.1.call-update
  8.0 0.0 reduce-scatter.2.cloned.1.call-start
  8.1 1.7 %shard_map.46 = bf16[128,1024]{1,0:T(8,128)(2,1)} custom-call(bf16[128,512]{1,0:T(8,128)(2,1)} %a_ref.1, bf16[128,512]{1,0:T(8,128)(2,1)} %b_ref.1), custom_call_target="tpu_custom_call" | custom-call | tf_op jit(solution)/shard_map/pallas_call | solution.py:120
  9.7 7.7 %collective-permute-start.2 = (bf16[128,1024]{1,0:T(8,128)(2,1)}, bf16[128,1024]{1,0:T(8,128)(2,1)S(1)}, u32[]{:S(2)}, u32[]{:S(2)}) collective-permute-start(bf16[128,1024]{1,0:T(8,128)(2,1)} %shard_map.46), channel_id=1, source_target_pairs={{0,32},{1,33},{2,34},{3,35},{4,36},{5,37},{6,38},{7,39},{8,40},{9,... | collective-permute-start | bytes 786440 | tf_op jit(solution)/shard_map/ppermute | solution.py:118
  17.5 2.7 %collective-permute-start.1 = (bf16[128,1024]{1,0:T(8,128)(2,1)}, bf16[128,1024]{1,0:T(8,128)(2,1)S(1)}, u32[]{:S(2)}, u32[]{:S(2)}) collective-permute-start(bf16[128,1024]{1,0:T(8,128)(2,1)} %shard_map.46), channel_id=1, source_target_pairs={{0,16},{1,17},{2,18},{3,19},{4,20},{5,21},{6,22},{7,23},{8,24},{9,... | collective-permute-start | bytes 786440 | tf_op jit(solution)/shard_map/ppermute | solution.py:118
  20.2 2.6 %collective-permute-start = (bf16[128,1024]{1,0:T(8,128)(2,1)}, bf16[128,1024]{1,0:T(8,128)(2,1)S(1)}, u32[]{:S(2)}, u32[]{:S(2)}) collective-permute-start(bf16[128,1024]{1,0:T(8,128)(2,1)} %shard_map.46), channel_id=1, source_target_pairs={{0,8},{1,9},{2,10},{3,11},{4,12},{5,13},{6,14},{7,15},{8,16},{9,17... | collective-permute-start | bytes 786440 | tf_op jit(solution)/shard_map/ppermute | solution.py:118
  22.8 6.0 %collective-permute-start.4 = (bf16[128,1024]{1,0:T(8,128)(2,1)}, bf16[128,1024]{1,0:T(8,128)(2,1)S(1)}, u32[]{:S(2)}, u32[]{:S(2)}) collective-permute-start(bf16[128,1024]{1,0:T(8,128)(2,1)} %shard_map.46), channel_id=1, source_target_pairs={{0,40},{1,41},{2,42},{3,43},{4,44},{5,45},{6,46},{7,47},{8,48},{9,... | collective-permute-start | bytes 786440 | tf_op jit(solution)/shard_map/ppermute | solution.py:118
  28.8 1.3 collective-permute-done.2.refs_2_
  30.1 11.1 %collective-permute-done.1.refs_1_ = bf16[128,1024]{1,0:T(8,128)(2,1)S(1)} collective-permute-done((bf16[128,1024]{1,0:T(8,128)(2,1)}, bf16[128,1024]{1,0:T(8,128)(2,1)S(1)}, u32[]{:S(2)}, u32[]{:S(2)}) %collective-permute-start.1) | collective-permute-done | bytes 262176 | tf_op jit(solution)/shard_map/ppermute | solution.py:118
  41.3 5.3 %collective-permute-done.refs_0_ = bf16[128,1024]{1,0:T(8,128)(2,1)S(1)} collective-permute-done((bf16[128,1024]{1,0:T(8,128)(2,1)}, bf16[128,1024]{1,0:T(8,128)(2,1)S(1)}, u32[]{:S(2)}, u32[]{:S(2)}) %collective-permute-start) | collective-permute-done | bytes 262176 | tf_op jit(solution)/shard_map/ppermute | solution.py:118
  46.5 25.9 %all-gather.5.cloned.1.call-done.samples_ref = bf16[1024,512]{1,0:T(8,128)(2,1)} async-done(((bf16[128,512]{1,0:T(8,128)(2,1)}), bf16[1024,512]{1,0:T(8,128)(2,1)}) %all-gather.5.cloned.1.call-update) | async-done | bytes 1048592 | tf_op jit(solution)/shard_map/all_gather | solution.py:127
  72.4 1.2 copy-done
  73.7 3.6 %shard_map.47 = f32[8,4,128,128]{3,2,1,0:T(8,128)} custom-call(bf16[1024,512]{1,0:T(8,128)(2,1)S(1)} %copy-done, bf16[1024,512]{1,0:T(8,128)(2,1)} %all-gather.5.cloned.1.call-done.samples_ref, bf16[128,1024]{1,0:T(8,128)(2,1)S(1)} %collective-permute-done.refs_0_, bf16[128,1024]{1,0:T(8,128)(2,1)S(1)} %collective-permute-done.1.refs_1_, ...), custom_call_target="tpu_custom_call" | custom-call | flops 268435456 | bytes 6291456 | tf_op jit(solution)/shard_map/pallas_call | solution.py:132
  77.3 0.0 reduce-scatter.2.cloned.1.call-update
  77.3 0.0 collective-permute-done.4.refs_0_
  77.3 1.2 copy-done.1
  78.5 3.3 %shard_map.48 = f32[8,1,128,128]{3,2,1,0:T(8,128)S(1)} custom-call(bf16[1024,512]{1,0:T(8,128)(2,1)S(1)} %copy-done.1, bf16[1024,512]{1,0:T(8,128)(2,1)} %all-gather.5.cloned.1.call-done.samples_ref, bf16[128,1024]{1,0:T(8,128)(2,1)S(1)} %collective-permute-done.4.refs_0_), custom_call_target="tpu_custom_call" | custom-call | flops 161061273600 | bytes 6291456 | tf_op jit(solution)/shard_map/pallas_call | solution.py:132
  81.8 0.0 copy-start.2
  81.8 28.6 %all_to_all.5.parts_ref = f32[8,1,128,128]{3,2,1,0:T(8,128)S(1)} all-to-all(f32[8,1,128,128]{3,2,1,0:T(8,128)S(1)} %shard_map.48), channel_id=1, replica_groups=mesh['z'=8,'y'=8,'k'=8] {'z'}, dimensions={0} | all-to-all | bytes 1048576 | tf_op jit(solution)/shard_map/all_to_all | solution.py:154
  110.4 5.2 %collective-permute-start.6 = (f32[128,128]{1,0:T(8,128)S(1)}, f32[128,128]{1,0:T(8,128)S(1)}, u32[]{:S(2)}, u32[]{:S(2)}) collective-permute-start(f32[128,128]{1,0:T(8,128)S(1)} %shard_map.49), channel_id=1, source_target_pairs={{0,24},{1,25},{2,26},{3,27},{4,28},{5,29},{6,30},{7,31},{8,32},{9,... | collective-permute-start | bytes 196616 | tf_op jit(solution)/shard_map/ppermute | solution.py:118
  115.7 4.0 %collective-permute-start.5 = (f32[128,128]{1,0:T(8,128)S(1)}, f32[128,128]{1,0:T(8,128)S(1)}, u32[]{:S(2)}, u32[]{:S(2)}) collective-permute-start(f32[128,128]{1,0:T(8,128)S(1)} %shard_map.49), channel_id=1, source_target_pairs={{0,0},{1,7},{2,6},{3,5},{4,4},{5,3},{6,2},{7,1},{8,8},{9,15},{10,1... | collective-permute-start | bytes 196616 | tf_op jit(solution)/shard_map/ppermute | solution.py:118
  119.7 10.3 %reduce-scatter.2.cloned.1.call-done = f32[1,4,128,128]{3,2,1,0:T(8,128)} async-done(((f32[8,4,128,128]{3,2,1,0:T(8,128)}), f32[1,4,128,128]{3,2,1,0:T(8,128)}) %reduce-scatter.2.cloned.1.call-update) | async-done | bytes 262160 | tf_op jit(solution)/shard_map/reduce_scatter | solution.py:150
  130.0 3.8 %collective-permute-start.3 = (f32[4,128,128]{2,1,0:T(8,128)}, f32[4,128,128]{2,1,0:T(8,128)S(1)}, u32[]{:S(2)}, u32[]{:S(2)}) collective-permute-start(f32[4,128,128]{2,1,0:T(8,128)} %bitcast.10), channel_id=1, source_target_pairs={{0,0},{1,7},{2,6},{3,5},{4,4},{5,3},{6,2},{7,1},{8,8},{9,15},{10,1... | collective-permute-start | bytes 786440 | tf_op jit(solution)/shard_map/ppermute | solution.py:118
  133.8 0.9 slice_bitcast_fusion
  134.7 5.7 %collective-permute-start.8 = (f32[128,128]{1,0:T(8,128)S(1)}, f32[128,128]{1,0:T(8,128)S(1)}, u32[]{:S(2)}, u32[]{:S(2)}) collective-permute-start(f32[128,128]{1,0:T(8,128)S(1)} %get-tuple-element.5), channel_id=1, source_target_pairs={{0,48},{1,49},{2,50},{3,51},{4,52},{5,53},{6,54},{7,55},{8,56},{9,... | collective-permute-start | bytes 196616 | tf_op jit(solution)/shard_map/ppermute | solution.py:118
  140.4 3.3 %collective-permute-start.7 = (f32[128,128]{1,0:T(8,128)S(1)}, f32[128,128]{1,0:T(8,128)S(1)}, u32[]{:S(2)}, u32[]{:S(2)}) collective-permute-start(f32[128,128]{1,0:T(8,128)S(1)} %get-tuple-element.6), channel_id=1, source_target_pairs={{0,56},{1,57},{2,58},{3,59},{4,60},{5,61},{6,62},{7,63},{8,0},{9,1... | collective-permute-start | bytes 196616 | tf_op jit(solution)/shard_map/ppermute | solution.py:118
  143.7 0.0 collective-permute-done.5.late
  143.7 0.0 collective-permute-done.8.refs_2_
  143.7 2.9 %collective-permute-done.7.refs_1_ = f32[128,128]{1,0:T(8,128)S(1)} collective-permute-done((f32[128,128]{1,0:T(8,128)S(1)}, f32[128,128]{1,0:T(8,128)S(1)}, u32[]{:S(2)}, u32[]{:S(2)}) %collective-permute-start.7) | collective-permute-done | bytes 65568 | tf_op jit(solution)/shard_map/ppermute | solution.py:118
  146.5 1.6 %shard_map.50 = f32[8,128,128]{2,1,0:T(8,128)} custom-call(s32[8]{0:T(128)S(1)} %bitcast.9, f32[4,128,128]{2,1,0:T(8,128)S(1)} %collective-permute-done.3.mirrored, f32[128,128]{1,0:T(8,128)S(1)} %collective-permute-done.5.late, f32[128,128]{1,0:T(8,128)S(1)} %collective-permute-done.6.refs_0_, f32[128,128]{1,0:T(8,128)S(1)} %collective-permute-done.7.refs_1_, ...), custom_call_target="tpu_custom_call" | custom-call | tf_op jit(solution)/shard_map/pallas_call | solution.py:166
  (10 shorter events, 0.0 us)
Async XLA Ops:
  6.5 40.0 %all-gather.3.cloned.1.call-start = ((), (), s32[]{:S(2)}) async-start(), calls=%async_computation.2 | async-start | bytes 1179648 | tf_op jit(solution)/shard_map/all_gather | solution.py:127
  7.3 65.2 %all-gather.5.cloned.1.call-start = ((), (), s32[]{:S(2)}) async-start(), calls=%async_computation.3 | async-start | bytes 1179648 | tf_op jit(solution)/shard_map/all_gather | solution.py:127
  8.0 122.0 %reduce-scatter.2.cloned.1.call-start = ((), (), s32[]{:S(2)}) async-start(), calls=%async_computation.4 | async-start | bytes 2359296 | tf_op jit(solution)/shard_map/reduce_scatter | solution.py:150
  9.7 20.4 %collective-permute-start.2 = (bf16[128,1024]{1,0:T(8,128)(2,1)}, bf16[128,1024]{1,0:T(8,128)(2,1)S(1)}, u32[]{:S(2)}, u32[]{:S(2)}) collective-permute-start(bf16[128,1024]{1,0:T(8,128)(2,1)} %shard_map.46), channel_id=1, source_target_pairs={{0,32},{1,33},{2,34},{3,35},{4,36},{5,37},{6,38},{7,39},{8,40},{9,... | collective-permute-start | bytes 786440 | tf_op jit(solution)/shard_map/ppermute | solution.py:118
  17.5 23.8 %collective-permute-start.1 = (bf16[128,1024]{1,0:T(8,128)(2,1)}, bf16[128,1024]{1,0:T(8,128)(2,1)S(1)}, u32[]{:S(2)}, u32[]{:S(2)}) collective-permute-start(bf16[128,1024]{1,0:T(8,128)(2,1)} %shard_map.46), channel_id=1, source_target_pairs={{0,16},{1,17},{2,18},{3,19},{4,20},{5,21},{6,22},{7,23},{8,24},{9,... | collective-permute-start | bytes 786440 | tf_op jit(solution)/shard_map/ppermute | solution.py:118
  20.2 26.4 %collective-permute-start = (bf16[128,1024]{1,0:T(8,128)(2,1)}, bf16[128,1024]{1,0:T(8,128)(2,1)S(1)}, u32[]{:S(2)}, u32[]{:S(2)}) collective-permute-start(bf16[128,1024]{1,0:T(8,128)(2,1)} %shard_map.46), channel_id=1, source_target_pairs={{0,8},{1,9},{2,10},{3,11},{4,12},{5,13},{6,14},{7,15},{8,16},{9,17... | collective-permute-start | bytes 786440 | tf_op jit(solution)/shard_map/ppermute | solution.py:118
  22.8 54.6 %collective-permute-start.4 = (bf16[128,1024]{1,0:T(8,128)(2,1)}, bf16[128,1024]{1,0:T(8,128)(2,1)S(1)}, u32[]{:S(2)}, u32[]{:S(2)}) collective-permute-start(bf16[128,1024]{1,0:T(8,128)(2,1)} %shard_map.46), channel_id=1, source_target_pairs={{0,40},{1,41},{2,42},{3,43},{4,44},{5,45},{6,46},{7,47},{8,48},{9,... | collective-permute-start | bytes 786440 | tf_op jit(solution)/shard_map/ppermute | solution.py:118
  72.4 1.2 copy-start
  77.3 1.2 copy-start.1
  78.5 68.0 %copy-start.3 = (s32[1,1,8]{2,1,0:T(1,128)S(1)}, s32[1,1,8]{2,1,0:T(1,128)}, u32[]{:S(2)}) copy-start(s32[1,1,8]{2,1,0:T(1,128)} %param.7) | copy-start | bytes 100
  81.8 64.7 %copy-start.2 = (f32[1,1,8,128,128]{4,3,2,1,0:T(8,128)S(1)}, f32[1,1,8,128,128]{4,3,2,1,0:T(8,128)}, u32[]{:S(2)}) copy-start(f32[1,1,8,128,128]{4,3,2,1,0:T(8,128)} %param.6) | copy-start | bytes 1572868
  110.4 33.2 %collective-permute-start.6 = (f32[128,128]{1,0:T(8,128)S(1)}, f32[128,128]{1,0:T(8,128)S(1)}, u32[]{:S(2)}, u32[]{:S(2)}) collective-permute-start(f32[128,128]{1,0:T(8,128)S(1)} %shard_map.49), channel_id=1, source_target_pairs={{0,24},{1,25},{2,26},{3,27},{4,28},{5,29},{6,30},{7,31},{8,32},{9,... | collective-permute-start | bytes 196616 | tf_op jit(solution)/shard_map/ppermute | solution.py:118
  115.7 28.0 %collective-permute-start.5 = (f32[128,128]{1,0:T(8,128)S(1)}, f32[128,128]{1,0:T(8,128)S(1)}, u32[]{:S(2)}, u32[]{:S(2)}) collective-permute-start(f32[128,128]{1,0:T(8,128)S(1)} %shard_map.49), channel_id=1, source_target_pairs={{0,0},{1,7},{2,6},{3,5},{4,4},{5,3},{6,2},{7,1},{8,8},{9,15},{10,1... | collective-permute-start | bytes 196616 | tf_op jit(solution)/shard_map/ppermute | solution.py:118
  130.0 16.5 %collective-permute-start.3 = (f32[4,128,128]{2,1,0:T(8,128)}, f32[4,128,128]{2,1,0:T(8,128)S(1)}, u32[]{:S(2)}, u32[]{:S(2)}) collective-permute-start(f32[4,128,128]{2,1,0:T(8,128)} %bitcast.10), channel_id=1, source_target_pairs={{0,0},{1,7},{2,6},{3,5},{4,4},{5,3},{6,2},{7,1},{8,8},{9,15},{10,1... | collective-permute-start | bytes 786440 | tf_op jit(solution)/shard_map/ppermute | solution.py:118
  134.7 9.0 %collective-permute-start.8 = (f32[128,128]{1,0:T(8,128)S(1)}, f32[128,128]{1,0:T(8,128)S(1)}, u32[]{:S(2)}, u32[]{:S(2)}) collective-permute-start(f32[128,128]{1,0:T(8,128)S(1)} %get-tuple-element.5), channel_id=1, source_target_pairs={{0,48},{1,49},{2,50},{3,51},{4,52},{5,53},{6,54},{7,55},{8,56},{9,... | collective-permute-start | bytes 196616 | tf_op jit(solution)/shard_map/ppermute | solution.py:118
  140.4 6.2 %collective-permute-start.7 = (f32[128,128]{1,0:T(8,128)S(1)}, f32[128,128]{1,0:T(8,128)S(1)}, u32[]{:S(2)}, u32[]{:S(2)}) collective-permute-start(f32[128,128]{1,0:T(8,128)S(1)} %get-tuple-element.6), channel_id=1, source_target_pairs={{0,56},{1,57},{2,58},{3,59},{4,60},{5,61},{6,62},{7,63},{8,0},{9,1... | collective-permute-start | bytes 196616 | tf_op jit(solution)/shard_map/ppermute | solution.py:118
Sparse Core Ops, SparseCore 0:
  9.5 32.0 all-gather.2
  43.8 28.5 all-gather.4
  77.4 52.5 reduce-scatter.1

commit v12 on v10

--- a/solution.py
+++ b/solution.py
@@ -11,10 +11,10 @@
 LASSO = 0.1
 RIDGE = 0.5
 AXES = ("z", "y", "k")
-EARLY = (0, 7, 2, 4)
-TURNED = (1, 2)
-LATE = 5
-SENT = (7, 2, 5, 4)
+EARLY = (0, 7, 4)
+TURNED = (1,)
+LATE = (3, 6)
+SENT = (7, 4, 3, 6)
 CHUNKS = 2
 MIB = 2**20
 
@@ -65,8 +65,11 @@
         copy.wait()
 
 
-def added(parts_ref, out_ref):
-    out_ref[...] = jnp.sum(parts_ref[:, 0], axis=0)
+def added(parts_ref, out_ref, *each):
+    for i, ref in enumerate(each):
+        total = jnp.sum(parts_ref[:, i], axis=0)
+        out_ref[i] = total
+        ref[...] = total
 
 
 def finish(n, tile, scale, active_ref, mirrored, late, *refs):
@@ -92,10 +95,11 @@
             shrunk = jnp.where(on_diag, stepped, shrunk)
         out_ref[t] = shrunk * active_ref[t].astype(jnp.float32)
 
-    put(LATE, late[...])
+    for i, d in enumerate(LATE):
+        put(d, late[i])
     for i, d in enumerate(EARLY):
         put(d, mirrored[i])
-    for d, ref in zip((LATE,) + tuple(EARLY[i] for i in TURNED), arrived):
+    for d, ref in zip(LATE + tuple(EARLY[i] for i in TURNED), arrived):
         put(n - d, ref[...].T)
 
 
@@ -144,15 +148,16 @@
         multiplied([panel[d] for d in EARLY[1:]], 1, once), "z", scatter_dimension=0, tiled=True
     )[0]
     weight = 600 * once
-    parts = lax.all_to_all(multiplied([panel[LATE]], 0, weight), "z", 0, 0, tiled=True)
-    late = pl.pallas_call(
+    parts = lax.all_to_all(multiplied([panel[d] for d in LATE], 0, weight), "z", 0, 0, tiled=True)
+    square = jax.ShapeDtypeStruct((tile, tile), jnp.float32)
+    late, *each = pl.pallas_call(
         added,
-        out_shape=jax.ShapeDtypeStruct((tile, tile), jnp.float32),
+        out_shape=[jax.ShapeDtypeStruct((len(LATE), tile, tile), jnp.float32)] + [square] * len(LATE),
         in_specs=[vmem],
-        out_specs=vmem,
+        out_specs=[vmem] * (1 + len(LATE)),
         compiler_params=pltpu.CompilerParams(vmem_limit_bytes=16 * MIB),
     )(parts)
-    arrived = [moved(late, lambda z, y, k: (z, y + LATE, k))]
+    arrived = [moved(a, lambda z, y, k, d=d: (z, y + d, k)) for a, d in zip(each, LATE)]
     late = moved(late, lambda z, y, k: (z, y, z - k))
     mirrored = moved(early, lambda z, y, k: (z, y, z - k))
     arrived += [moved(early[i], lambda z, y, k, d=EARLY[i]: (z, y + d, k)) for i in TURNED]

time: 128 us -> 135 us (1.055)
  waiting for transfers between devices: 36.6 us -> 21.9 us
  blocking collectives: 33.8 us -> 45.5 us
  starting transfers between devices: 32.4 us -> 41.2 us
    all_to_all x1, blocking collectives: 33.8 us -> 45.5 us  [local(): lax.all_to_all(multiplied([panel[d] for d in LATE], 0, weight), 'z', 0, 0...]
    reduce_scatter x1, waiting for transfers between devices: 10.5 us -> 0.02 us  [local(): lax.psum_scatter(multiplied([panel[d] for d in EARLY[1:]], 1, once), 'z',...]
    ppermute x9, waiting for transfers between devices: 21.3 us -> 11.8 us  [moved(): return lax.ppermute(a, AXES, [(index(*i), index(*to(*i))) for i in ids])]
    ppermute x9, starting transfers between devices: 32.4 us -> 41.1 us  [moved(): return lax.ppermute(a, AXES, [(index(*i), index(*to(*i))) for i in ids])]
    all_gather x1, waiting for transfers between devices: 4.84 us -> 10.1 us  [local(): rows = lax.all_gather(own, 'k', axis=0, tiled=True)]
  transfers between devices with their start and end apart: 11 -> 11, of which waited for: 7 -> 3; matrix products, arithmetic and copies ran while one was open for 1% -> 1% of each run, Pallas kernels for 6% -> 6%
where the time goes in v12:
time: 135 us; the launch traced here: 134 us
  blocking collectives  45.5 us (34%)
  starting transfers between devices  41.2 us (31%)
  waiting for transfers between devices  21.9 us (16%)
  between operations  13.6 us (10%)
  Pallas kernels  11.1 us (8%)
    all_to_all x1, blocking collectives, local(): lax.all_to_all(multiplied([panel[d] for d in LATE], 0, weight), 'z', 0, 0...  45.5 us
    ppermute x9, starting transfers between devices, moved(): return lax.ppermute(a, AXES, [(index(*i), index(*to(*i))) for i in ids])  41.1 us
    ppermute x9, waiting for transfers between devices, moved(): return lax.ppermute(a, AXES, [(index(*i), index(*to(*i))) for i in ids])  11.8 us
    all_gather x1, waiting for transfers between devices, local(): rows = lax.all_gather(own, 'k', axis=0, tiled=True)  10.1 us
    pallas_call x2, Pallas kernels, multiplied(): pl.pallas_call(functools.partial(products, n, tile, depth, count, offset)...  7.78 us
  transfers between devices with their start and end apart: 11, of which 3 were waited for; matrix products, arithmetic and copies ran while one was open for 1% of the time, Pallas kernels for 6%

profile of v12, /device:TPU:18, one launch (start us, length us, event | category | flops | bytes accessed | tf_op | source)
XLA Modules:
  0.0 134.1 jit_solution(16463366310115791322)
XLA Ops:
  6.5 1.7 %shard_map.46 = bf16[128,1024]{1,0:T(8,128)(2,1)} custom-call(bf16[128,512]{1,0:T(8,128)(2,1)} %a_ref.1, bf16[128,512]{1,0:T(8,128)(2,1)} %b_ref.1), custom_call_target="tpu_custom_call" | custom-call | tf_op jit(solution)/shard_map/pallas_call | solution.py:117
  8.2 0.0 all-gather.2.cloned.1.call-update
  8.2 0.0 reduce-scatter.2.cloned.1.call-start
  8.3 3.5 %collective-permute-start = (bf16[128,1024]{1,0:T(8,128)(2,1)}, bf16[128,1024]{1,0:T(8,128)(2,1)S(1)}, u32[]{:S(2)}, u32[]{:S(2)}) collective-permute-start(bf16[128,1024]{1,0:T(8,128)(2,1)} %shard_map.46), channel_id=1, source_target_pairs={{0,8},{1,9},{2,10},{3,11},{4,12},{5,13},{6,14},{7,15},{8,16},{9,17... | collective-permute-start | bytes 786440 | tf_op jit(solution)/shard_map/ppermute | solution.py:115
  11.8 5.0 %collective-permute-start.1 = (bf16[128,1024]{1,0:T(8,128)(2,1)}, bf16[128,1024]{1,0:T(8,128)(2,1)S(1)}, u32[]{:S(2)}, u32[]{:S(2)}) collective-permute-start(bf16[128,1024]{1,0:T(8,128)(2,1)} %shard_map.46), channel_id=1, source_target_pairs={{0,32},{1,33},{2,34},{3,35},{4,36},{5,37},{6,38},{7,39},{8,40},{9,... | collective-permute-start | bytes 786440 | tf_op jit(solution)/shard_map/ppermute | solution.py:115
  16.8 6.0 %collective-permute-start.3 = (bf16[128,1024]{1,0:T(8,128)(2,1)}, bf16[128,1024]{1,0:T(8,128)(2,1)S(1)}, u32[]{:S(2)}, u32[]{:S(2)}) collective-permute-start(bf16[128,1024]{1,0:T(8,128)(2,1)} %shard_map.46), channel_id=1, source_target_pairs={{0,40},{1,41},{2,42},{3,43},{4,44},{5,45},{6,46},{7,47},{8,48},{9,... | collective-permute-start | bytes 786440 | tf_op jit(solution)/shard_map/ppermute | solution.py:115
  22.9 2.7 %collective-permute-start.4 = (bf16[128,1024]{1,0:T(8,128)(2,1)}, bf16[128,1024]{1,0:T(8,128)(2,1)S(1)}, u32[]{:S(2)}, u32[]{:S(2)}) collective-permute-start(bf16[128,1024]{1,0:T(8,128)(2,1)} %shard_map.46), channel_id=1, source_target_pairs={{0,16},{1,17},{2,18},{3,19},{4,20},{5,21},{6,22},{7,23},{8,24},{9,... | collective-permute-start | bytes 786440 | tf_op jit(solution)/shard_map/ppermute | solution.py:115
  25.6 0.0 collective-permute-done.refs_0_
  25.6 7.6 %collective-permute-done.1.refs_1_ = bf16[128,1024]{1,0:T(8,128)(2,1)S(1)} collective-permute-done((bf16[128,1024]{1,0:T(8,128)(2,1)}, bf16[128,1024]{1,0:T(8,128)(2,1)S(1)}, u32[]{:S(2)}, u32[]{:S(2)}) %collective-permute-start.1) | collective-permute-done | bytes 262176 | tf_op jit(solution)/shard_map/ppermute | solution.py:115
  33.1 10.1 %all-gather.2.cloned.1.call-done.rows_ref = bf16[1024,1024]{1,0:T(8,128)(2,1)} async-done(((bf16[128,1024]{1,0:T(8,128)(2,1)}), bf16[1024,1024]{1,0:T(8,128)(2,1)}) %all-gather.2.cloned.1.call-update) | async-done | bytes 2097168 | tf_op jit(solution)/shard_map/all_gather | solution.py:124
  43.2 3.6 %shard_map.47 = f32[8,3,128,128]{3,2,1,0:T(8,128)} custom-call(bf16[1024,1024]{1,0:T(8,128)(2,1)} %all-gather.2.cloned.1.call-done.rows_ref, bf16[128,1024]{1,0:T(8,128)(2,1)S(1)} %collective-permute-done.refs_0_, bf16[128,1024]{1,0:T(8,128)(2,1)S(1)} %collective-permute-done.1.refs_1_), custom_call_target="tpu_custom_call" | custom-call | flops 268435456 | bytes 6291456 | tf_op jit(solution)/shard_map/pallas_call | solution.py:129
  46.9 0.0 reduce-scatter.2.cloned.1.call-update
  46.9 0.0 collective-permute-done.3.refs_0_
  46.9 0.0 collective-permute-done.4.refs_1_
  46.9 4.2 %shard_map.48 = f32[8,2,128,128]{3,2,1,0:T(8,128)S(1)} custom-call(bf16[1024,1024]{1,0:T(8,128)(2,1)} %all-gather.2.cloned.1.call-done.rows_ref, bf16[128,1024]{1,0:T(8,128)(2,1)S(1)} %collective-permute-done.3.refs_0_, bf16[128,1024]{1,0:T(8,128)(2,1)S(1)} %collective-permute-done.4.refs_1_), custom_call_target="tpu_custom_call" | custom-call | flops 161061273600 | bytes 6291456 | tf_op jit(solution)/shard_map/pallas_call | solution.py:129
  51.1 0.0 copy-start
  51.1 0.0 copy-start.1
  51.1 45.5 %all_to_all.5.parts_ref = f32[8,2,128,128]{3,2,1,0:T(8,128)S(1)} all-to-all(f32[8,2,128,128]{3,2,1,0:T(8,128)S(1)} %shard_map.48), channel_id=1, replica_groups=mesh['z'=8,'y'=8,'k'=8] {'z'}, dimensions={0} | all-to-all | bytes 2097152 | tf_op jit(solution)/shard_map/all_to_all | solution.py:151
  96.6 0.1 shard_map.49
  96.7 3.9 %collective-permute-start.5 = (f32[2,128,128]{2,1,0:T(8,128)S(1)}, f32[2,128,128]{2,1,0:T(8,128)S(1)}, u32[]{:S(2)}, u32[]{:S(2)}) collective-permute-start(f32[2,128,128]{2,1,0:T(8,128)S(1)} %get-tuple-element.8), channel_id=1, source_target_pairs={{0,0},{1,7},{2,6},{3,5},{4,4},{5,3},{6,2},{7,1},{8,8},{9,15},{10,1... | collective-permute-start | bytes 393224 | tf_op jit(solution)/shard_map/ppermute | solution.py:115
  100.6 10.0 %collective-permute-start.6 = (f32[128,128]{1,0:T(8,128)S(1)}, f32[128,128]{1,0:T(8,128)S(1)}, u32[]{:S(2)}, u32[]{:S(2)}) collective-permute-start(f32[128,128]{1,0:T(8,128)S(1)} %get-tuple-element.9), channel_id=1, source_target_pairs={{0,24},{1,25},{2,26},{3,27},{4,28},{5,29},{6,30},{7,31},{8,32},{9,... | collective-permute-start | bytes 196616 | tf_op jit(solution)/shard_map/ppermute | solution.py:115
  110.7 4.6 %collective-permute-start.7 = (f32[128,128]{1,0:T(8,128)S(1)}, f32[128,128]{1,0:T(8,128)S(1)}, u32[]{:S(2)}, u32[]{:S(2)}) collective-permute-start(f32[128,128]{1,0:T(8,128)S(1)} %get-tuple-element.10), channel_id=1, source_target_pairs={{0,48},{1,49},{2,50},{3,51},{4,52},{5,53},{6,54},{7,55},{8,56},{9,... | collective-permute-start | bytes 196616 | tf_op jit(solution)/shard_map/ppermute | solution.py:115
  115.3 0.0 reduce-scatter.2.cloned.1.call-done
  115.3 3.4 %collective-permute-start.2 = (f32[3,128,128]{2,1,0:T(8,128)}, f32[3,128,128]{2,1,0:T(8,128)S(1)}, u32[]{:S(2)}, u32[]{:S(2)}) collective-permute-start(f32[3,128,128]{2,1,0:T(8,128)} %bitcast.8), channel_id=1, source_target_pairs={{0,0},{1,7},{2,6},{3,5},{4,4},{5,3},{6,2},{7,1},{8,8},{9,15},{10,1... | collective-permute-start | bytes 589832 | tf_op jit(solution)/shard_map/ppermute | solution.py:115
  118.7 0.9 slice_bitcast_fusion
  119.6 1.9 %collective-permute-start.8 = (f32[128,128]{1,0:T(8,128)S(1)}, f32[128,128]{1,0:T(8,128)S(1)}, u32[]{:S(2)}, u32[]{:S(2)}) collective-permute-start(f32[128,128]{1,0:T(8,128)S(1)} %slice_bitcast_fusion), channel_id=1, source_target_pairs={{0,56},{1,57},{2,58},{3,59},{4,60},{5,61},{6,62},{7,63},{8,0},{9,1... | collective-permute-start | bytes 196616 | tf_op jit(solution)/shard_map/ppermute | solution.py:115
  121.5 0.0 collective-permute-done.6.refs_0_
  121.5 0.0 collective-permute-done.7.refs_1_
  121.5 0.0 collective-permute-done.5.late
  121.5 4.2 %collective-permute-done.8.refs_2_ = f32[128,128]{1,0:T(8,128)S(1)} collective-permute-done((f32[128,128]{1,0:T(8,128)S(1)}, f32[128,128]{1,0:T(8,128)S(1)}, u32[]{:S(2)}, u32[]{:S(2)}) %collective-permute-start.8) | collective-permute-done | bytes 65568 | tf_op jit(solution)/shard_map/ppermute | solution.py:115
  125.7 0.0 collective-permute-done.2.mirrored
  125.7 1.6 %shard_map.50 = f32[8,128,128]{2,1,0:T(8,128)} custom-call(s32[8]{0:T(128)S(1)} %bitcast.7, f32[3,128,128]{2,1,0:T(8,128)S(1)} %collective-permute-done.2.mirrored, f32[2,128,128]{2,1,0:T(8,128)S(1)} %collective-permute-done.5.late, f32[128,128]{1,0:T(8,128)S(1)} %collective-permute-done.6.refs_0_, f32[128,128]{1,0:T(8,128)S(1)} %collective-permute-done.7.refs_1_, ...), custom_call_target="tpu_custom_call" | custom-call | tf_op jit(solution)/shard_map/pallas_call | solution.py:164
  (3 shorter events, 0.0 us)
Async XLA Ops:
  6.5 36.7 %all-gather.2.cloned.1.call-start = ((), (), s32[]{:S(2)}) async-start(), calls=%async_computation.2 | async-start | bytes 2359296 | tf_op jit(solution)/shard_map/all_gather | solution.py:124
  8.2 107.1 %reduce-scatter.2.cloned.1.call-start = ((), (), s32[]{:S(2)}) async-start(), calls=%async_computation.3 | async-start | bytes 1769472 | tf_op jit(solution)/shard_map/reduce_scatter | solution.py:147
  8.3 17.3 %collective-permute-start = (bf16[128,1024]{1,0:T(8,128)(2,1)}, bf16[128,1024]{1,0:T(8,128)(2,1)S(1)}, u32[]{:S(2)}, u32[]{:S(2)}) collective-permute-start(bf16[128,1024]{1,0:T(8,128)(2,1)} %shard_map.46), channel_id=1, source_target_pairs={{0,8},{1,9},{2,10},{3,11},{4,12},{5,13},{6,14},{7,15},{8,16},{9,17... | collective-permute-start | bytes 786440 | tf_op jit(solution)/shard_map/ppermute | solution.py:115
  11.8 21.4 %collective-permute-start.1 = (bf16[128,1024]{1,0:T(8,128)(2,1)}, bf16[128,1024]{1,0:T(8,128)(2,1)S(1)}, u32[]{:S(2)}, u32[]{:S(2)}) collective-permute-start(bf16[128,1024]{1,0:T(8,128)(2,1)} %shard_map.46), channel_id=1, source_target_pairs={{0,32},{1,33},{2,34},{3,35},{4,36},{5,37},{6,38},{7,39},{8,40},{9,... | collective-permute-start | bytes 786440 | tf_op jit(solution)/shard_map/ppermute | solution.py:115
  16.8 30.0 %collective-permute-start.3 = (bf16[128,1024]{1,0:T(8,128)(2,1)}, bf16[128,1024]{1,0:T(8,128)(2,1)S(1)}, u32[]{:S(2)}, u32[]{:S(2)}) collective-permute-start(bf16[128,1024]{1,0:T(8,128)(2,1)} %shard_map.46), channel_id=1, source_target_pairs={{0,40},{1,41},{2,42},{3,43},{4,44},{5,45},{6,46},{7,47},{8,48},{9,... | collective-permute-start | bytes 786440 | tf_op jit(solution)/shard_map/ppermute | solution.py:115
  22.9 24.0 %collective-permute-start.4 = (bf16[128,1024]{1,0:T(8,128)(2,1)}, bf16[128,1024]{1,0:T(8,128)(2,1)S(1)}, u32[]{:S(2)}, u32[]{:S(2)}) collective-permute-start(bf16[128,1024]{1,0:T(8,128)(2,1)} %shard_map.46), channel_id=1, source_target_pairs={{0,16},{1,17},{2,18},{3,19},{4,20},{5,21},{6,22},{7,23},{8,24},{9,... | collective-permute-start | bytes 786440 | tf_op jit(solution)/shard_map/ppermute | solution.py:115
  51.1 74.7 %copy-start = (f32[1,1,8,128,128]{4,3,2,1,0:T(8,128)S(1)}, f32[1,1,8,128,128]{4,3,2,1,0:T(8,128)}, u32[]{:S(2)}) copy-start(f32[1,1,8,128,128]{4,3,2,1,0:T(8,128)} %param.6) | copy-start | bytes 1572868
  51.1 74.7 %copy-start.1 = (s32[1,1,8]{2,1,0:T(1,128)S(1)}, s32[1,1,8]{2,1,0:T(1,128)}, u32[]{:S(2)}) copy-start(s32[1,1,8]{2,1,0:T(1,128)} %param.7) | copy-start | bytes 100
  96.7 24.8 %collective-permute-start.5 = (f32[2,128,128]{2,1,0:T(8,128)S(1)}, f32[2,128,128]{2,1,0:T(8,128)S(1)}, u32[]{:S(2)}, u32[]{:S(2)}) collective-permute-start(f32[2,128,128]{2,1,0:T(8,128)S(1)} %get-tuple-element.8), channel_id=1, source_target_pairs={{0,0},{1,7},{2,6},{3,5},{4,4},{5,3},{6,2},{7,1},{8,8},{9,15},{10,1... | collective-permute-start | bytes 393224 | tf_op jit(solution)/shard_map/ppermute | solution.py:115
  100.6 20.9 %collective-permute-start.6 = (f32[128,128]{1,0:T(8,128)S(1)}, f32[128,128]{1,0:T(8,128)S(1)}, u32[]{:S(2)}, u32[]{:S(2)}) collective-permute-start(f32[128,128]{1,0:T(8,128)S(1)} %get-tuple-element.9), channel_id=1, source_target_pairs={{0,24},{1,25},{2,26},{3,27},{4,28},{5,29},{6,30},{7,31},{8,32},{9,... | collective-permute-start | bytes 196616 | tf_op jit(solution)/shard_map/ppermute | solution.py:115
  110.7 10.9 %collective-permute-start.7 = (f32[128,128]{1,0:T(8,128)S(1)}, f32[128,128]{1,0:T(8,128)S(1)}, u32[]{:S(2)}, u32[]{:S(2)}) collective-permute-start(f32[128,128]{1,0:T(8,128)S(1)} %get-tuple-element.10), channel_id=1, source_target_pairs={{0,48},{1,49},{2,50},{3,51},{4,52},{5,53},{6,54},{7,55},{8,56},{9,... | collective-permute-start | bytes 196616 | tf_op jit(solution)/shard_map/ppermute | solution.py:115
  115.3 10.4 %collective-permute-start.2 = (f32[3,128,128]{2,1,0:T(8,128)}, f32[3,128,128]{2,1,0:T(8,128)S(1)}, u32[]{:S(2)}, u32[]{:S(2)}) collective-permute-start(f32[3,128,128]{2,1,0:T(8,128)} %bitcast.8), channel_id=1, source_target_pairs={{0,0},{1,7},{2,6},{3,5},{4,4},{5,3},{6,2},{7,1},{8,8},{9,15},{10,1... | collective-permute-start | bytes 589832 | tf_op jit(solution)/shard_map/ppermute | solution.py:115
  119.6 6.1 %collective-permute-start.8 = (f32[128,128]{1,0:T(8,128)S(1)}, f32[128,128]{1,0:T(8,128)S(1)}, u32[]{:S(2)}, u32[]{:S(2)}) collective-permute-start(f32[128,128]{1,0:T(8,128)S(1)} %slice_bitcast_fusion), channel_id=1, source_target_pairs={{0,56},{1,57},{2,58},{3,59},{4,60},{5,61},{6,62},{7,63},{8,0},{9,1... | collective-permute-start | bytes 196616 | tf_op jit(solution)/shard_map/ppermute | solution.py:115
Sparse Core Ops, SparseCore 0:
  9.5 33.6 all-gather.1
  47.0 57.2 reduce-scatter.1

commit v13 on v9

--- a/solution.py
+++ b/solution.py
@@ -11,10 +11,10 @@
 LASSO = 0.1
 RIDGE = 0.5
 AXES = ("z", "y", "k")
-EARLY = (0, 7, 6, 4)
-TURNED = (1, 2)
+EARLY = (0, 7, 1, 6, 4)
+TURNED = (3,)
 LATE = 3
-SENT = (7, 6, 3, 4)
+SENT = (7, 1, 6, 3, 4)
 CHUNKS = 2
 MIB = 2**20
 

time: 126 us -> 138 us (1.095)
  the two profiles are of different devices: /device:TPU:26 before, /device:TPU:18 now
where the time goes in v13:
time: 138 us
  waiting for transfers between devices  64.3 us (47%)
  starting transfers between devices  47.5 us (34%)
  between operations  13.5 us (10%)
  Pallas kernels  11.6 us (8%)
    reduce_scatter x1, waiting for transfers between devices, local(): lax.psum_scatter(multiplied([panel[d] for d in EARLY[1:]], 1, once), 'z',...  42.9 us
    ppermute x9, starting transfers between devices, moved(): return lax.ppermute(a, AXES, [(index(*i), index(*to(*i))) for i in ids])  37.2 us
    ppermute x9, waiting for transfers between devices, moved(): return lax.ppermute(a, AXES, [(index(*i), index(*to(*i))) for i in ids])  21.3 us
    all_to_all x1, starting transfers between devices, local(): lax.all_to_all(multiplied([panel[LATE]], 0, weight), 'z', 0, 0, tiled=True)  10.3 us
    pallas_call x2, Pallas kernels, multiplied(): pl.pallas_call(functools.partial(products, n, tile, depth, count, offset)...  8.27 us
  transfers between devices with their start and end apart: 12, of which 5 were waited for; matrix products, arithmetic and copies ran while one was open for 1% of the time, Pallas kernels for 6%

profile of v13, /device:TPU:18, one launch (start us, length us, event | category | flops | bytes accessed | tf_op | source)
XLA Modules:
  0.0 137.8 jit_solution(3646310403813785195)
XLA Ops:
  6.5 1.7 %shard_map.46 = bf16[128,1024]{1,0:T(8,128)(2,1)} custom-call(bf16[128,512]{1,0:T(8,128)(2,1)} %a_ref.1, bf16[128,512]{1,0:T(8,128)(2,1)} %b_ref.1), custom_call_target="tpu_custom_call" | custom-call | tf_op jit(solution)/shard_map/pallas_call | solution.py:113
  8.2 0.0 all-gather.2.cloned.1.call-update
  8.2 0.0 reduce-scatter.2.cloned.1.call-start
  8.3 5.9 %collective-permute-start.3 = (bf16[128,1024]{1,0:T(8,128)(2,1)}, bf16[128,1024]{1,0:T(8,128)(2,1)S(1)}, u32[]{:S(2)}, u32[]{:S(2)}) collective-permute-start(bf16[128,1024]{1,0:T(8,128)(2,1)} %shard_map.46), channel_id=1, source_target_pairs={{0,32},{1,33},{2,34},{3,35},{4,36},{5,37},{6,38},{7,39},{8,40},{9,... | collective-permute-start | bytes 786440 | tf_op jit(solution)/shard_map/ppermute | solution.py:111
  14.2 1.9 %collective-permute-start.2 = (bf16[128,1024]{1,0:T(8,128)(2,1)}, bf16[128,1024]{1,0:T(8,128)(2,1)S(1)}, u32[]{:S(2)}, u32[]{:S(2)}) collective-permute-start(bf16[128,1024]{1,0:T(8,128)(2,1)} %shard_map.46), channel_id=1, source_target_pairs={{0,16},{1,17},{2,18},{3,19},{4,20},{5,21},{6,22},{7,23},{8,24},{9,... | collective-permute-start | bytes 786440 | tf_op jit(solution)/shard_map/ppermute | solution.py:111
  16.2 4.0 %collective-permute-start.1 = (bf16[128,1024]{1,0:T(8,128)(2,1)}, bf16[128,1024]{1,0:T(8,128)(2,1)S(1)}, u32[]{:S(2)}, u32[]{:S(2)}) collective-permute-start(bf16[128,1024]{1,0:T(8,128)(2,1)} %shard_map.46), channel_id=1, source_target_pairs={{0,56},{1,57},{2,58},{3,59},{4,60},{5,61},{6,62},{7,63},{8,0},{9,1... | collective-permute-start | bytes 786440 | tf_op jit(solution)/shard_map/ppermute | solution.py:111
  20.2 1.9 %collective-permute-start = (bf16[128,1024]{1,0:T(8,128)(2,1)}, bf16[128,1024]{1,0:T(8,128)(2,1)S(1)}, u32[]{:S(2)}, u32[]{:S(2)}) collective-permute-start(bf16[128,1024]{1,0:T(8,128)(2,1)} %shard_map.46), channel_id=1, source_target_pairs={{0,8},{1,9},{2,10},{3,11},{4,12},{5,13},{6,14},{7,15},{8,16},{9,17... | collective-permute-start | bytes 786440 | tf_op jit(solution)/shard_map/ppermute | solution.py:111
  22.1 7.9 %collective-permute-start.5 = (bf16[128,1024]{1,0:T(8,128)(2,1)}, bf16[128,1024]{1,0:T(8,128)(2,1)S(1)}, u32[]{:S(2)}, u32[]{:S(2)}) collective-permute-start(bf16[128,1024]{1,0:T(8,128)(2,1)} %shard_map.46), channel_id=1, source_target_pairs={{0,40},{1,41},{2,42},{3,43},{4,44},{5,45},{6,46},{7,47},{8,48},{9,... | collective-permute-start | bytes 786440 | tf_op jit(solution)/shard_map/ppermute | solution.py:111
  30.1 0.0 collective-permute-done.3.refs_3_
  30.1 10.5 %collective-permute-done.2.refs_2_ = bf16[128,1024]{1,0:T(8,128)(2,1)S(1)} collective-permute-done((bf16[128,1024]{1,0:T(8,128)(2,1)}, bf16[128,1024]{1,0:T(8,128)(2,1)S(1)}, u32[]{:S(2)}, u32[]{:S(2)}) %collective-permute-start.2) | collective-permute-done | bytes 262176 | tf_op jit(solution)/shard_map/ppermute | solution.py:111
  40.5 0.0 collective-permute-done.1.refs_1_
  40.5 4.5 %collective-permute-done.refs_0_ = bf16[128,1024]{1,0:T(8,128)(2,1)S(1)} collective-permute-done((bf16[128,1024]{1,0:T(8,128)(2,1)}, bf16[128,1024]{1,0:T(8,128)(2,1)S(1)}, u32[]{:S(2)}, u32[]{:S(2)}) %collective-permute-start) | collective-permute-done | bytes 262176 | tf_op jit(solution)/shard_map/ppermute | solution.py:111
  45.1 4.9 %shard_map.47 = f32[8,5,128,128]{3,2,1,0:T(8,128)} custom-call(bf16[1024,1024]{1,0:T(8,128)(2,1)} %all-gather.2.cloned.1.call-done.rows_ref, bf16[128,1024]{1,0:T(8,128)(2,1)S(1)} %collective-permute-done.refs_0_, bf16[128,1024]{1,0:T(8,128)(2,1)S(1)} %collective-permute-done.1.refs_1_, bf16[128,1024]{1,0:T(8,128)(2,1)S(1)} %collective-permute-done.2.refs_2_, ...), custom_call_target="tpu_custom_call" | custom-call | flops 268435456 | bytes 6291456 | tf_op jit(solution)/shard_map/pallas_call | solution.py:125
  50.0 0.0 reduce-scatter.2.cloned.1.call-update
  50.0 0.0 collective-permute-done.5.refs_0_
  50.0 0.0 copy-start
  50.0 0.0 copy-start.1
  50.0 3.4 %shard_map.48 = f32[8,1,128,128]{3,2,1,0:T(8,128)} custom-call(bf16[1024,1024]{1,0:T(8,128)(2,1)} %all-gather.2.cloned.1.call-done.rows_ref, bf16[128,1024]{1,0:T(8,128)(2,1)S(1)} %collective-permute-done.5.refs_0_), custom_call_target="tpu_custom_call" | custom-call | flops 161061273600 | bytes 6291456 | tf_op jit(solution)/shard_map/pallas_call | solution.py:125
  53.4 10.3 %all-to-all-start = ((f32[8,1,128,128]{3,2,1,0:T(8,128)}), f32[8,1,128,128]{3,2,1,0:T(8,128)S(1)}, u32[]{:S(2)}, u32[]{:S(2)}) async-start(f32[8,1,128,128]{3,2,1,0:T(8,128)} %shard_map.48), calls=%async_computation.1 | async-start | bytes 1048576 | tf_op jit(solution)/shard_map/all_to_all | solution.py:147
  63.8 42.9 %reduce-scatter.2.cloned.1.call-done = f32[1,5,128,128]{3,2,1,0:T(8,128)} async-done(((f32[8,5,128,128]{3,2,1,0:T(8,128)}), f32[1,5,128,128]{3,2,1,0:T(8,128)}) %reduce-scatter.2.cloned.1.call-update) | async-done | bytes 327696 | tf_op jit(solution)/shard_map/reduce_scatter | solution.py:143
  106.6 4.1 %collective-permute-start.4 = (f32[5,128,128]{2,1,0:T(8,128)}, f32[5,128,128]{2,1,0:T(8,128)S(1)}, u32[]{:S(2)}, u32[]{:S(2)}) collective-permute-start(f32[5,128,128]{2,1,0:T(8,128)} %bitcast.8), channel_id=1, source_target_pairs={{0,0},{1,7},{2,6},{3,5},{4,4},{5,3},{6,2},{7,1},{8,8},{9,15},{10,1... | collective-permute-start | bytes 983048 | tf_op jit(solution)/shard_map/ppermute | solution.py:111
  110.8 0.0 all-to-all-done.parts_ref
  110.8 6.1 %collective-permute-start.7 = (f32[128,128]{1,0:T(8,128)S(1)}, f32[128,128]{1,0:T(8,128)S(1)}, u32[]{:S(2)}, u32[]{:S(2)}) collective-permute-start(f32[128,128]{1,0:T(8,128)S(1)} %shard_map.49), channel_id=1, source_target_pairs={{0,24},{1,25},{2,26},{3,27},{4,28},{5,29},{6,30},{7,31},{8,32},{9,... | collective-permute-start | bytes 196616 | tf_op jit(solution)/shard_map/ppermute | solution.py:111
  116.9 3.3 %collective-permute-start.6 = (f32[128,128]{1,0:T(8,128)S(1)}, f32[128,128]{1,0:T(8,128)S(1)}, u32[]{:S(2)}, u32[]{:S(2)}) collective-permute-start(f32[128,128]{1,0:T(8,128)S(1)} %shard_map.49), channel_id=1, source_target_pairs={{0,0},{1,7},{2,6},{3,5},{4,4},{5,3},{6,2},{7,1},{8,8},{9,15},{10,1... | collective-permute-start | bytes 196616 | tf_op jit(solution)/shard_map/ppermute | solution.py:111
  120.2 0.8 slice_bitcast_fusion
  121.1 1.9 %collective-permute-start.8 = (f32[128,128]{1,0:T(8,128)S(1)}, f32[128,128]{1,0:T(8,128)S(1)}, u32[]{:S(2)}, u32[]{:S(2)}) collective-permute-start(f32[128,128]{1,0:T(8,128)S(1)} %slice_bitcast_fusion), channel_id=1, source_target_pairs={{0,48},{1,49},{2,50},{3,51},{4,52},{5,53},{6,54},{7,55},{8,56},{9,... | collective-permute-start | bytes 196616 | tf_op jit(solution)/shard_map/ppermute | solution.py:111
  123.0 0.0 collective-permute-done.7.refs_0_
  123.0 1.5 %collective-permute-done.6.late = f32[128,128]{1,0:T(8,128)S(1)} collective-permute-done((f32[128,128]{1,0:T(8,128)S(1)}, f32[128,128]{1,0:T(8,128)S(1)}, u32[]{:S(2)}, u32[]{:S(2)}) %collective-permute-start.6) | collective-permute-done | bytes 65568 | tf_op jit(solution)/shard_map/ppermute | solution.py:111
  124.6 4.8 %collective-permute-done.8.refs_1_ = f32[128,128]{1,0:T(8,128)S(1)} collective-permute-done((f32[128,128]{1,0:T(8,128)S(1)}, f32[128,128]{1,0:T(8,128)S(1)}, u32[]{:S(2)}, u32[]{:S(2)}) %collective-permute-start.8) | collective-permute-done | bytes 65568 | tf_op jit(solution)/shard_map/ppermute | solution.py:111
  129.4 0.0 collective-permute-done.4.mirrored
  129.4 0.0 copy-done
  129.4 1.6 %shard_map.50 = f32[8,128,128]{2,1,0:T(8,128)} custom-call(s32[8]{0:T(128)S(1)} %bitcast.7, f32[5,128,128]{2,1,0:T(8,128)S(1)} %collective-permute-done.4.mirrored, f32[128,128]{1,0:T(8,128)S(1)} %collective-permute-done.6.late, f32[128,128]{1,0:T(8,128)S(1)} %collective-permute-done.7.refs_0_, f32[128,128]{1,0:T(8,128)S(1)} %collective-permute-done.8.refs_1_, ...), custom_call_target="tpu_custom_call" | custom-call | tf_op jit(solution)/shard_map/pallas_call | solution.py:159
  (4 shorter events, 0.0 us)
Async XLA Ops:
  6.5 38.5 %all-gather.2.cloned.1.call-start = ((), (), s32[]{:S(2)}) async-start(), calls=%async_computation.2 | async-start | bytes 2359296 | tf_op jit(solution)/shard_map/all_gather | solution.py:120
  8.2 98.4 %reduce-scatter.2.cloned.1.call-start = ((), (), s32[]{:S(2)}) async-start(), calls=%async_computation.3 | async-start | bytes 2949120 | tf_op jit(solution)/shard_map/reduce_scatter | solution.py:143
  8.3 21.8 %collective-permute-start.3 = (bf16[128,1024]{1,0:T(8,128)(2,1)}, bf16[128,1024]{1,0:T(8,128)(2,1)S(1)}, u32[]{:S(2)}, u32[]{:S(2)}) collective-permute-start(bf16[128,1024]{1,0:T(8,128)(2,1)} %shard_map.46), channel_id=1, source_target_pairs={{0,32},{1,33},{2,34},{3,35},{4,36},{5,37},{6,38},{7,39},{8,40},{9,... | collective-permute-start | bytes 786440 | tf_op jit(solution)/shard_map/ppermute | solution.py:111
  14.2 26.3 %collective-permute-start.2 = (bf16[128,1024]{1,0:T(8,128)(2,1)}, bf16[128,1024]{1,0:T(8,128)(2,1)S(1)}, u32[]{:S(2)}, u32[]{:S(2)}) collective-permute-start(bf16[128,1024]{1,0:T(8,128)(2,1)} %shard_map.46), channel_id=1, source_target_pairs={{0,16},{1,17},{2,18},{3,19},{4,20},{5,21},{6,22},{7,23},{8,24},{9,... | collective-permute-start | bytes 786440 | tf_op jit(solution)/shard_map/ppermute | solution.py:111
  16.2 24.4 %collective-permute-start.1 = (bf16[128,1024]{1,0:T(8,128)(2,1)}, bf16[128,1024]{1,0:T(8,128)(2,1)S(1)}, u32[]{:S(2)}, u32[]{:S(2)}) collective-permute-start(bf16[128,1024]{1,0:T(8,128)(2,1)} %shard_map.46), channel_id=1, source_target_pairs={{0,56},{1,57},{2,58},{3,59},{4,60},{5,61},{6,62},{7,63},{8,0},{9,1... | collective-permute-start | bytes 786440 | tf_op jit(solution)/shard_map/ppermute | solution.py:111
  20.2 24.9 %collective-permute-start = (bf16[128,1024]{1,0:T(8,128)(2,1)}, bf16[128,1024]{1,0:T(8,128)(2,1)S(1)}, u32[]{:S(2)}, u32[]{:S(2)}) collective-permute-start(bf16[128,1024]{1,0:T(8,128)(2,1)} %shard_map.46), channel_id=1, source_target_pairs={{0,8},{1,9},{2,10},{3,11},{4,12},{5,13},{6,14},{7,15},{8,16},{9,17... | collective-permute-start | bytes 786440 | tf_op jit(solution)/shard_map/ppermute | solution.py:111
  22.1 27.9 %collective-permute-start.5 = (bf16[128,1024]{1,0:T(8,128)(2,1)}, bf16[128,1024]{1,0:T(8,128)(2,1)S(1)}, u32[]{:S(2)}, u32[]{:S(2)}) collective-permute-start(bf16[128,1024]{1,0:T(8,128)(2,1)} %shard_map.46), channel_id=1, source_target_pairs={{0,40},{1,41},{2,42},{3,43},{4,44},{5,45},{6,46},{7,47},{8,48},{9,... | collective-permute-start | bytes 786440 | tf_op jit(solution)/shard_map/ppermute | solution.py:111
  50.0 79.4 %copy-start = (f32[1,1,8,128,128]{4,3,2,1,0:T(8,128)S(1)}, f32[1,1,8,128,128]{4,3,2,1,0:T(8,128)}, u32[]{:S(2)}) copy-start(f32[1,1,8,128,128]{4,3,2,1,0:T(8,128)} %param.6) | copy-start | bytes 1572868
  50.0 79.3 %copy-start.1 = (s32[1,1,8]{2,1,0:T(1,128)S(1)}, s32[1,1,8]{2,1,0:T(1,128)}, u32[]{:S(2)}) copy-start(s32[1,1,8]{2,1,0:T(1,128)} %param.7) | copy-start | bytes 100
  53.4 57.4 %all-to-all-start = ((f32[8,1,128,128]{3,2,1,0:T(8,128)}), f32[8,1,128,128]{3,2,1,0:T(8,128)S(1)}, u32[]{:S(2)}, u32[]{:S(2)}) async-start(f32[8,1,128,128]{3,2,1,0:T(8,128)} %shard_map.48), calls=%async_computation.1 | async-start | bytes 1048576 | tf_op jit(solution)/shard_map/all_to_all | solution.py:147
  106.6 22.7 %collective-permute-start.4 = (f32[5,128,128]{2,1,0:T(8,128)}, f32[5,128,128]{2,1,0:T(8,128)S(1)}, u32[]{:S(2)}, u32[]{:S(2)}) collective-permute-start(f32[5,128,128]{2,1,0:T(8,128)} %bitcast.8), channel_id=1, source_target_pairs={{0,0},{1,7},{2,6},{3,5},{4,4},{5,3},{6,2},{7,1},{8,8},{9,15},{10,1... | collective-permute-start | bytes 983048 | tf_op jit(solution)/shard_map/ppermute | solution.py:111
  110.8 12.2 %collective-permute-start.7 = (f32[128,128]{1,0:T(8,128)S(1)}, f32[128,128]{1,0:T(8,128)S(1)}, u32[]{:S(2)}, u32[]{:S(2)}) collective-permute-start(f32[128,128]{1,0:T(8,128)S(1)} %shard_map.49), channel_id=1, source_target_pairs={{0,24},{1,25},{2,26},{3,27},{4,28},{5,29},{6,30},{7,31},{8,32},{9,... | collective-permute-start | bytes 196616 | tf_op jit(solution)/shard_map/ppermute | solution.py:111
  116.9 7.7 %collective-permute-start.6 = (f32[128,128]{1,0:T(8,128)S(1)}, f32[128,128]{1,0:T(8,128)S(1)}, u32[]{:S(2)}, u32[]{:S(2)}) collective-permute-start(f32[128,128]{1,0:T(8,128)S(1)} %shard_map.49), channel_id=1, source_target_pairs={{0,0},{1,7},{2,6},{3,5},{4,4},{5,3},{6,2},{7,1},{8,8},{9,15},{10,1... | collective-permute-start | bytes 196616 | tf_op jit(solution)/shard_map/ppermute | solution.py:111
  121.1 8.3 %collective-permute-start.8 = (f32[128,128]{1,0:T(8,128)S(1)}, f32[128,128]{1,0:T(8,128)S(1)}, u32[]{:S(2)}, u32[]{:S(2)}) collective-permute-start(f32[128,128]{1,0:T(8,128)S(1)} %slice_bitcast_fusion), channel_id=1, source_target_pairs={{0,48},{1,49},{2,50},{3,51},{4,52},{5,53},{6,54},{7,55},{8,56},{9,... | collective-permute-start | bytes 196616 | tf_op jit(solution)/shard_map/ppermute | solution.py:111
Sparse Core Ops, SparseCore 0:
  9.5 33.6 all-gather.1
  50.1 56.4 reduce-scatter.1

commit v14 on v10

--- a/solution.py
+++ b/solution.py
@@ -11,10 +11,10 @@
 LASSO = 0.1
 RIDGE = 0.5
 AXES = ("z", "y", "k")
-EARLY = (0, 7, 2, 4)
+EARLY = (0, 1, 2, 4)
 TURNED = (1, 2)
 LATE = 5
-SENT = (7, 2, 5, 4)
+SENT = (1, 2, 5, 4)
 CHUNKS = 2
 MIB = 2**20
 

time: 128 us -> 128 us (level)
  the two profiles are of different devices: /device:TPU:18 before, /device:TPU:2 now
where the time goes in v14:
time: 128 us; the launch traced here: 127 us
  starting transfers between devices  36 us (28%)
  waiting for transfers between devices  33.8 us (26%)
  blocking collectives  32.5 us (25%)
  between operations  13.5 us (11%)
  Pallas kernels  10.4 us (8%)
    ppermute x9, starting transfers between devices, moved(): return lax.ppermute(a, AXES, [(index(*i), index(*to(*i))) for i in ids])  35.9 us
    all_to_all x1, blocking collectives, local(): lax.all_to_all(multiplied([panel[LATE]], 0, weight), 'z', 0, 0, tiled=True)  32.5 us
    ppermute x9, waiting for transfers between devices, moved(): return lax.ppermute(a, AXES, [(index(*i), index(*to(*i))) for i in ids])  23.6 us
    reduce_scatter x1, waiting for transfers between devices, local(): lax.psum_scatter(multiplied([panel[d] for d in EARLY[1:]], 1, once), 'z',...  10.2 us
    pallas_call x2, Pallas kernels, multiplied(): pl.pallas_call(functools.partial(products, n, tile, depth, count, offset)...  7.12 us
  transfers between devices with their start and end apart: 11, of which 5 were waited for; matrix products, arithmetic and copies ran while one was open for 1% of the time, Pallas kernels for 6%

profile of v14, /device:TPU:2, one launch (start us, length us, event | category | flops | bytes accessed | tf_op | source)
XLA Modules:
  0.0 127.1 jit_solution(8762523586350483379)
XLA Ops:
  6.5 0.0 all-gather.2.cloned.1.call-start
  6.5 1.7 %shard_map.46 = bf16[128,1024]{1,0:T(8,128)(2,1)} custom-call(bf16[128,512]{1,0:T(8,128)(2,1)} %a_ref.1, bf16[128,512]{1,0:T(8,128)(2,1)} %b_ref.1), custom_call_target="tpu_custom_call" | custom-call | tf_op jit(solution)/shard_map/pallas_call | solution.py:113
  8.2 0.0 all-gather.2.cloned.1.call-update
  8.2 0.0 reduce-scatter.2.cloned.1.call-start
  8.3 7.7 %collective-permute-start.2 = (bf16[128,1024]{1,0:T(8,128)(2,1)}, bf16[128,1024]{1,0:T(8,128)(2,1)S(1)}, u32[]{:S(2)}, u32[]{:S(2)}) collective-permute-start(bf16[128,1024]{1,0:T(8,128)(2,1)} %shard_map.46), channel_id=1, source_target_pairs={{0,32},{1,33},{2,34},{3,35},{4,36},{5,37},{6,38},{7,39},{8,40},{9,... | collective-permute-start | bytes 786440 | tf_op jit(solution)/shard_map/ppermute | solution.py:111
  16.0 2.2 %collective-permute-start.1 = (bf16[128,1024]{1,0:T(8,128)(2,1)}, bf16[128,1024]{1,0:T(8,128)(2,1)S(1)}, u32[]{:S(2)}, u32[]{:S(2)}) collective-permute-start(bf16[128,1024]{1,0:T(8,128)(2,1)} %shard_map.46), channel_id=1, source_target_pairs={{0,48},{1,49},{2,50},{3,51},{4,52},{5,53},{6,54},{7,55},{8,56},{9,... | collective-permute-start | bytes 786440 | tf_op jit(solution)/shard_map/ppermute | solution.py:111
  18.3 2.4 %collective-permute-start = (bf16[128,1024]{1,0:T(8,128)(2,1)}, bf16[128,1024]{1,0:T(8,128)(2,1)S(1)}, u32[]{:S(2)}, u32[]{:S(2)}) collective-permute-start(bf16[128,1024]{1,0:T(8,128)(2,1)} %shard_map.46), channel_id=1, source_target_pairs={{0,56},{1,57},{2,58},{3,59},{4,60},{5,61},{6,62},{7,63},{8,0},{9,1... | collective-permute-start | bytes 786440 | tf_op jit(solution)/shard_map/ppermute | solution.py:111
  20.7 5.5 %collective-permute-start.4 = (bf16[128,1024]{1,0:T(8,128)(2,1)}, bf16[128,1024]{1,0:T(8,128)(2,1)S(1)}, u32[]{:S(2)}, u32[]{:S(2)}) collective-permute-start(bf16[128,1024]{1,0:T(8,128)(2,1)} %shard_map.46), channel_id=1, source_target_pairs={{0,24},{1,25},{2,26},{3,27},{4,28},{5,29},{6,30},{7,31},{8,32},{9,... | collective-permute-start | bytes 786440 | tf_op jit(solution)/shard_map/ppermute | solution.py:111
  26.2 0.0 collective-permute-done.2.refs_2_
  26.2 14.0 %collective-permute-done.1.refs_1_ = bf16[128,1024]{1,0:T(8,128)(2,1)S(1)} collective-permute-done((bf16[128,1024]{1,0:T(8,128)(2,1)}, bf16[128,1024]{1,0:T(8,128)(2,1)S(1)}, u32[]{:S(2)}, u32[]{:S(2)}) %collective-permute-start.1) | collective-permute-done | bytes 262176 | tf_op jit(solution)/shard_map/ppermute | solution.py:111
  40.2 5.2 %collective-permute-done.refs_0_ = bf16[128,1024]{1,0:T(8,128)(2,1)S(1)} collective-permute-done((bf16[128,1024]{1,0:T(8,128)(2,1)}, bf16[128,1024]{1,0:T(8,128)(2,1)S(1)}, u32[]{:S(2)}, u32[]{:S(2)}) %collective-permute-start) | collective-permute-done | bytes 262176 | tf_op jit(solution)/shard_map/ppermute | solution.py:111
  45.4 3.7 %shard_map.47 = f32[8,4,128,128]{3,2,1,0:T(8,128)} custom-call(bf16[1024,1024]{1,0:T(8,128)(2,1)} %all-gather.2.cloned.1.call-done.rows_ref, bf16[128,1024]{1,0:T(8,128)(2,1)S(1)} %collective-permute-done.refs_0_, bf16[128,1024]{1,0:T(8,128)(2,1)S(1)} %collective-permute-done.1.refs_1_, bf16[128,1024]{1,0:T(8,128)(2,1)S(1)} %collective-permute-done.2.refs_2_), custom_call_target="tpu_custom_call" | custom-call | flops 268435456 | bytes 6291456 | tf_op jit(solution)/shard_map/pallas_call | solution.py:125
  49.2 0.0 reduce-scatter.2.cloned.1.call-update
  49.2 0.0 collective-permute-done.4.refs_0_
  49.2 0.0 copy-start.1
  49.2 3.4 %shard_map.48 = f32[8,1,128,128]{3,2,1,0:T(8,128)S(1)} custom-call(bf16[1024,1024]{1,0:T(8,128)(2,1)} %all-gather.2.cloned.1.call-done.rows_ref, bf16[128,1024]{1,0:T(8,128)(2,1)S(1)} %collective-permute-done.4.refs_0_), custom_call_target="tpu_custom_call" | custom-call | flops 161061273600 | bytes 6291456 | tf_op jit(solution)/shard_map/pallas_call | solution.py:125
  52.6 0.0 copy-start
  52.6 32.5 %all_to_all.5.parts_ref = f32[8,1,128,128]{3,2,1,0:T(8,128)S(1)} all-to-all(f32[8,1,128,128]{3,2,1,0:T(8,128)S(1)} %shard_map.48), channel_id=1, replica_groups=mesh['z'=8,'y'=8,'k'=8] {'z'}, dimensions={0} | all-to-all | bytes 1048576 | tf_op jit(solution)/shard_map/all_to_all | solution.py:147
  85.1 3.4 %collective-permute-start.6 = (f32[128,128]{1,0:T(8,128)S(1)}, f32[128,128]{1,0:T(8,128)S(1)}, u32[]{:S(2)}, u32[]{:S(2)}) collective-permute-start(f32[128,128]{1,0:T(8,128)S(1)} %shard_map.49), channel_id=1, source_target_pairs={{0,40},{1,41},{2,42},{3,43},{4,44},{5,45},{6,46},{7,47},{8,48},{9,... | collective-permute-start | bytes 196616 | tf_op jit(solution)/shard_map/ppermute | solution.py:111
  88.6 4.1 %collective-permute-start.5 = (f32[128,128]{1,0:T(8,128)S(1)}, f32[128,128]{1,0:T(8,128)S(1)}, u32[]{:S(2)}, u32[]{:S(2)}) collective-permute-start(f32[128,128]{1,0:T(8,128)S(1)} %shard_map.49), channel_id=1, source_target_pairs={{0,0},{1,7},{2,6},{3,5},{4,4},{5,3},{6,2},{7,1},{8,8},{9,15},{10,1... | collective-permute-start | bytes 196616 | tf_op jit(solution)/shard_map/ppermute | solution.py:111
  92.6 10.2 %reduce-scatter.2.cloned.1.call-done = f32[1,4,128,128]{3,2,1,0:T(8,128)} async-done(((f32[8,4,128,128]{3,2,1,0:T(8,128)}), f32[1,4,128,128]{3,2,1,0:T(8,128)}) %reduce-scatter.2.cloned.1.call-update) | async-done | bytes 262160 | tf_op jit(solution)/shard_map/reduce_scatter | solution.py:143
  102.8 4.0 %collective-permute-start.3 = (f32[4,128,128]{2,1,0:T(8,128)}, f32[4,128,128]{2,1,0:T(8,128)S(1)}, u32[]{:S(2)}, u32[]{:S(2)}) collective-permute-start(f32[4,128,128]{2,1,0:T(8,128)} %bitcast.10), channel_id=1, source_target_pairs={{0,0},{1,7},{2,6},{3,5},{4,4},{5,3},{6,2},{7,1},{8,8},{9,15},{10,1... | collective-permute-start | bytes 786440 | tf_op jit(solution)/shard_map/ppermute | solution.py:111
  106.8 0.9 slice_bitcast_fusion
  107.7 3.6 %collective-permute-start.8 = (f32[128,128]{1,0:T(8,128)S(1)}, f32[128,128]{1,0:T(8,128)S(1)}, u32[]{:S(2)}, u32[]{:S(2)}) collective-permute-start(f32[128,128]{1,0:T(8,128)S(1)} %get-tuple-element.5), channel_id=1, source_target_pairs={{0,16},{1,17},{2,18},{3,19},{4,20},{5,21},{6,22},{7,23},{8,24},{9,... | collective-permute-start | bytes 196616 | tf_op jit(solution)/shard_map/ppermute | solution.py:111
  111.3 3.0 %collective-permute-start.7 = (f32[128,128]{1,0:T(8,128)S(1)}, f32[128,128]{1,0:T(8,128)S(1)}, u32[]{:S(2)}, u32[]{:S(2)}) collective-permute-start(f32[128,128]{1,0:T(8,128)S(1)} %get-tuple-element.6), channel_id=1, source_target_pairs={{0,8},{1,9},{2,10},{3,11},{4,12},{5,13},{6,14},{7,15},{8,16},{9,17... | collective-permute-start | bytes 196616 | tf_op jit(solution)/shard_map/ppermute | solution.py:111
  114.3 0.0 collective-permute-done.6.refs_0_
  114.4 0.0 collective-permute-done.5.late
  114.4 1.6 %collective-permute-done.8.refs_2_ = f32[128,128]{1,0:T(8,128)S(1)} collective-permute-done((f32[128,128]{1,0:T(8,128)S(1)}, f32[128,128]{1,0:T(8,128)S(1)}, u32[]{:S(2)}, u32[]{:S(2)}) %collective-permute-start.8) | collective-permute-done | bytes 65568 | tf_op jit(solution)/shard_map/ppermute | solution.py:111
  116.0 2.7 %collective-permute-done.7.refs_1_ = f32[128,128]{1,0:T(8,128)S(1)} collective-permute-done((f32[128,128]{1,0:T(8,128)S(1)}, f32[128,128]{1,0:T(8,128)S(1)}, u32[]{:S(2)}, u32[]{:S(2)}) %collective-permute-start.7) | collective-permute-done | bytes 65568 | tf_op jit(solution)/shard_map/ppermute | solution.py:111
  118.7 0.0 collective-permute-done.3.mirrored
  118.7 0.0 copy-done.1
  118.7 1.6 %shard_map.50 = f32[8,128,128]{2,1,0:T(8,128)} custom-call(s32[8]{0:T(128)S(1)} %bitcast.9, f32[4,128,128]{2,1,0:T(8,128)S(1)} %collective-permute-done.3.mirrored, f32[128,128]{1,0:T(8,128)S(1)} %collective-permute-done.5.late, f32[128,128]{1,0:T(8,128)S(1)} %collective-permute-done.6.refs_0_, f32[128,128]{1,0:T(8,128)S(1)} %collective-permute-done.7.refs_1_, ...), custom_call_target="tpu_custom_call" | custom-call | tf_op jit(solution)/shard_map/pallas_call | solution.py:159
  (3 shorter events, 0.0 us)
Async XLA Ops:
  6.5 38.9 %all-gather.2.cloned.1.call-start = ((), (), s32[]{:S(2)}) async-start(), calls=%async_computation.2 | async-start | bytes 2359296 | tf_op jit(solution)/shard_map/all_gather | solution.py:120
  8.2 94.5 %reduce-scatter.2.cloned.1.call-start = ((), (), s32[]{:S(2)}) async-start(), calls=%async_computation.3 | async-start | bytes 2359296 | tf_op jit(solution)/shard_map/reduce_scatter | solution.py:143
  8.3 17.9 %collective-permute-start.2 = (bf16[128,1024]{1,0:T(8,128)(2,1)}, bf16[128,1024]{1,0:T(8,128)(2,1)S(1)}, u32[]{:S(2)}, u32[]{:S(2)}) collective-permute-start(bf16[128,1024]{1,0:T(8,128)(2,1)} %shard_map.46), channel_id=1, source_target_pairs={{0,32},{1,33},{2,34},{3,35},{4,36},{5,37},{6,38},{7,39},{8,40},{9,... | collective-permute-start | bytes 786440 | tf_op jit(solution)/shard_map/ppermute | solution.py:111
  16.0 24.2 %collective-permute-start.1 = (bf16[128,1024]{1,0:T(8,128)(2,1)}, bf16[128,1024]{1,0:T(8,128)(2,1)S(1)}, u32[]{:S(2)}, u32[]{:S(2)}) collective-permute-start(bf16[128,1024]{1,0:T(8,128)(2,1)} %shard_map.46), channel_id=1, source_target_pairs={{0,48},{1,49},{2,50},{3,51},{4,52},{5,53},{6,54},{7,55},{8,56},{9,... | collective-permute-start | bytes 786440 | tf_op jit(solution)/shard_map/ppermute | solution.py:111
  18.3 27.1 %collective-permute-start = (bf16[128,1024]{1,0:T(8,128)(2,1)}, bf16[128,1024]{1,0:T(8,128)(2,1)S(1)}, u32[]{:S(2)}, u32[]{:S(2)}) collective-permute-start(bf16[128,1024]{1,0:T(8,128)(2,1)} %shard_map.46), channel_id=1, source_target_pairs={{0,56},{1,57},{2,58},{3,59},{4,60},{5,61},{6,62},{7,63},{8,0},{9,1... | collective-permute-start | bytes 786440 | tf_op jit(solution)/shard_map/ppermute | solution.py:111
  20.7 28.5 %collective-permute-start.4 = (bf16[128,1024]{1,0:T(8,128)(2,1)}, bf16[128,1024]{1,0:T(8,128)(2,1)S(1)}, u32[]{:S(2)}, u32[]{:S(2)}) collective-permute-start(bf16[128,1024]{1,0:T(8,128)(2,1)} %shard_map.46), channel_id=1, source_target_pairs={{0,24},{1,25},{2,26},{3,27},{4,28},{5,29},{6,30},{7,31},{8,32},{9,... | collective-permute-start | bytes 786440 | tf_op jit(solution)/shard_map/ppermute | solution.py:111
  49.2 69.5 %copy-start.1 = (s32[1,1,8]{2,1,0:T(1,128)S(1)}, s32[1,1,8]{2,1,0:T(1,128)}, u32[]{:S(2)}) copy-start(s32[1,1,8]{2,1,0:T(1,128)} %param.7) | copy-start | bytes 100
  52.6 66.0 %copy-start = (f32[1,1,8,128,128]{4,3,2,1,0:T(8,128)S(1)}, f32[1,1,8,128,128]{4,3,2,1,0:T(8,128)}, u32[]{:S(2)}) copy-start(f32[1,1,8,128,128]{4,3,2,1,0:T(8,128)} %param.6) | copy-start | bytes 1572868
  85.1 29.2 %collective-permute-start.6 = (f32[128,128]{1,0:T(8,128)S(1)}, f32[128,128]{1,0:T(8,128)S(1)}, u32[]{:S(2)}, u32[]{:S(2)}) collective-permute-start(f32[128,128]{1,0:T(8,128)S(1)} %shard_map.49), channel_id=1, source_target_pairs={{0,40},{1,41},{2,42},{3,43},{4,44},{5,45},{6,46},{7,47},{8,48},{9,... | collective-permute-start | bytes 196616 | tf_op jit(solution)/shard_map/ppermute | solution.py:111
  88.6 25.8 %collective-permute-start.5 = (f32[128,128]{1,0:T(8,128)S(1)}, f32[128,128]{1,0:T(8,128)S(1)}, u32[]{:S(2)}, u32[]{:S(2)}) collective-permute-start(f32[128,128]{1,0:T(8,128)S(1)} %shard_map.49), channel_id=1, source_target_pairs={{0,0},{1,7},{2,6},{3,5},{4,4},{5,3},{6,2},{7,1},{8,8},{9,15},{10,1... | collective-permute-start | bytes 196616 | tf_op jit(solution)/shard_map/ppermute | solution.py:111
  102.8 15.9 %collective-permute-start.3 = (f32[4,128,128]{2,1,0:T(8,128)}, f32[4,128,128]{2,1,0:T(8,128)S(1)}, u32[]{:S(2)}, u32[]{:S(2)}) collective-permute-start(f32[4,128,128]{2,1,0:T(8,128)} %bitcast.10), channel_id=1, source_target_pairs={{0,0},{1,7},{2,6},{3,5},{4,4},{5,3},{6,2},{7,1},{8,8},{9,15},{10,1... | collective-permute-start | bytes 786440 | tf_op jit(solution)/shard_map/ppermute | solution.py:111
  107.7 8.3 %collective-permute-start.8 = (f32[128,128]{1,0:T(8,128)S(1)}, f32[128,128]{1,0:T(8,128)S(1)}, u32[]{:S(2)}, u32[]{:S(2)}) collective-permute-start(f32[128,128]{1,0:T(8,128)S(1)} %get-tuple-element.5), channel_id=1, source_target_pairs={{0,16},{1,17},{2,18},{3,19},{4,20},{5,21},{6,22},{7,23},{8,24},{9,... | collective-permute-start | bytes 196616 | tf_op jit(solution)/shard_map/ppermute | solution.py:111
  111.3 7.4 %collective-permute-start.7 = (f32[128,128]{1,0:T(8,128)S(1)}, f32[128,128]{1,0:T(8,128)S(1)}, u32[]{:S(2)}, u32[]{:S(2)}) collective-permute-start(f32[128,128]{1,0:T(8,128)S(1)} %get-tuple-element.6), channel_id=1, source_target_pairs={{0,8},{1,9},{2,10},{3,11},{4,12},{5,13},{6,14},{7,15},{8,16},{9,17... | collective-permute-start | bytes 196616 | tf_op jit(solution)/shard_map/ppermute | solution.py:111
Sparse Core Ops, SparseCore 0:
  9.5 33.8 all-gather.1
  49.3 53.4 reduce-scatter.1

commit v15 on v9

--- a/solution.py
+++ b/solution.py
@@ -11,10 +11,10 @@
 LASSO = 0.1
 RIDGE = 0.5
 AXES = ("z", "y", "k")
-EARLY = (0, 7, 6, 4)
+EARLY = (0, 1, 6, 4)
 TURNED = (1, 2)
 LATE = 3
-SENT = (7, 6, 3, 4)
+SENT = (1, 6, 3, 4)
 CHUNKS = 2
 MIB = 2**20
 

time: 126 us -> 128 us (1.016)
  the two profiles are of different devices: /device:TPU:26 before, /device:TPU:2 now
where the time goes in v15:
time: 128 us
  starting transfers between devices  37 us (29%)
  blocking collectives  33.8 us (26%)
  waiting for transfers between devices  31.9 us (25%)
  between operations  13.5 us (11%)
  Pallas kernels  10.4 us (8%)
    ppermute x9, starting transfers between devices, moved(): return lax.ppermute(a, AXES, [(index(*i), index(*to(*i))) for i in ids])  37 us
    all_to_all x1, blocking collectives, local(): lax.all_to_all(multiplied([panel[LATE]], 0, weight), 'z', 0, 0, tiled=True)  33.8 us
    ppermute x9, waiting for transfers between devices, moved(): return lax.ppermute(a, AXES, [(index(*i), index(*to(*i))) for i in ids])  19.5 us
    pallas_call x2, Pallas kernels, multiplied(): pl.pallas_call(functools.partial(products, n, tile, depth, count, offset)...  7.13 us
    reduce_scatter x1, waiting for transfers between devices, local(): lax.psum_scatter(multiplied([panel[d] for d in EARLY[1:]], 1, once), 'z',...  6.25 us
    all_gather x1, waiting for transfers between devices, local(): rows = lax.all_gather(own, 'k', axis=0, tiled=True)  6.09 us
  transfers between devices with their start and end apart: 11, of which 7 were waited for; matrix products, arithmetic and copies ran while one was open for 1% of the time, Pallas kernels for 6%

profile of v15, /device:TPU:2, one launch (start us, length us, event | category | flops | bytes accessed | tf_op | source)
XLA Modules:
  0.0 127.6 jit_solution(8050418267833624081)
XLA Ops:
  6.5 0.0 all-gather.2.cloned.1.call-start
  6.5 1.7 %shard_map.46 = bf16[128,1024]{1,0:T(8,128)(2,1)} custom-call(bf16[128,512]{1,0:T(8,128)(2,1)} %a_ref.1, bf16[128,512]{1,0:T(8,128)(2,1)} %b_ref.1), custom_call_target="tpu_custom_call" | custom-call | tf_op jit(solution)/shard_map/pallas_call | solution.py:113
  8.2 0.0 all-gather.2.cloned.1.call-update
  8.2 0.0 reduce-scatter.2.cloned.1.call-start
  8.3 7.7 %collective-permute-start.2 = (bf16[128,1024]{1,0:T(8,128)(2,1)}, bf16[128,1024]{1,0:T(8,128)(2,1)S(1)}, u32[]{:S(2)}, u32[]{:S(2)}) collective-permute-start(bf16[128,1024]{1,0:T(8,128)(2,1)} %shard_map.46), channel_id=1, source_target_pairs={{0,32},{1,33},{2,34},{3,35},{4,36},{5,37},{6,38},{7,39},{8,40},{9,... | collective-permute-start | bytes 786440 | tf_op jit(solution)/shard_map/ppermute | solution.py:111
  16.0 2.7 %collective-permute-start.1 = (bf16[128,1024]{1,0:T(8,128)(2,1)}, bf16[128,1024]{1,0:T(8,128)(2,1)S(1)}, u32[]{:S(2)}, u32[]{:S(2)}) collective-permute-start(bf16[128,1024]{1,0:T(8,128)(2,1)} %shard_map.46), channel_id=1, source_target_pairs={{0,16},{1,17},{2,18},{3,19},{4,20},{5,21},{6,22},{7,23},{8,24},{9,... | collective-permute-start | bytes 786440 | tf_op jit(solution)/shard_map/ppermute | solution.py:111
  18.7 4.5 %collective-permute-start = (bf16[128,1024]{1,0:T(8,128)(2,1)}, bf16[128,1024]{1,0:T(8,128)(2,1)S(1)}, u32[]{:S(2)}, u32[]{:S(2)}) collective-permute-start(bf16[128,1024]{1,0:T(8,128)(2,1)} %shard_map.46), channel_id=1, source_target_pairs={{0,56},{1,57},{2,58},{3,59},{4,60},{5,61},{6,62},{7,63},{8,0},{9,1... | collective-permute-start | bytes 786440 | tf_op jit(solution)/shard_map/ppermute | solution.py:111
  23.2 1.9 %collective-permute-start.4 = (bf16[128,1024]{1,0:T(8,128)(2,1)}, bf16[128,1024]{1,0:T(8,128)(2,1)S(1)}, u32[]{:S(2)}, u32[]{:S(2)}) collective-permute-start(bf16[128,1024]{1,0:T(8,128)(2,1)} %shard_map.46), channel_id=1, source_target_pairs={{0,40},{1,41},{2,42},{3,43},{4,44},{5,45},{6,46},{7,47},{8,48},{9,... | collective-permute-start | bytes 786440 | tf_op jit(solution)/shard_map/ppermute | solution.py:111
  25.1 3.6 %collective-permute-done.2.refs_2_ = bf16[128,1024]{1,0:T(8,128)(2,1)S(1)} collective-permute-done((bf16[128,1024]{1,0:T(8,128)(2,1)}, bf16[128,1024]{1,0:T(8,128)(2,1)S(1)}, u32[]{:S(2)}, u32[]{:S(2)}) %collective-permute-start.2) | collective-permute-done | bytes 262176 | tf_op jit(solution)/shard_map/ppermute | solution.py:111
  28.7 5.3 %collective-permute-done.1.refs_1_ = bf16[128,1024]{1,0:T(8,128)(2,1)S(1)} collective-permute-done((bf16[128,1024]{1,0:T(8,128)(2,1)}, bf16[128,1024]{1,0:T(8,128)(2,1)S(1)}, u32[]{:S(2)}, u32[]{:S(2)}) %collective-permute-start.1) | collective-permute-done | bytes 262176 | tf_op jit(solution)/shard_map/ppermute | solution.py:111
  34.0 3.4 %collective-permute-done.refs_0_ = bf16[128,1024]{1,0:T(8,128)(2,1)S(1)} collective-permute-done((bf16[128,1024]{1,0:T(8,128)(2,1)}, bf16[128,1024]{1,0:T(8,128)(2,1)S(1)}, u32[]{:S(2)}, u32[]{:S(2)}) %collective-permute-start) | collective-permute-done | bytes 262176 | tf_op jit(solution)/shard_map/ppermute | solution.py:111
  37.3 6.1 %all-gather.2.cloned.1.call-done.rows_ref = bf16[1024,1024]{1,0:T(8,128)(2,1)} async-done(((bf16[128,1024]{1,0:T(8,128)(2,1)}), bf16[1024,1024]{1,0:T(8,128)(2,1)}) %all-gather.2.cloned.1.call-update) | async-done | bytes 2097168 | tf_op jit(solution)/shard_map/all_gather | solution.py:120
  43.4 3.7 %shard_map.47 = f32[8,4,128,128]{3,2,1,0:T(8,128)} custom-call(bf16[1024,1024]{1,0:T(8,128)(2,1)} %all-gather.2.cloned.1.call-done.rows_ref, bf16[128,1024]{1,0:T(8,128)(2,1)S(1)} %collective-permute-done.refs_0_, bf16[128,1024]{1,0:T(8,128)(2,1)S(1)} %collective-permute-done.1.refs_1_, bf16[128,1024]{1,0:T(8,128)(2,1)S(1)} %collective-permute-done.2.refs_2_), custom_call_target="tpu_custom_call" | custom-call | flops 268435456 | bytes 6291456 | tf_op jit(solution)/shard_map/pallas_call | solution.py:125
  47.2 0.0 reduce-scatter.2.cloned.1.call-update
  47.2 4.2 %collective-permute-done.4.refs_0_ = bf16[128,1024]{1,0:T(8,128)(2,1)S(1)} collective-permute-done((bf16[128,1024]{1,0:T(8,128)(2,1)}, bf16[128,1024]{1,0:T(8,128)(2,1)S(1)}, u32[]{:S(2)}, u32[]{:S(2)}) %collective-permute-start.4) | collective-permute-done | bytes 262176 | tf_op jit(solution)/shard_map/ppermute | solution.py:111
  51.3 3.4 %shard_map.48 = f32[8,1,128,128]{3,2,1,0:T(8,128)S(1)} custom-call(bf16[1024,1024]{1,0:T(8,128)(2,1)} %all-gather.2.cloned.1.call-done.rows_ref, bf16[128,1024]{1,0:T(8,128)(2,1)S(1)} %collective-permute-done.4.refs_0_), custom_call_target="tpu_custom_call" | custom-call | flops 161061273600 | bytes 6291456 | tf_op jit(solution)/shard_map/pallas_call | solution.py:125
  54.8 0.0 copy-start
  54.8 33.8 %all_to_all.5.parts_ref = f32[8,1,128,128]{3,2,1,0:T(8,128)S(1)} all-to-all(f32[8,1,128,128]{3,2,1,0:T(8,128)S(1)} %shard_map.48), channel_id=1, replica_groups=mesh['z'=8,'y'=8,'k'=8] {'z'}, dimensions={0} | all-to-all | bytes 1048576 | tf_op jit(solution)/shard_map/all_to_all | solution.py:147
  88.6 3.8 %collective-permute-start.6 = (f32[128,128]{1,0:T(8,128)S(1)}, f32[128,128]{1,0:T(8,128)S(1)}, u32[]{:S(2)}, u32[]{:S(2)}) collective-permute-start(f32[128,128]{1,0:T(8,128)S(1)} %shard_map.49), channel_id=1, source_target_pairs={{0,24},{1,25},{2,26},{3,27},{4,28},{5,29},{6,30},{7,31},{8,32},{9,... | collective-permute-start | bytes 196616 | tf_op jit(solution)/shard_map/ppermute | solution.py:111
  92.4 4.1 %collective-permute-start.5 = (f32[128,128]{1,0:T(8,128)S(1)}, f32[128,128]{1,0:T(8,128)S(1)}, u32[]{:S(2)}, u32[]{:S(2)}) collective-permute-start(f32[128,128]{1,0:T(8,128)S(1)} %shard_map.49), channel_id=1, source_target_pairs={{0,0},{1,7},{2,6},{3,5},{4,4},{5,3},{6,2},{7,1},{8,8},{9,15},{10,1... | collective-permute-start | bytes 196616 | tf_op jit(solution)/shard_map/ppermute | solution.py:111
  96.5 6.3 %reduce-scatter.2.cloned.1.call-done = f32[1,4,128,128]{3,2,1,0:T(8,128)} async-done(((f32[8,4,128,128]{3,2,1,0:T(8,128)}), f32[1,4,128,128]{3,2,1,0:T(8,128)}) %reduce-scatter.2.cloned.1.call-update) | async-done | bytes 262160 | tf_op jit(solution)/shard_map/reduce_scatter | solution.py:143
  102.8 3.9 %collective-permute-start.3 = (f32[4,128,128]{2,1,0:T(8,128)}, f32[4,128,128]{2,1,0:T(8,128)S(1)}, u32[]{:S(2)}, u32[]{:S(2)}) collective-permute-start(f32[4,128,128]{2,1,0:T(8,128)} %bitcast.10), channel_id=1, source_target_pairs={{0,0},{1,7},{2,6},{3,5},{4,4},{5,3},{6,2},{7,1},{8,8},{9,15},{10,1... | collective-permute-start | bytes 786440 | tf_op jit(solution)/shard_map/ppermute | solution.py:111
  106.6 0.9 slice_bitcast_fusion
  107.5 3.3 %collective-permute-start.8 = (f32[128,128]{1,0:T(8,128)S(1)}, f32[128,128]{1,0:T(8,128)S(1)}, u32[]{:S(2)}, u32[]{:S(2)}) collective-permute-start(f32[128,128]{1,0:T(8,128)S(1)} %get-tuple-element.5), channel_id=1, source_target_pairs={{0,48},{1,49},{2,50},{3,51},{4,52},{5,53},{6,54},{7,55},{8,56},{9,... | collective-permute-start | bytes 196616 | tf_op jit(solution)/shard_map/ppermute | solution.py:111
  110.9 5.1 %collective-permute-start.7 = (f32[128,128]{1,0:T(8,128)S(1)}, f32[128,128]{1,0:T(8,128)S(1)}, u32[]{:S(2)}, u32[]{:S(2)}) collective-permute-start(f32[128,128]{1,0:T(8,128)S(1)} %get-tuple-element.6), channel_id=1, source_target_pairs={{0,8},{1,9},{2,10},{3,11},{4,12},{5,13},{6,14},{7,15},{8,16},{9,17... | collective-permute-start | bytes 196616 | tf_op jit(solution)/shard_map/ppermute | solution.py:111
  116.0 0.0 collective-permute-done.6.refs_0_
  116.0 0.0 collective-permute-done.5.late
  116.0 0.0 collective-permute-done.8.refs_2_
  116.0 3.1 %collective-permute-done.7.refs_1_ = f32[128,128]{1,0:T(8,128)S(1)} collective-permute-done((f32[128,128]{1,0:T(8,128)S(1)}, f32[128,128]{1,0:T(8,128)S(1)}, u32[]{:S(2)}, u32[]{:S(2)}) %collective-permute-start.7) | collective-permute-done | bytes 65568 | tf_op jit(solution)/shard_map/ppermute | solution.py:111
  119.2 0.0 collective-permute-done.3.mirrored
  119.2 0.0 copy-done.1
  119.2 1.6 %shard_map.50 = f32[8,128,128]{2,1,0:T(8,128)} custom-call(s32[8]{0:T(128)S(1)} %bitcast.9, f32[4,128,128]{2,1,0:T(8,128)S(1)} %collective-permute-done.3.mirrored, f32[128,128]{1,0:T(8,128)S(1)} %collective-permute-done.5.late, f32[128,128]{1,0:T(8,128)S(1)} %collective-permute-done.6.refs_0_, f32[128,128]{1,0:T(8,128)S(1)} %collective-permute-done.7.refs_1_, ...), custom_call_target="tpu_custom_call" | custom-call | tf_op jit(solution)/shard_map/pallas_call | solution.py:159
  (3 shorter events, 0.0 us)
Async XLA Ops:
  6.5 36.9 %all-gather.2.cloned.1.call-start = ((), (), s32[]{:S(2)}) async-start(), calls=%async_computation.2 | async-start | bytes 2359296 | tf_op jit(solution)/shard_map/all_gather | solution.py:120
  8.2 94.5 %reduce-scatter.2.cloned.1.call-start = ((), (), s32[]{:S(2)}) async-start(), calls=%async_computation.3 | async-start | bytes 2359296 | tf_op jit(solution)/shard_map/reduce_scatter | solution.py:143
  8.3 20.4 %collective-permute-start.2 = (bf16[128,1024]{1,0:T(8,128)(2,1)}, bf16[128,1024]{1,0:T(8,128)(2,1)S(1)}, u32[]{:S(2)}, u32[]{:S(2)}) collective-permute-start(bf16[128,1024]{1,0:T(8,128)(2,1)} %shard_map.46), channel_id=1, source_target_pairs={{0,32},{1,33},{2,34},{3,35},{4,36},{5,37},{6,38},{7,39},{8,40},{9,... | collective-permute-start | bytes 786440 | tf_op jit(solution)/shard_map/ppermute | solution.py:111
  16.0 17.9 %collective-permute-start.1 = (bf16[128,1024]{1,0:T(8,128)(2,1)}, bf16[128,1024]{1,0:T(8,128)(2,1)S(1)}, u32[]{:S(2)}, u32[]{:S(2)}) collective-permute-start(bf16[128,1024]{1,0:T(8,128)(2,1)} %shard_map.46), channel_id=1, source_target_pairs={{0,16},{1,17},{2,18},{3,19},{4,20},{5,21},{6,22},{7,23},{8,24},{9,... | collective-permute-start | bytes 786440 | tf_op jit(solution)/shard_map/ppermute | solution.py:111
  18.7 18.6 %collective-permute-start = (bf16[128,1024]{1,0:T(8,128)(2,1)}, bf16[128,1024]{1,0:T(8,128)(2,1)S(1)}, u32[]{:S(2)}, u32[]{:S(2)}) collective-permute-start(bf16[128,1024]{1,0:T(8,128)(2,1)} %shard_map.46), channel_id=1, source_target_pairs={{0,56},{1,57},{2,58},{3,59},{4,60},{5,61},{6,62},{7,63},{8,0},{9,1... | collective-permute-start | bytes 786440 | tf_op jit(solution)/shard_map/ppermute | solution.py:111
  23.2 28.1 %collective-permute-start.4 = (bf16[128,1024]{1,0:T(8,128)(2,1)}, bf16[128,1024]{1,0:T(8,128)(2,1)S(1)}, u32[]{:S(2)}, u32[]{:S(2)}) collective-permute-start(bf16[128,1024]{1,0:T(8,128)(2,1)} %shard_map.46), channel_id=1, source_target_pairs={{0,40},{1,41},{2,42},{3,43},{4,44},{5,45},{6,46},{7,47},{8,48},{9,... | collective-permute-start | bytes 786440 | tf_op jit(solution)/shard_map/ppermute | solution.py:111
  51.3 67.8 %copy-start.1 = (s32[1,1,8]{2,1,0:T(1,128)S(1)}, s32[1,1,8]{2,1,0:T(1,128)}, u32[]{:S(2)}) copy-start(s32[1,1,8]{2,1,0:T(1,128)} %param.7) | copy-start | bytes 100
  54.8 64.4 %copy-start = (f32[1,1,8,128,128]{4,3,2,1,0:T(8,128)S(1)}, f32[1,1,8,128,128]{4,3,2,1,0:T(8,128)}, u32[]{:S(2)}) copy-start(f32[1,1,8,128,128]{4,3,2,1,0:T(8,128)} %param.6) | copy-start | bytes 1572868
  88.6 27.4 %collective-permute-start.6 = (f32[128,128]{1,0:T(8,128)S(1)}, f32[128,128]{1,0:T(8,128)S(1)}, u32[]{:S(2)}, u32[]{:S(2)}) collective-permute-start(f32[128,128]{1,0:T(8,128)S(1)} %shard_map.49), channel_id=1, source_target_pairs={{0,24},{1,25},{2,26},{3,27},{4,28},{5,29},{6,30},{7,31},{8,32},{9,... | collective-permute-start | bytes 196616 | tf_op jit(solution)/shard_map/ppermute | solution.py:111
  92.4 23.6 %collective-permute-start.5 = (f32[128,128]{1,0:T(8,128)S(1)}, f32[128,128]{1,0:T(8,128)S(1)}, u32[]{:S(2)}, u32[]{:S(2)}) collective-permute-start(f32[128,128]{1,0:T(8,128)S(1)} %shard_map.49), channel_id=1, source_target_pairs={{0,0},{1,7},{2,6},{3,5},{4,4},{5,3},{6,2},{7,1},{8,8},{9,15},{10,1... | collective-permute-start | bytes 196616 | tf_op jit(solution)/shard_map/ppermute | solution.py:111
  102.8 16.4 %collective-permute-start.3 = (f32[4,128,128]{2,1,0:T(8,128)}, f32[4,128,128]{2,1,0:T(8,128)S(1)}, u32[]{:S(2)}, u32[]{:S(2)}) collective-permute-start(f32[4,128,128]{2,1,0:T(8,128)} %bitcast.10), channel_id=1, source_target_pairs={{0,0},{1,7},{2,6},{3,5},{4,4},{5,3},{6,2},{7,1},{8,8},{9,15},{10,1... | collective-permute-start | bytes 786440 | tf_op jit(solution)/shard_map/ppermute | solution.py:111
  107.5 8.5 %collective-permute-start.8 = (f32[128,128]{1,0:T(8,128)S(1)}, f32[128,128]{1,0:T(8,128)S(1)}, u32[]{:S(2)}, u32[]{:S(2)}) collective-permute-start(f32[128,128]{1,0:T(8,128)S(1)} %get-tuple-element.5), channel_id=1, source_target_pairs={{0,48},{1,49},{2,50},{3,51},{4,52},{5,53},{6,54},{7,55},{8,56},{9,... | collective-permute-start | bytes 196616 | tf_op jit(solution)/shard_map/ppermute | solution.py:111
  110.9 8.3 %collective-permute-start.7 = (f32[128,128]{1,0:T(8,128)S(1)}, f32[128,128]{1,0:T(8,128)S(1)}, u32[]{:S(2)}, u32[]{:S(2)}) collective-permute-start(f32[128,128]{1,0:T(8,128)S(1)} %get-tuple-element.6), channel_id=1, source_target_pairs={{0,8},{1,9},{2,10},{3,11},{4,12},{5,13},{6,14},{7,15},{8,16},{9,17... | collective-permute-start | bytes 196616 | tf_op jit(solution)/shard_map/ppermute | solution.py:111
Sparse Core Ops, SparseCore 0:
  9.5 33.8 all-gather.1
  47.3 55.4 reduce-scatter.1
